TPU v7x, 32 devices: a whole 2x2x4 slice. The times are simulated.
32 devices in a mesh: grp: 4 (over y, core), seq: 8 (over z, x).
Axes of the slice: x: 2, y: 2, z: 4, core: 2. Of those that a mesh axis runs over, the one named last changes fastest.
Arguments:
- tokens: bfloat16 [4, 1024, 1024], P('grp', 'seq'), may hold values from -40 to 40
- queries: bfloat16 [4, 1024, 512], P('grp', 'seq'), may hold values from -8 to 8
- keys: bfloat16 [4, 1024, 512], P('grp', 'seq'), may hold values from -8 to 8
- values: bfloat16 [4, 1024, 512], P('grp', 'seq'), may hold values from -6 to 6
- attn_mask: int32 [4, 8, 8], P('grp', 'seq'), may hold values from 0 to 1, as said below
- out_proj: bfloat16 [512, 1024], replicated, may hold values from -0.25 to 0.25
- norm_gain_vector: float32 [1024], replicated, may hold values from 0.5 to 1.5
- w1_packed: bfloat16 [32, 2, 128, 128], P('grp'), may hold values from -0.375 to 0.375
- w1_rows: int32 [32, 2], replicated, may hold values from 0 to 7, as said below
- w2_packed: bfloat16 [32, 2, 128, 128], P('grp'), may hold values from -0.1875 to 0.1875
- w2_cols: int32 [32, 2], replicated, may hold values from 0 to 7, as said below
- grad_out: bfloat16 [4, 1024, 1024], P('grp', 'seq'), may hold values from -6 to 6
Outputs:
- output: bfloat16 [4, 1024, 1024], P('grp', 'seq')
- grad_tokens: bfloat16 [4, 1024, 1024], P('grp', 'seq')
Inputs may be any that keep to these rules, and one draw needn't show every extreme that they name: attn_mask[s, i, i] is 1 for every sheet s and block i. `w1_rows`: the 2 entries of a row are distinct. `w2_cols`: the 2 entries of a row are distinct.
All inputs are finite; a program needn't handle non-finite values.
Results may differ from a plain program's by a relative error of at most 0.0035.
The roundings to bfloat16 on the way count: a program that leaves them out, or rounds other values in their place, can miss the bound.
Values may be sent and summed in bfloat16 or wider, within the bound.
No kernel may reach another device: no remote copies, remote signals or barrier semaphores. Data moves between devices by JAX's collectives and lax.ppermute only.
A program may use at most 64 MiB of HBM per device.

v0:
```python
import jax
import jax.numpy as jnp
from jax import lax
from jax.sharding import PartitionSpec as P

D = 1024
HD = 64
HEADS = 8
BLK = 128


def gelu_slope(pre):
    return (
        0.5 * (1.0 + jax.scipy.special.erf(pre * 0.7071067811865476))
        + pre * jnp.exp(-0.5 * pre * pre) * 0.3989422804014327
    )


def expand_mask(mask):
    rows_blk, cols_blk = mask.shape
    wide = jnp.broadcast_to(mask[:, None, :, None], (rows_blk, BLK, cols_blk, BLK))
    return wide.reshape(rows_blk * BLK, cols_blk * BLK) > 0


def split_heads(array):
    return array.reshape(array.shape[0], HEADS, HD).transpose(1, 0, 2)


def join_heads(array):
    return array.transpose(1, 0, 2).reshape(array.shape[1], HEADS * HD)


def attend_forward(query, key_rows, value_rows, allowed):
    scale = HD ** (-0.5)

    def one_head(args):
        q_head, k_head, v_head = args
        scores = jnp.dot(q_head, k_head.T, preferred_element_type=jnp.float32) * scale
        scores = jnp.where(allowed, scores, -jnp.inf)
        top = jnp.max(scores, axis=1, keepdims=True)
        weight = jnp.exp(scores - top)
        total = jnp.sum(weight, axis=1, keepdims=True)
        prob = (weight / total).astype(jnp.bfloat16)
        return jnp.dot(prob, v_head, preferred_element_type=jnp.float32)

    heads_out = lax.map(
        one_head, (split_heads(query), split_heads(key_rows), split_heads(value_rows))
    )
    return join_heads(heads_out).astype(jnp.bfloat16)


def layer_norm_forward(hidden_state, gain_vector):
    mean_row = jnp.mean(hidden_state, axis=1, keepdims=True)
    mean_removed = hidden_state - mean_row
    reciprocal_deviation = lax.rsqrt(
        jnp.mean(mean_removed * mean_removed, axis=1, keepdims=True) + 1e-06
    )
    unit_rows = mean_removed * reciprocal_deviation
    return (unit_rows, reciprocal_deviation, (unit_rows * gain_vector).astype(jnp.bfloat16))


def layer_norm_backward(
    normed_gradient, gain_vector, unit_rows, reciprocal_deviation, gradient_rows
):
    unit_gradient = normed_gradient * gain_vector
    inner_product = (
        unit_gradient
        - jnp.mean(unit_gradient, axis=1, keepdims=True)
        - unit_rows * jnp.mean(unit_gradient * unit_rows, axis=1, keepdims=True)
    )
    return (gradient_rows.astype(jnp.float32) + reciprocal_deviation * inner_product).astype(
        jnp.bfloat16
    )


def panel_terms(first_blocks, second_blocks, row_table, col_table, normed_rows, gradient_rows):
    tok_rows = normed_rows.shape[0]
    width_blocks = D // BLK
    block_ids = jnp.arange(width_blocks, dtype=jnp.int32)[None, None, :]
    row_place = (row_table[:, :, None] == block_ids).astype(jnp.float32)
    col_place = (col_table[:, :, None] == block_ids).astype(jnp.float32)
    normed_sel = jnp.take(normed_rows.reshape(tok_rows, width_blocks, BLK), row_table, axis=1)
    pre = jnp.einsum("tcnk,cnkj->tcj", normed_sel, first_blocks, preferred_element_type=jnp.float32)
    act = jax.nn.gelu(pre, approximate=False).astype(jnp.bfloat16)
    forward_part = jnp.einsum(
        "tck,cnkj->tcnj", act, second_blocks, preferred_element_type=jnp.float32
    )
    mlp_part = jnp.einsum(
        "tcnj,cnb->tbj", forward_part, col_place, precision=lax.Precision.HIGHEST
    ).reshape(tok_rows, D)
    grad_sel = jnp.take(gradient_rows.reshape(tok_rows, width_blocks, BLK), col_table, axis=1)
    dact = jnp.einsum("tcnj,cnkj->tck", grad_sel, second_blocks, preferred_element_type=jnp.float32)
    dpre = (dact * gelu_slope(pre)).astype(jnp.bfloat16)
    back_part = jnp.einsum("tcj,cnkj->tcnk", dpre, first_blocks, preferred_element_type=jnp.float32)
    dnormed_part = jnp.einsum(
        "tcnk,cnb->tbk", back_part, row_place, precision=lax.Precision.HIGHEST
    ).reshape(tok_rows, D)
    return (mlp_part, dnormed_part)


def body(
    tokens,
    queries,
    keys,
    values,
    attn_mask,
    out_proj,
    norm_gain_vector,
    w1_packed,
    w1_rows,
    w2_packed,
    w2_cols,
    grad_out,
):
    rows_in = tokens[0]
    query = queries[0]
    gradient_rows = grad_out[0]
    allowed = expand_mask(attn_mask[0])
    key_rows, value_rows = (
        lax.all_gather(keys[0], "seq", axis=0, tiled=True),
        lax.all_gather(values[0], "seq", axis=0, tiled=True),
    )
    attn = attend_forward(query, key_rows, value_rows, allowed)
    hidden_state = rows_in.astype(jnp.float32) + jnp.dot(
        attn, out_proj, preferred_element_type=jnp.float32
    )
    unit_rows, reciprocal_deviation, normed_rows = layer_norm_forward(
        hidden_state, norm_gain_vector
    )
    first_all, second_all = (
        lax.all_gather(w1_packed, "grp", axis=0, tiled=True),
        lax.all_gather(w2_packed, "grp", axis=0, tiled=True),
    )
    mlp, normed_gradient = panel_terms(
        first_all, second_all, w1_rows, w2_cols, normed_rows, gradient_rows
    )
    result = (hidden_state + mlp).astype(jnp.bfloat16)
    incoming_gradient_rows = layer_norm_backward(
        normed_gradient, norm_gain_vector, unit_rows, reciprocal_deviation, gradient_rows
    )
    return (result[None], incoming_gradient_rows[None])


def solution(mesh):
    return jax.shard_map(
        body,
        mesh=mesh,
        in_specs=(
            P("grp", "seq", None),
            P("grp", "seq", None),
            P("grp", "seq", None),
            P("grp", "seq", None),
            P("grp", "seq", None),
            P(),
            P(),
            P("grp", None, None, None),
            P(),
            P("grp", None, None, None),
            P(),
            P("grp", "seq", None),
        ),
        out_specs=(P("grp", "seq", None), P("grp", "seq", None)),
        check_vma=False,
    )
```

profile of v0, /device:TPU:1, one launch (start us, length us, event | category | flops | bytes accessed | tf_op | source)
XLA Modules:
  0.0 173.2 jit_solution(16410536072970037898)
XLA Ops:
  7.2 1.8 %copy.46 = bf16[1,128,512]{1,2,0:T(8,128)(2,1)} copy(bf16[1,128,512]{2,1,0:T(8,128)(2,1)} %param.18) | data formatting | bytes 262144 | tf_op args[2]
  9.1 1.7 copy.47
  17.6 2.2 %gather_fusion.1 = bf16[64,128,128]{2,1,0:T(8,128)(2,1)} fusion(bf16[128,8,128]{2,0,1:T(8,128)(2,1)S(1)} %copy.58, s32[1024]{0:T(1024)S(1)} %pad_clamp_fusion), kind=kCustom, calls=%fused_computation.1.clone | custom fusion | bytes 4194560 | tf_op jit(solution)/shard_map/jit(_take)/gather | solution.py:91
  19.8 30.1 %all-gather.11.cloned.1.call-done = bf16[1,1024,512]{1,2,0:T(8,128)(2,1)} async-done(((bf16[1,128,512]{1,2,0:T(8,128)(2,1)}), bf16[1,1024,512]{1,2,0:T(8,128)(2,1)}) %all-gather.11.cloned.1.call-update) | async-done | bytes 1048592 | tf_op jit(solution)/shard_map/all_gather | solution.py:120
  49.9 41.1 %all-gather.13.cloned.1.call-done = bf16[1,1024,512]{1,2,0:T(8,128)(2,1)} async-done(((bf16[1,128,512]{1,2,0:T(8,128)(2,1)}), bf16[1,1024,512]{1,2,0:T(8,128)(2,1)}) %all-gather.13.cloned.1.call-update) | async-done | bytes 1048592 | tf_op jit(solution)/shard_map/all_gather | solution.py:121
  90.9 21.8 %while.11 = (s32[]{:T(128)}, bf16[8,128,64]{1,2,0:T(8,128)(2,1)S(1)}, bf16[8,128,64]{1,2,0:T(8,128)(2,1)S(1)}, bf16[8,1024,64]{1,2,0:T(8,128)(2,1)}, bf16[8,1024...) while((s32[]{:T(128)}, bf16[8,128,64]{1,2,0:T(8,128)(2,1)S(1)}, ...), condition=%wide.region_3.4_spmd.clone, body=%wide.region_0.3_spmd.clone.sunk | while | flops 34602752 | bytes 1889877 | solution.py:46
  90.9 1.3 fusion.158
  93.7 1.2 fusion.158
  96.4 1.2 fusion.158
  97.9 1.2 fusion.160
  99.1 1.2 fusion.158
  100.6 1.2 fusion.160
  101.9 1.3 fusion.158
  103.4 1.2 fusion.160
  104.6 1.2 fusion.158
  107.3 1.2 fusion.158
  110.1 1.2 fusion.158
  113.6 2.2 %gather_fusion = bf16[64,128,128]{2,1,0:T(8,128)(2,1)} fusion(bf16[128,8,128]{2,0,1:T(8,128)(2,1)S(1)} %copy_bitcast_fusion, s32[1024]{0:T(1024)S(1)} %pad_clamp_fusion.1), kind=kCustom, calls=%fused_computation.clone | custom fusion | bytes 4194560 | tf_op jit(solution)/shard_map/jit(_take)/gather | solution.py:82
  116.9 4.3 %fusion.32 = f32[32,128,128,1]{2,1,3,0:T(8,128)} fusion(bf16[32,2,128,128]{3,2,1,0:T(8,128)(2,1)} %all-gather.7.cloned.1.call-done, bf16[32,2,128,128]{3,2,1,0:T(8,128)(2,1)} %bitcast.199, pred[32,2]{1,0:T(8,128)(4,1)S(1)} %copy.51), kind=kOutput, calls=%fused_computation.44 | convolution fusion | flops 269484032 | bytes 6291520 | tf_op jit(solution)/shard_map/tcnk,cnkj->tcj/dot_general | solution.py:83
  121.2 19.8 %all-gather.9.cloned.1.call-done = bf16[32,2,128,128]{3,2,1,0:T(8,128)(2,1)} async-done(((bf16[8,2,128,128]{3,2,1,0:T(8,128)(2,1)}), bf16[32,2,128,128]{3,2,1,0:T(8,128)(2,1)}) %all-gather.9.cloned.1.call-update) | async-done | bytes 2097168 | tf_op jit(solution)/shard_map/all_gather | solution.py:132
  141.0 6.8 %convolution_bitcast_fusion.2 = f32[128,32,2,128]{3,0,2,1:T(8,128)S(1)} fusion(bf16[32,2,128,128]{3,2,1,0:T(8,128)(2,1)} %all-gather.9.cloned.1.call-done, f32[32,128,128,1]{2,1,3,0:T(8,128)} %fusion.32), kind=kOutput, calls=%fused_computation.25 | convolution fusion | flops 302514176 | bytes 8388608 | tf_op jit(solution)/shard_map/tck,cnkj->tcnj/dot_general | solution.py:85
  147.8 3.8 %fusion.15 = f32[8,128,128,1]{2,0,3,1:T(8,128)S(1)} fusion(f32[128,32,2,128]{3,0,2,1:T(8,128)S(1)} %convolution_bitcast_fusion.2, s32[32,2]{0,1:T(2,128)S(1)} %copy-done.4), kind=kOutput, calls=%fused_computation.20 | convolution fusion | flops 100663808 | bytes 4718848 | tf_op jit(solution)/shard_map/tcnj,cnb->tbj/dot_general | solution.py:88
  151.6 7.2 %convolution_bitcast_fusion.1 = f32[128,32,2,128]{3,0,2,1:T(8,128)} fusion(bf16[32,2,128,128]{3,2,1,0:T(8,128)(2,1)} %all-gather.7.cloned.1.call-done, f32[32,128,128,1]{2,1,3,0:T(8,128)} %fusion.32, bf16[32,2,128,128]{3,2,1,0:T(8,128)(2,1)} %all-gather.9.cloned.1.call-done, bf16[32,2,128,128]{3,2,1,0:T(8,128)(2,1)} %bitcast.202, pred[32,2]{1,0:T(8,128)(4,1)S(1)} %copy.55), kind=kOutput, calls=%fused_computation.24 | convolution fusion | flops 543162368 | bytes 12582976 | tf_op jit(solution)/shard_map/tcj,cnkj->tcnk/dot_general | solution.py:94
  158.8 6.6 %fusion.96 = (f32[128]{0:T(128)S(1)}, f32[8,128,128,1]{2,0,3,1:T(8,128)S(1)}) fusion(f32[8,128]{1,0:T(8,128)S(1)} %bitcast.208, f32[128,32,2,128]{3,0,2,1:T(8,128)} %convolution_bitcast_fusion.1, s32[32,2]{0,1:T(2,128)S(1)} %copy-done.5), kind=kOutput, calls=%fused_computation.111 | convolution fusion | flops 100925824 | bytes 4723456 | tf_op jit(solution)/shard_map/tcnk,cnb->tbk/dot_general | solution.py:95
  (60 shorter events, 18.0 us)
Async XLA Ops:
  7.2 105.6 %copy-start = (bf16[512,1024]{1,0:T(8,128)(2,1)S(1)}, bf16[512,1024]{1,0:T(8,128)(2,1)}, u32[]{:S(2)}) copy-start(bf16[512,1024]{1,0:T(8,128)(2,1)} %param.21) | copy-start | bytes 3145732
  7.2 10.0 %copy-start.1 = (bf16[1,128,1024]{2,1,0:T(8,128)(2,1)S(1)}, bf16[1,128,1024]{2,1,0:T(8,128)(2,1)}, u32[]{:S(2)}) copy-start(bf16[1,128,1024]{2,1,0:T(8,128)(2,1)} %param.27) | copy-start | bytes 786436
  7.2 42.7 %all-gather.11.cloned.1.call-start = ((), (), s32[]{:S(2)}) async-start(), calls=%async_computation.2 | async-start | bytes 1179648 | tf_op jit(solution)/shard_map/all_gather | solution.py:120
  9.0 81.9 %all-gather.13.cloned.1.call-start = ((), (), s32[]{:S(2)}) async-start(), calls=%async_computation.3 | async-start | bytes 1179648 | tf_op jit(solution)/shard_map/all_gather | solution.py:121
  10.8 106.1 %all-gather.7.cloned.1.call-start = ((), (), s32[]{:S(2)}) async-start(), calls=%async_computation | async-start | bytes 2621440 | tf_op jit(solution)/shard_map/all_gather | solution.py:131
  11.5 129.5 %all-gather.9.cloned.1.call-start = ((), (), s32[]{:S(2)}) async-start(), calls=%async_computation.1 | async-start | bytes 2621440 | tf_op jit(solution)/shard_map/all_gather | solution.py:132
  90.9 21.9 %copy-start.2 = (bf16[1,128,1024]{2,1,0:T(8,128)(2,1)S(1)}, bf16[1,128,1024]{2,1,0:T(8,128)(2,1)}, u32[]{:S(2)}) copy-start(bf16[1,128,1024]{2,1,0:T(8,128)(2,1)} %param.16) | copy-start | bytes 786436
  112.8 0.7 copy-start.3
  121.2 26.6 %copy-start.4 = (s32[32,2]{0,1:T(2,128)S(1)}, s32[32,2]{0,1:T(2,128)}, u32[]{:S(2)}) copy-start(s32[32,2]{0,1:T(2,128)} %param.26) | copy-start | bytes 772
  151.6 7.2 %copy-start.5 = (s32[32,2]{0,1:T(2,128)S(1)}, s32[32,2]{0,1:T(2,128)}, u32[]{:S(2)}) copy-start(s32[32,2]{0,1:T(2,128)} %param.24) | copy-start | bytes 772
Sparse Core Ops, SparseCore 0:
  10.6 39.1 all-gather.10
  52.5 38.4 all-gather.12
  92.5 24.3 all-gather.6
  118.3 22.6 all-gather.8
where the time goes:
time: 174 us; the launch traced here: 173 us
  waiting for transfers between devices  93.3 us (54%)
  matrix products  48.9 us (28%)
  between operations  13.9 us (8%)
  local copies, waits for them, and re-layouts  9.87 us (6%)
  other arithmetic  6.95 us (4%)
    all_gather x1, waiting for transfers between devices, body(): lax.all_gather(values[0], 'seq', axis=0, tiled=True)  41.1 us
    all_gather x1, waiting for transfers between devices, body(): lax.all_gather(keys[0], 'seq', axis=0, tiled=True)  30.1 us
    all_gather x1, waiting for transfers between devices, body(): lax.all_gather(w2_packed, 'grp', axis=0, tiled=True)  19.8 us
    dot_general x8, matrix products, one_head(): jnp.dot(q_head, k_head.T, preferred_element_type=jnp.float32) * scale  9.98 us
    dot_general x8, matrix products, one_head(): return jnp.dot(prob, v_head, preferred_element_type=jnp.float32)  9.81 us
    dot_general x1, matrix products, panel_terms(): jnp.einsum('tcj,cnkj->tcnk', dpre, first_blocks, preferred_element_type=j...  7.17 us
    dot_general x1, matrix products, panel_terms(): jnp.einsum('tck,cnkj->tcnj', act, second_blocks, preferred_element_type=j...  6.77 us
    dot_general x1, matrix products, panel_terms(): jnp.einsum('tcnk,cnb->tbk', back_part, row_place, precision=lax.Precision...  6.59 us
  transfers between devices with their start and end apart: 4, of which 4 were waited for; matrix products, arithmetic and copies ran while one was open for 22% of the time, Pallas kernels for 0%

commit v1 on v0

v1 whole, which is shorter than its diff:
```python
import functools

import jax
import jax.numpy as jnp
from jax import lax
from jax.experimental import pallas as pl
from jax.experimental.pallas import tpu as pltpu
from jax.sharding import PartitionSpec as P

HD = 64
BLK = 128
NNZ = 2
LANES = 128
QUADS = 4
HEAD_BIT = 2
NT = (((1,), (1,)), ((), ()))
VMEM_LIMIT = 24 * 1024 * 1024
PACK_LIMIT = 59 * 1024 * 1024


def vmem():
    return pl.BlockSpec(memory_space=pltpu.VMEM)


def smem():
    return pl.BlockSpec(memory_space=pltpu.SMEM)


def hbm():
    return pl.BlockSpec(memory_space=pltpu.HBM)


def flips_of(seq_size):
    flips = [0]
    bit = 1
    while bit < seq_size:
        if bit not in (HEAD_BIT, 2 * HEAD_BIT):
            flips = flips + [f ^ bit for f in flips]
        bit *= 2
    return flips


def exchange(x, axis, size, flip):
    return lax.ppermute(x, axis, [(i, i ^ flip) for i in range(size)])


def after(x, *earlier):
    return lax.optimization_barrier((x, *earlier))[0]


def butterfly(x, axis, size, bits):
    held = [x]
    for bit in bits:
        held = held + [exchange(part, axis, size, bit) for part in held]
    return held


def mask_rows(seq_size):
    return 16 * ((seq_size + 15) // 16)


def pack_kernel(seq_size, q_ref, k_ref, v_ref, mask_ref, w1_ref, w2_ref, *outs):
    outs, joined_ref, sems = outs[:QUADS], outs[QUADS], outs[QUADS + 1]
    me = lax.axis_index("seq")
    group = lax.rem(me // HEAD_BIT, QUADS)
    rows = mask_rows(seq_size)
    half = w1_ref.shape[0]
    copies = []

    def start(source, target):
        copies.append(pltpu.make_async_copy(source, target, sems.at[len(copies)]))
        copies[-1].start()

    for s in range(QUADS):
        cols = pl.ds(pl.multiple_of(lax.bitwise_xor(group, s) * LANES, LANES), LANES)
        for i, ref in enumerate((q_ref, k_ref, v_ref)):
            start(ref.at[0, :, cols], outs[s].at[pl.ds(i * BLK, BLK)])
    start(w1_ref, joined_ref.at[pl.ds(0, half)])
    start(w2_ref, joined_ref.at[pl.ds(half, half)])
    row_id = lax.broadcasted_iota(jnp.int32, (rows, LANES), 0)
    for s in range(QUADS):
        there = lax.bitwise_xor(me, s * HEAD_BIT)
        allowed = jnp.zeros((rows, LANES), jnp.float32)
        for t, flip in enumerate(flips_of(seq_size)):
            for u in range(QUADS):
                block = lax.bitwise_xor(there, flip ^ (u * HEAD_BIT))
                bit = mask_ref[0, 0, block].astype(jnp.float32)
                allowed = jnp.where(row_id == t * QUADS + u, bit, allowed)
        outs[s][3 * BLK :, :] = allowed.astype(jnp.bfloat16)
    for copy in copies:
        copy.wait()


def pack(query, key, value, attn_mask, w1_packed, w2_packed, seq_size):
    rows = 3 * BLK + mask_rows(seq_size)
    joined = (2 * w1_packed.shape[0], *w1_packed.shape[1:])
    outs = pl.pallas_call(
        functools.partial(pack_kernel, seq_size),
        out_shape=[jax.ShapeDtypeStruct((rows, LANES), jnp.bfloat16)] * QUADS
        + [jax.ShapeDtypeStruct(joined, jnp.bfloat16)],
        in_specs=[hbm(), hbm(), hbm(), smem(), hbm(), hbm()],
        out_specs=[vmem()] * (QUADS + 1),
        scratch_shapes=[pltpu.SemaphoreType.DMA((3 * QUADS + 2,))],
        compiler_params=pltpu.CompilerParams(vmem_limit_bytes=PACK_LIMIT),
        name="pack",
    )(query, key, value, attn_mask, w1_packed, w2_packed)
    return outs[:QUADS], outs[QUADS]


def attend_kernel(first, last, parts, *refs):
    q_refs, refs = refs[:QUADS], refs[QUADS:]
    if not first:
        kv_refs, refs = refs[: QUADS * parts], refs[QUADS * parts :]
        state_refs, refs = refs[:3], refs[3:]
    scale = HD**-0.5 * 1.4426950408889634
    first_head = lax.broadcasted_iota(jnp.int32, (BLK, LANES), 1) < HD
    for s in range(QUADS):
        q = q_refs[s][0:BLK, :]
        zero = jnp.zeros_like(q)
        both = jnp.concatenate(
            [jnp.where(first_head, q, zero), jnp.where(first_head, zero, q)], axis=0
        )
        allowed = q_refs[s][3 * BLK :, :].astype(jnp.float32)
        if first:
            pairs = [(q_refs[u][BLK : 2 * BLK, :], q_refs[u][2 * BLK : 3 * BLK, :]) for u in range(QUADS)]
            base = 0
        else:
            pairs = [(ref[0:BLK, :], ref[BLK : 2 * BLK, :]) for ref in kv_refs]
            base = QUADS
        scores = []
        for row, (key, _) in enumerate(pairs):
            dots = lax.dot_general(both, key, NT, preferred_element_type=jnp.float32)
            scores.append(jnp.where(allowed[base + row : base + row + 1, :] > 0, dots, -1e30))
        top = functools.reduce(jnp.maximum, scores)
        if not first:
            top = jnp.maximum(top, state_refs[0][s])
        top = jnp.max(top, axis=1, keepdims=True)
        if first:
            total = jnp.zeros((2 * BLK, LANES), jnp.float32)
            mixed = jnp.zeros((2 * BLK, LANES), jnp.float32)
        else:
            shrink = jnp.exp2((state_refs[0][s] - top) * scale)
            total = state_refs[1][s] * shrink
            mixed = state_refs[2][s] * shrink
        for score, (_, value) in zip(scores, pairs):
            weight = jnp.exp2((score - top) * scale)
            total = total + weight
            mixed = mixed + jnp.dot(
                weight.astype(jnp.bfloat16), value, preferred_element_type=jnp.float32
            )
        if last:
            mixed = mixed / jnp.sum(total, axis=1, keepdims=True)
            refs[s][...] = jnp.where(first_head, mixed[:BLK], mixed[BLK:]).astype(jnp.bfloat16)
        else:
            refs[0][s] = jnp.broadcast_to(top, (2 * BLK, LANES))
            refs[1][s] = total
            refs[2][s] = mixed


def attend_own(packed):
    return pl.pallas_call(
        functools.partial(attend_kernel, True, False, 1),
        out_shape=[jax.ShapeDtypeStruct((QUADS, 2 * BLK, LANES), jnp.float32)] * 3,
        in_specs=[vmem()] * QUADS,
        out_specs=[vmem()] * 3,
        compiler_params=pltpu.CompilerParams(vmem_limit_bytes=VMEM_LIMIT),
        name="attend_own",
    )(*packed)


def attend_rest(packed, rest, state):
    return pl.pallas_call(
        functools.partial(attend_kernel, False, True, len(rest) // QUADS),
        out_shape=[jax.ShapeDtypeStruct((BLK, LANES), jnp.bfloat16)] * QUADS,
        in_specs=[vmem()] * (QUADS + len(rest) + 3),
        out_specs=[vmem()] * QUADS,
        compiler_params=pltpu.CompilerParams(vmem_limit_bytes=VMEM_LIMIT),
        name="attend_rest",
    )(*packed, *rest, *state)


def block_of(index):
    return pl.ds(pl.multiple_of(index * BLK, BLK), BLK)


def mlp_kernel(owners, rows_ref, cols_ref, *refs):
    attn_refs, refs = refs[:QUADS], refs[QUADS:]
    proj_ref, tokens_ref, gain_ref, grad_ref = refs[:4]
    weight_refs, refs = refs[4 : 4 + owners], refs[4 + owners :]
    out_ref, grad_out_ref, normed_ref, mlp_ref, back_ref, act_ref, dpre_ref, held_ref, sems = refs
    copies = [
        pltpu.make_async_copy(weight_refs[s], held_ref.at[s], sems.at[s]) for s in range(owners)
    ]
    for copy in copies:
        copy.start()
    blocks = held_ref.shape[1] // 2
    group = lax.rem(lax.axis_index("seq") // HEAD_BIT, QUADS)
    hidden = tokens_ref[0].astype(jnp.float32)
    for s in range(QUADS):
        hidden = hidden + jnp.dot(
            attn_refs[s][...],
            proj_ref[block_of(lax.bitwise_xor(group, s)), :],
            preferred_element_type=jnp.float32,
        )
    gain = gain_ref[...]
    mean = jnp.mean(hidden, axis=1, keepdims=True)
    centred = hidden - mean
    rstd = lax.rsqrt(jnp.mean(centred * centred, axis=1, keepdims=True) + 1e-06)
    unit = centred * rstd
    normed_ref[...] = (unit * gain).astype(jnp.bfloat16)
    mlp_ref[...] = hidden
    back_ref[...] = jnp.zeros_like(back_ref)
    me = lax.axis_index("grp")
    steps = [(s, c) for s in range(owners) for c in range(blocks)]

    def places(table_ref, s, c):
        block = lax.bitwise_xor(me, s) * blocks + c
        return [block_of(table_ref[n, block]) for n in range(NNZ)]

    for i, (s, c) in enumerate(steps):
        if c == 0:
            copies[s].wait()
        picked = jnp.concatenate([normed_ref[:, r] for r in places(rows_ref, s, c)], axis=1)
        grads = jnp.concatenate([grad_ref[0, :, r] for r in places(cols_ref, s, c)], axis=1)
        first = held_ref[s, c].reshape(NNZ * BLK, BLK)
        second = jnp.concatenate([held_ref[s, blocks + c, n] for n in range(NNZ)], axis=1)
        pre = jnp.dot(picked, first, preferred_element_type=jnp.float32)
        dact = lax.dot_general(grads, second, NT, preferred_element_type=jnp.float32)
        cdf = 0.5 * (1.0 + lax.erf(pre * 0.7071067811865476))
        slope = cdf + pre * jnp.exp(-0.5 * pre * pre) * 0.3989422804014327
        act_ref[i] = (pre * cdf).astype(jnp.bfloat16)
        dpre_ref[i] = (dact * slope).astype(jnp.bfloat16)
    for i, (s, c) in enumerate(steps):
        first = held_ref[s, c].reshape(NNZ * BLK, BLK)
        second = jnp.concatenate([held_ref[s, blocks + c, n] for n in range(NNZ)], axis=1)
        forward = jnp.dot(act_ref[i], second, preferred_element_type=jnp.float32)
        backward = lax.dot_general(dpre_ref[i], first, NT, preferred_element_type=jnp.float32)
        for n, col in enumerate(places(cols_ref, s, c)):
            mlp_ref[:, col] += forward[:, n * BLK : (n + 1) * BLK]
        for n, row in enumerate(places(rows_ref, s, c)):
            back_ref[:, row] += backward[:, n * BLK : (n + 1) * BLK]
    out_ref[0] = mlp_ref[...].astype(jnp.bfloat16)
    dxhat = back_ref[...] * gain
    dhidden = (
        dxhat
        - jnp.mean(dxhat, axis=1, keepdims=True)
        - unit * jnp.mean(dxhat * unit, axis=1, keepdims=True)
    )
    grad_out_ref[0] = (grad_ref[0].astype(jnp.float32) + rstd * dhidden).astype(jnp.bfloat16)


def mlp(w1_rows, w2_cols, attn, out_proj, tokens, gain, grad_out, weights):
    owners = len(weights)
    shape = tokens.shape
    hidden_blocks = w1_rows.shape[1]
    near = (*attn, out_proj, tokens, gain, grad_out)
    return pl.pallas_call(
        functools.partial(mlp_kernel, owners),
        out_shape=[jax.ShapeDtypeStruct(shape, jnp.bfloat16)] * 2,
        in_specs=[smem()] * 2 + [vmem()] * len(near) + [hbm()] * owners,
        out_specs=[vmem()] * 2,
        scratch_shapes=[
            pltpu.VMEM(shape[1:], jnp.bfloat16),
            pltpu.VMEM(shape[1:], jnp.float32),
            pltpu.VMEM(shape[1:], jnp.float32),
            pltpu.VMEM((hidden_blocks, BLK, BLK), jnp.bfloat16),
            pltpu.VMEM((hidden_blocks, BLK, BLK), jnp.bfloat16),
            pltpu.VMEM((owners, *weights[0].shape), jnp.bfloat16),
            pltpu.SemaphoreType.DMA((owners,)),
        ],
        compiler_params=pltpu.CompilerParams(vmem_limit_bytes=VMEM_LIMIT),
        name="mlp",
    )(w1_rows, w2_cols, *near, *weights)


def body(
    seq_size,
    grp_size,
    tokens,
    queries,
    keys,
    values,
    attn_mask,
    out_proj,
    norm_gain_vector,
    w1_packed,
    w1_rows,
    w2_packed,
    w2_cols,
    grad_out,
):
    grp_bits = []
    bit = grp_size // 2
    while bit:
        grp_bits.append(bit)
        bit //= 2
    flips = [f for f in flips_of(seq_size) if f and f & (f - 1) == 0]

    packed, joined = pack(queries, keys, values, attn_mask, w1_packed, w2_packed, seq_size)
    weights = {0: joined, grp_bits[0]: exchange(joined, "grp", grp_size, grp_bits[0])}
    packed = [packed[0]] + [
        exchange(packed[s], "seq", seq_size, s * HEAD_BIT) for s in range(1, QUADS)
    ]
    own = [p[BLK : 3 * BLK] for p in packed]
    held = [butterfly(part, "seq", seq_size, flips) for part in own]
    for bit in grp_bits[1:]:
        weights[bit] = exchange(after(joined, *packed[1:]), "grp", grp_size, bit)
    state = attend_own(packed)
    rest = [held[u][t] for t in range(1, len(held[0])) for u in range(QUADS)]
    attn = attend_rest(packed, rest, state)
    attn = [attn[0]] + [exchange(attn[s], "seq", seq_size, s * HEAD_BIT) for s in range(1, QUADS)]
    masks = [0]
    for bit in grp_bits:
        for m in masks:
            if m ^ bit not in weights:
                weights[m ^ bit] = exchange(after(weights[m], *attn[1:]), "grp", grp_size, bit)
        masks = masks + [m ^ bit for m in masks]
    output, grad_tokens = mlp(
        w1_rows.T,
        w2_cols.T,
        attn,
        out_proj,
        tokens,
        norm_gain_vector[None],
        grad_out,
        [weights[m] for m in range(grp_size)],
    )
    return (output, grad_tokens)


def solution(mesh):
    return jax.shard_map(
        functools.partial(body, mesh.shape["seq"], mesh.shape["grp"]),
        mesh=mesh,
        in_specs=(
            P("grp", "seq", None),
            P("grp", "seq", None),
            P("grp", "seq", None),
            P("grp", "seq", None),
            P("grp", "seq", None),
            P(),
            P(),
            P("grp", None, None, None),
            P(),
            P("grp", None, None, None),
            P(),
            P("grp", "seq", None),
        ),
        out_specs=(P("grp", "seq", None), P("grp", "seq", None)),
        check_vma=False,
    )
```

time: 174 us -> 45.1 us (0.26)
  waiting for transfers between devices: 93.3 us -> 6.59 us
  matrix products: 48.9 us -> 0 us
  starting transfers between devices: 0.16 us -> 23.6 us
  between operations: 13.9 us -> 0.74 us
  Pallas kernels: 0 us -> 12.1 us
  local copies, waits for them, and re-layouts: 9.87 us -> 1.54 us
  other arithmetic: 6.95 us -> 0 us
    all_gather x4 -> x0, waiting for transfers between devices: 92 us -> none  [the longest x1 41.1 us: body(): lax.all_gather(values[0], 'seq', axis=0, tiled=True)]
    dot_general x22 -> x0, matrix products: 48.9 us -> none  [the longest x8 9.98 us: one_head(): jnp.dot(q_head, k_head.T, preferred_element_type=jnp.float32) * scale]
    ppermute x0 -> x13, starting transfers between devices: none -> 23.6 us  [exchange(): return lax.ppermute(x, axis, [(i, i ^ flip) for i in range(size)])]
    pallas_call x0 -> x4, Pallas kernels: none -> 12.1 us  [the longest x1 6.23 us: mlp(): pl.pallas_call(functools.partial(mlp_kernel, owners), out_shape=[jax.Shap...]
    ppermute x0 -> x13, waiting for transfers between devices: none -> 6.59 us  [exchange(): return lax.ppermute(x, axis, [(i, i ^ flip) for i in range(size)])]
    gather x2 -> x0, local copies, waits for them, and re-layouts: 4.35 us -> none  [the longest x1 2.18 us: panel_terms(): jnp.take(gradient_rows.reshape(tok_rows, width_blocks, BLK), col_table, a...]
    unnamed x16, local copies, waits for them, and re-layouts: 4.68 us -> 0.68 us
    reduce_sum x10 -> x0, other arithmetic: 2.31 us -> none  [the longest x8 1.88 us: one_head(): total = jnp.sum(weight, axis=1, keepdims=True)]
  transfers between devices with their start and end apart: 4 -> 13, of which waited for: 4 -> 4; matrix products, arithmetic and copies ran while one was open for 22% -> 2% of each run, Pallas kernels for 0% -> 6%
where the time goes in v1:
time: 45.1 us; the launch traced here: 44.6 us
  starting transfers between devices  23.6 us (52%)
  Pallas kernels  12.1 us (27%)
  waiting for transfers between devices  6.59 us (15%)
  local copies, waits for them, and re-layouts  1.54 us (3%)
  between operations  0.74 us (2%)
    ppermute x13, starting transfers between devices, exchange(): return lax.ppermute(x, axis, [(i, i ^ flip) for i in range(size)])  23.6 us
    ppermute x13, waiting for transfers between devices, exchange(): return lax.ppermute(x, axis, [(i, i ^ flip) for i in range(size)])  6.59 us
    pallas_call x1, Pallas kernels, mlp(): pl.pallas_call(functools.partial(mlp_kernel, owners), out_shape=[jax.Shap...  6.23 us
    pallas_call x1, Pallas kernels, pack(): pl.pallas_call(functools.partial(pack_kernel, seq_size), out_shape=[jax.S...  3.37 us
    pallas_call x1, Pallas kernels, attend_rest(): pl.pallas_call(functools.partial(attend_kernel, False, True, len(rest) //...  1.36 us
    pallas_call x1, Pallas kernels, attend_own(): pl.pallas_call(functools.partial(attend_kernel, True, False, 1), out_shap...  1.14 us
  transfers between devices with their start and end apart: 13, of which 4 were waited for; matrix products, arithmetic and copies ran while one was open for 2% of the time, Pallas kernels for 6%

profile of v1, /device:TPU:1, one launch (start us, length us, event | category | flops | bytes accessed | tf_op | source)
XLA Modules:
  0.0 44.6 jit_solution(3693302501252441662)
XLA Ops:
  0.6 3.4 %pack.1 = (bf16[400,128]{1,0:T(8,128)(2,1)}, bf16[400,128]{1,0:T(8,128)(2,1)}, bf16[400,128]{1,0:T(8,128)(2,1)}, bf16[400,128]{1,0:T(8,128)(2,1)}, bf16[16,2,128,128]{3,2,1,0:T(8,128)(2,1)}) custom-call(bf16[1,128,512]{2,1,0:T(8,128)(2,1)} %q_ref.1, bf16[1,128,512]{2,1,0:T(8,128)(2,1)} %k_ref.1, bf16[1,128,512]{2,1,0:T(8,128)(2,1)} %v_ref.1, ...), custom_call_target="tpu_custom_call" | custom-call | tf_op jit(solution)/shard_map/pack/pallas_call | solution.py:97
  4.0 2.1 %collective-permute-start.11 = (bf16[16,2,128,128]{3,2,1,0:T(8,128)(2,1)}, bf16[16,2,128,128]{3,2,1,0:T(8,128)(2,1)S(1)}, u32[]{:S(2)}, u32[]{:S(2)}) collective-permute-start(bf16[16,2,128,128]{3,2,1,0:T(8,128)(2,1)} %get-tuple-element.28.refs_8_), channel_id=1, source_target_pairs={{0,16},{8,24},{16,0},{24,8},{1,17},{9,25},{17,1},{25,9},{2,18},{10... | collective-permute-start | bytes 3145736 | tf_op jit(solution)/shard_map/ppermute | solution.py:44
  6.1 1.3 %collective-permute-start = (bf16[400,128]{1,0:T(8,128)(2,1)}, bf16[400,128]{1,0:T(8,128)(2,1)S(1)}, u32[]{:S(2)}, u32[]{:S(2)}) collective-permute-start(bf16[400,128]{1,0:T(8,128)(2,1)} %get-tuple-element.17), channel_id=1, source_target_pairs={{0,2},{1,3},{2,0},{3,1},{4,6},{5,7},{6,4},{7,5},{8,10},{9,11},{10,... | collective-permute-start | bytes 307208 | tf_op jit(solution)/shard_map/ppermute | solution.py:44
  7.4 2.3 %collective-permute-start.1 = (bf16[400,128]{1,0:T(8,128)(2,1)}, bf16[400,128]{1,0:T(8,128)(2,1)S(1)}, u32[]{:S(2)}, u32[]{:S(2)}) collective-permute-start(bf16[400,128]{1,0:T(8,128)(2,1)} %get-tuple-element.18), channel_id=1, source_target_pairs={{0,4},{1,5},{2,6},{3,7},{4,0},{5,1},{6,2},{7,3},{8,12},{9,13},{10,... | collective-permute-start | bytes 307208 | tf_op jit(solution)/shard_map/ppermute | solution.py:44
  9.8 0.0 collective-permute-start.2
  9.8 0.8 %slice.12 = bf16[256,128]{1,0:T(8,128)(2,1)S(1)} slice(bf16[400,128]{1,0:T(8,128)(2,1)} %get-tuple-element.16.refs_0_), slice={[128:384], [0:128]} | slice | bytes 131072 | tf_op jit(solution)/shard_map/slice | solution.py:304
  10.6 1.2 %collective-permute-start.3 = (bf16[256,128]{1,0:T(8,128)(2,1)S(1)}, bf16[256,128]{1,0:T(8,128)(2,1)S(1)}, u32[]{:S(2)}, u32[]{:S(2)}) collective-permute-start(bf16[256,128]{1,0:T(8,128)(2,1)S(1)} %slice.12), channel_id=1, source_target_pairs={{0,1},{1,0},{2,3},{3,2},{4,5},{5,4},{6,7},{7,6},{8,9},{9,8},{10,11... | collective-permute-start | bytes 196616 | tf_op jit(solution)/shard_map/ppermute | solution.py:44
  11.8 0.0 copy-start.2
  11.8 0.3 collective-permute-start.4
  12.2 0.4 collective-permute-done.1.refs_2_
  12.6 1.2 %collective-permute-start.5 = (bf16[256,128]{1,0:T(8,128)(2,1)S(1)}, bf16[256,128]{1,0:T(8,128)(2,1)S(1)}, u32[]{:S(2)}, u32[]{:S(2)}) collective-permute-start(bf16[256,128]{1,0:T(8,128)(2,1)S(1)} %slice.17), channel_id=1, source_target_pairs={{0,1},{1,0},{2,3},{3,2},{4,5},{5,4},{6,7},{7,6},{8,9},{9,8},{10,11... | collective-permute-start | bytes 196616 | tf_op jit(solution)/shard_map/ppermute | solution.py:44
  13.8 2.8 %collective-permute-done.2.refs_3_ = bf16[400,128]{1,0:T(8,128)(2,1)S(1)} collective-permute-done((bf16[400,128]{1,0:T(8,128)(2,1)}, bf16[400,128]{1,0:T(8,128)(2,1)S(1)}, u32[]{:S(2)}, u32[]{:S(2)}) %collective-permute-start.2) | collective-permute-done | bytes 102432 | tf_op jit(solution)/shard_map/ppermute | solution.py:44
  16.6 1.2 %collective-permute-start.6 = (bf16[256,128]{1,0:T(8,128)(2,1)S(1)}, bf16[256,128]{1,0:T(8,128)(2,1)S(1)}, u32[]{:S(2)}, u32[]{:S(2)}) collective-permute-start(bf16[256,128]{1,0:T(8,128)(2,1)S(1)} %slice.18), channel_id=1, source_target_pairs={{0,1},{1,0},{2,3},{3,2},{4,5},{5,4},{6,7},{7,6},{8,9},{9,8},{10,11... | collective-permute-start | bytes 196616 | tf_op jit(solution)/shard_map/ppermute | solution.py:44
  17.9 1.1 %attend_own.1 = (f32[4,256,128]{2,1,0:T(8,128)S(1)}, f32[4,256,128]{2,1,0:T(8,128)S(1)}, f32[4,256,128]{2,1,0:T(8,128)S(1)}) custom-call(bf16[400,128]{1,0:T(8,128)(2,1)S(1)} %copy-done.2, bf16[400,128]{1,0:T(8,128)(2,1)S(1)} %collective-permute-done.refs_1_, bf16[400,128]{1,0:T(8,128)(2,1)S(1)} %collective-permute-done.1.refs_2_, ...), custom_call_target="tpu_custom_call" | custom-call | tf_op jit(solution)/shard_map/attend_own/pallas_call | solution.py:161
  19.0 1.0 %collective-permute-done.6.refs_7_ = bf16[256,128]{1,0:T(8,128)(2,1)S(1)} collective-permute-done((bf16[256,128]{1,0:T(8,128)(2,1)S(1)}, bf16[256,128]{1,0:T(8,128)(2,1)S(1)}, u32[]{:S(2)}, u32[]{:S(2)}) %collective-permute-start.6) | collective-permute-done | bytes 65568 | tf_op jit(solution)/shard_map/ppermute | solution.py:44
  20.1 1.4 %attend_rest.1 = (bf16[128,128]{1,0:T(8,128)(2,1)S(1)}, bf16[128,128]{1,0:T(8,128)(2,1)S(1)}, bf16[128,128]{1,0:T(8,128)(2,1)S(1)}, bf16[128,128]{1,0:T(8,128)(2,1)S(1)}) custom-call(bf16[400,128]{1,0:T(8,128)(2,1)S(1)} %copy-done.2, bf16[400,128]{1,0:T(8,128)(2,1)S(1)} %collective-permute-done.refs_1_, bf16[400,128]{1,0:T(8,128)(2,1)S(1)} %collective-permute-done.1.refs_2_, ...), custom_call_target="tpu_custom_call" | custom-call | tf_op jit(solution)/shard_map/attend_rest/pallas_call | solution.py:172
  21.4 3.1 %collective-permute-start.7 = (bf16[128,128]{1,0:T(8,128)(2,1)S(1)}, bf16[128,128]{1,0:T(8,128)(2,1)S(1)}, u32[]{:S(2)}, u32[]{:S(2)}) collective-permute-start(bf16[128,128]{1,0:T(8,128)(2,1)S(1)} %get-tuple-element.24), channel_id=1, source_target_pairs={{0,2},{1,3},{2,0},{3,1},{4,6},{5,7},{6,4},{7,5},{8,10},{9,11},{10,... | collective-permute-start | bytes 98312 | tf_op jit(solution)/shard_map/ppermute | solution.py:44
  24.5 0.4 collective-permute-start.8
  25.0 1.7 %collective-permute-start.9 = (bf16[128,128]{1,0:T(8,128)(2,1)S(1)}, bf16[128,128]{1,0:T(8,128)(2,1)S(1)}, u32[]{:S(2)}, u32[]{:S(2)}) collective-permute-start(bf16[128,128]{1,0:T(8,128)(2,1)S(1)} %get-tuple-element.26), channel_id=1, source_target_pairs={{0,6},{1,7},{2,4},{3,5},{4,2},{5,3},{6,0},{7,1},{8,14},{9,15},{10,... | collective-permute-start | bytes 98312 | tf_op jit(solution)/shard_map/ppermute | solution.py:44
  26.7 4.3 %collective-permute-start.10 = (bf16[16,2,128,128]{3,2,1,0:T(8,128)(2,1)S(1)}, bf16[16,2,128,128]{3,2,1,0:T(8,128)(2,1)S(1)}, u32[]{:S(2)}, u32[]{:S(2)}) collective-permute-start(bf16[16,2,128,128]{3,2,1,0:T(8,128)(2,1)S(1)} %copy-done.1), channel_id=1, source_target_pairs={{0,8},{8,0},{16,24},{24,16},{1,9},{9,1},{17,25},{25,17},{2,10},{10... | collective-permute-start | bytes 3145736 | tf_op jit(solution)/shard_map/ppermute | solution.py:44
  31.0 4.3 %collective-permute-start.12 = (bf16[16,2,128,128]{3,2,1,0:T(8,128)(2,1)S(1)}, bf16[16,2,128,128]{3,2,1,0:T(8,128)(2,1)S(1)}, u32[]{:S(2)}, u32[]{:S(2)}) collective-permute-start(bf16[16,2,128,128]{3,2,1,0:T(8,128)(2,1)S(1)} %collective-permute-done.11.refs_10_), channel_id=1, source_target_pairs={{0,8},{8,0},{16,24},{24,16},{1,9},{9,1},{17,25},{25,17},{2,10},{10... | collective-permute-start | bytes 3145736 | tf_op jit(solution)/shard_map/ppermute | solution.py:44
  35.4 2.3 %collective-permute-done.12.refs_11_ = bf16[16,2,128,128]{3,2,1,0:T(8,128)(2,1)S(1)} collective-permute-done((bf16[16,2,128,128]{3,2,1,0:T(8,128)(2,1)S(1)}, bf16[16,2,128,128]{3,2,1,0:T(8,128)(2,1)S(1)}, u32[]{:S(2)}, u32[]{:S(2)}) %collective-permute-start.12) | collective-permute-done | bytes 1048608 | tf_op jit(solution)/shard_map/ppermute | solution.py:44
  37.7 0.6 %copy-done.6 = s32[32,2]{0,1:T(2,128)S(1)} copy-done((s32[32,2]{0,1:T(2,128)S(1)}, s32[32,2]{0,1:T(2,128)}, u32[]{:S(2)}) %copy-start.6) | copy-done | bytes 280
  38.3 6.2 %mlp.1 = (bf16[1,128,1024]{2,1,0:T(8,128)(2,1)}, bf16[1,128,1024]{2,1,0:T(8,128)(2,1)}) custom-call(s32[2,32]{1,0:T(2,128)S(1)} %bitcast.4, s32[2,32]{1,0:T(2,128)S(1)} %bitcast.5, bf16[128,128]{1,0:T(8,128)(2,1)S(1)} %get-tuple-element.23.refs_0_, bf16[128,128]{1,0:T(8,128)(2,1)S(1)} %collective-permute-done.7.refs_1_, ...), custom_call_target="tpu_custom_call" | custom-call | tf_op jit(solution)/shard_map/mlp/pallas_call | solution.py:257
  (26 shorter events, 0.1 us)
Async XLA Ops:
  4.0 27.0 %collective-permute-start.11 = (bf16[16,2,128,128]{3,2,1,0:T(8,128)(2,1)}, bf16[16,2,128,128]{3,2,1,0:T(8,128)(2,1)S(1)}, u32[]{:S(2)}, u32[]{:S(2)}) collective-permute-start(bf16[16,2,128,128]{3,2,1,0:T(8,128)(2,1)} %get-tuple-element.28.refs_8_), channel_id=1, source_target_pairs={{0,16},{8,24},{16,0},{24,8},{1,17},{9,25},{17,1},{25,9},{2,18},{10... | collective-permute-start | bytes 3145736 | tf_op jit(solution)/shard_map/ppermute | solution.py:44
  6.1 5.7 %collective-permute-start = (bf16[400,128]{1,0:T(8,128)(2,1)}, bf16[400,128]{1,0:T(8,128)(2,1)S(1)}, u32[]{:S(2)}, u32[]{:S(2)}) collective-permute-start(bf16[400,128]{1,0:T(8,128)(2,1)} %get-tuple-element.17), channel_id=1, source_target_pairs={{0,2},{1,3},{2,0},{3,1},{4,6},{5,7},{6,4},{7,5},{8,10},{9,11},{10,... | collective-permute-start | bytes 307208 | tf_op jit(solution)/shard_map/ppermute | solution.py:44
  7.4 5.2 %collective-permute-start.1 = (bf16[400,128]{1,0:T(8,128)(2,1)}, bf16[400,128]{1,0:T(8,128)(2,1)S(1)}, u32[]{:S(2)}, u32[]{:S(2)}) collective-permute-start(bf16[400,128]{1,0:T(8,128)(2,1)} %get-tuple-element.18), channel_id=1, source_target_pairs={{0,4},{1,5},{2,6},{3,7},{4,0},{5,1},{6,2},{7,3},{8,12},{9,13},{10,... | collective-permute-start | bytes 307208 | tf_op jit(solution)/shard_map/ppermute | solution.py:44
  9.8 6.9 %collective-permute-start.2 = (bf16[400,128]{1,0:T(8,128)(2,1)}, bf16[400,128]{1,0:T(8,128)(2,1)S(1)}, u32[]{:S(2)}, u32[]{:S(2)}) collective-permute-start(bf16[400,128]{1,0:T(8,128)(2,1)} %get-tuple-element.19), channel_id=1, source_target_pairs={{0,6},{1,7},{2,4},{3,5},{4,2},{5,3},{6,0},{7,1},{8,14},{9,15},{10,... | collective-permute-start | bytes 307208 | tf_op jit(solution)/shard_map/ppermute | solution.py:44
  10.6 8.4 %collective-permute-start.3 = (bf16[256,128]{1,0:T(8,128)(2,1)S(1)}, bf16[256,128]{1,0:T(8,128)(2,1)S(1)}, u32[]{:S(2)}, u32[]{:S(2)}) collective-permute-start(bf16[256,128]{1,0:T(8,128)(2,1)S(1)} %slice.12), channel_id=1, source_target_pairs={{0,1},{1,0},{2,3},{3,2},{4,5},{5,4},{6,7},{7,6},{8,9},{9,8},{10,11... | collective-permute-start | bytes 196616 | tf_op jit(solution)/shard_map/ppermute | solution.py:44
  11.8 6.0 %copy-start.2 = (bf16[400,128]{1,0:T(8,128)(2,1)S(1)}, bf16[400,128]{1,0:T(8,128)(2,1)}, u32[]{:S(2)}) copy-start(bf16[400,128]{1,0:T(8,128)(2,1)} %get-tuple-element.16.refs_0_) | copy-start | bytes 307204
  11.8 7.2 %collective-permute-start.4 = (bf16[256,128]{1,0:T(8,128)(2,1)S(1)}, bf16[256,128]{1,0:T(8,128)(2,1)S(1)}, u32[]{:S(2)}, u32[]{:S(2)}) collective-permute-start(bf16[256,128]{1,0:T(8,128)(2,1)S(1)} %slice.16), channel_id=1, source_target_pairs={{0,1},{1,0},{2,3},{3,2},{4,5},{5,4},{6,7},{7,6},{8,9},{9,8},{10,11... | collective-permute-start | bytes 196616 | tf_op jit(solution)/shard_map/ppermute | solution.py:44
  12.6 6.4 %collective-permute-start.5 = (bf16[256,128]{1,0:T(8,128)(2,1)S(1)}, bf16[256,128]{1,0:T(8,128)(2,1)S(1)}, u32[]{:S(2)}, u32[]{:S(2)}) collective-permute-start(bf16[256,128]{1,0:T(8,128)(2,1)S(1)} %slice.17), channel_id=1, source_target_pairs={{0,1},{1,0},{2,3},{3,2},{4,5},{5,4},{6,7},{7,6},{8,9},{9,8},{10,11... | collective-permute-start | bytes 196616 | tf_op jit(solution)/shard_map/ppermute | solution.py:44
  16.6 3.4 %collective-permute-start.6 = (bf16[256,128]{1,0:T(8,128)(2,1)S(1)}, bf16[256,128]{1,0:T(8,128)(2,1)S(1)}, u32[]{:S(2)}, u32[]{:S(2)}) collective-permute-start(bf16[256,128]{1,0:T(8,128)(2,1)S(1)} %slice.18), channel_id=1, source_target_pairs={{0,1},{1,0},{2,3},{3,2},{4,5},{5,4},{6,7},{7,6},{8,9},{9,8},{10,11... | collective-permute-start | bytes 196616 | tf_op jit(solution)/shard_map/ppermute | solution.py:44
  17.9 19.8 %copy-start.3 = (bf16[1,128,1024]{2,1,0:T(8,128)(2,1)S(1)}, bf16[1,128,1024]{2,1,0:T(8,128)(2,1)}, u32[]{:S(2)}) copy-start(bf16[1,128,1024]{2,1,0:T(8,128)(2,1)} %refs_5_.1) | copy-start | bytes 786436
  17.9 19.8 %copy-start.4 = (bf16[1,128,1024]{2,1,0:T(8,128)(2,1)S(1)}, bf16[1,128,1024]{2,1,0:T(8,128)(2,1)}, u32[]{:S(2)}) copy-start(bf16[1,128,1024]{2,1,0:T(8,128)(2,1)} %refs_7_.1) | copy-start | bytes 786436
  20.1 6.6 %copy-start.1 = (bf16[16,2,128,128]{3,2,1,0:T(8,128)(2,1)S(1)}, bf16[16,2,128,128]{3,2,1,0:T(8,128)(2,1)}, u32[]{:S(2)}) copy-start(bf16[16,2,128,128]{3,2,1,0:T(8,128)(2,1)} %get-tuple-element.28.refs_8_) | copy-start | bytes 3145732
  20.1 17.6 %copy-start = (bf16[512,1024]{1,0:T(8,128)(2,1)S(1)}, bf16[512,1024]{1,0:T(8,128)(2,1)}, u32[]{:S(2)}) copy-start(bf16[512,1024]{1,0:T(8,128)(2,1)} %refs_4_.1) | copy-start | bytes 3145732
  20.1 17.6 %copy-start.7 = (s32[32,2]{0,1:T(2,128)S(1)}, s32[32,2]{0,1:T(2,128)}, u32[]{:S(2)}) copy-start(s32[32,2]{0,1:T(2,128)} %param.22) | copy-start | bytes 772
  21.4 9.6 %collective-permute-start.7 = (bf16[128,128]{1,0:T(8,128)(2,1)S(1)}, bf16[128,128]{1,0:T(8,128)(2,1)S(1)}, u32[]{:S(2)}, u32[]{:S(2)}) collective-permute-start(bf16[128,128]{1,0:T(8,128)(2,1)S(1)} %get-tuple-element.24), channel_id=1, source_target_pairs={{0,2},{1,3},{2,0},{3,1},{4,6},{5,7},{6,4},{7,5},{8,10},{9,11},{10,... | collective-permute-start | bytes 98312 | tf_op jit(solution)/shard_map/ppermute | solution.py:44
  24.5 6.5 %collective-permute-start.8 = (bf16[128,128]{1,0:T(8,128)(2,1)S(1)}, bf16[128,128]{1,0:T(8,128)(2,1)S(1)}, u32[]{:S(2)}, u32[]{:S(2)}) collective-permute-start(bf16[128,128]{1,0:T(8,128)(2,1)S(1)} %get-tuple-element.25), channel_id=1, source_target_pairs={{0,4},{1,5},{2,6},{3,7},{4,0},{5,1},{6,2},{7,3},{8,12},{9,13},{10,... | collective-permute-start | bytes 98312 | tf_op jit(solution)/shard_map/ppermute | solution.py:44
  25.0 12.7 %copy-start.5 = (f32[1024]{0:T(1024)S(1)}, f32[1024]{0:T(1024)}, u32[]{:S(2)}) copy-start(f32[1024]{0:T(1024)} %param.18) | copy-start | bytes 12292
  25.0 6.1 %collective-permute-start.9 = (bf16[128,128]{1,0:T(8,128)(2,1)S(1)}, bf16[128,128]{1,0:T(8,128)(2,1)S(1)}, u32[]{:S(2)}, u32[]{:S(2)}) collective-permute-start(bf16[128,128]{1,0:T(8,128)(2,1)S(1)} %get-tuple-element.26), channel_id=1, source_target_pairs={{0,6},{1,7},{2,4},{3,5},{4,2},{5,3},{6,0},{7,1},{8,14},{9,15},{10,... | collective-permute-start | bytes 98312 | tf_op jit(solution)/shard_map/ppermute | solution.py:44
  26.7 8.7 %collective-permute-start.10 = (bf16[16,2,128,128]{3,2,1,0:T(8,128)(2,1)S(1)}, bf16[16,2,128,128]{3,2,1,0:T(8,128)(2,1)S(1)}, u32[]{:S(2)}, u32[]{:S(2)}) collective-permute-start(bf16[16,2,128,128]{3,2,1,0:T(8,128)(2,1)S(1)} %copy-done.1), channel_id=1, source_target_pairs={{0,8},{8,0},{16,24},{24,16},{1,9},{9,1},{17,25},{25,17},{2,10},{10... | collective-permute-start | bytes 3145736 | tf_op jit(solution)/shard_map/ppermute | solution.py:44
  31.0 6.6 %collective-permute-start.12 = (bf16[16,2,128,128]{3,2,1,0:T(8,128)(2,1)S(1)}, bf16[16,2,128,128]{3,2,1,0:T(8,128)(2,1)S(1)}, u32[]{:S(2)}, u32[]{:S(2)}) collective-permute-start(bf16[16,2,128,128]{3,2,1,0:T(8,128)(2,1)S(1)} %collective-permute-done.11.refs_10_), channel_id=1, source_target_pairs={{0,8},{8,0},{16,24},{24,16},{1,9},{9,1},{17,25},{25,17},{2,10},{10... | collective-permute-start | bytes 3145736 | tf_op jit(solution)/shard_map/ppermute | solution.py:44
  37.7 0.7 %copy-start.6 = (s32[32,2]{0,1:T(2,128)S(1)}, s32[32,2]{0,1:T(2,128)}, u32[]{:S(2)}) copy-start(s32[32,2]{0,1:T(2,128)} %param.20) | copy-start | bytes 772

commit v2 on v1

v2 whole, which is shorter than its diff:
```python
import functools

import jax
import jax.numpy as jnp
from jax import lax
from jax.experimental import pallas as pl
from jax.experimental.pallas import tpu as pltpu
from jax.sharding import PartitionSpec as P

HD = 64
BLK = 128
NNZ = 2
LANES = 128
QUADS = 4
HEAD_BIT = 2
NT = (((1,), (1,)), ((), ()))
ORDER = (2, 3, 1)
VMEM_LIMIT = 24 * 1024 * 1024
PACK_LIMIT = 60 * 1024 * 1024


def vmem():
    return pl.BlockSpec(memory_space=pltpu.VMEM)


def smem():
    return pl.BlockSpec(memory_space=pltpu.SMEM)


def hbm():
    return pl.BlockSpec(memory_space=pltpu.HBM)


def flips_of(seq_size):
    flips = [0]
    bit = 1
    while bit < seq_size:
        if bit not in (HEAD_BIT, 2 * HEAD_BIT):
            flips = flips + [f ^ bit for f in flips]
        bit *= 2
    return flips


def exchange(x, axis, size, flip):
    return lax.ppermute(x, axis, [(i, i ^ flip) for i in range(size)])


def after(x, *earlier):
    return lax.optimization_barrier((x, *earlier))[0]


def butterfly(x, axis, size, bits):
    held = [x]
    for bit in bits:
        held = held + [exchange(part, axis, size, bit) for part in held]
    return held


def mask_rows(seq_size):
    return 16 * ((seq_size + 15) // 16)


def pack_kernel(seq_size, q_ref, k_ref, v_ref, mask_ref, *outs):
    me = lax.axis_index("seq")
    group = lax.rem(me // HEAD_BIT, QUADS)
    rows = mask_rows(seq_size)
    row_id = lax.broadcasted_iota(jnp.int32, (rows, LANES), 0)
    for s in range(QUADS):
        cols = pl.ds(pl.multiple_of(lax.bitwise_xor(group, s) * LANES, LANES), LANES)
        for i, ref in enumerate((q_ref, k_ref, v_ref)):
            outs[s][i * BLK : (i + 1) * BLK, :] = ref[0, :, cols]
        there = lax.bitwise_xor(me, s * HEAD_BIT)
        allowed = jnp.zeros((rows, LANES), jnp.float32)
        for t, flip in enumerate(flips_of(seq_size)):
            for u in range(QUADS):
                block = lax.bitwise_xor(there, flip ^ (u * HEAD_BIT))
                bit = mask_ref[0, 0, block].astype(jnp.float32)
                allowed = jnp.where(row_id == t * QUADS + u, bit, allowed)
        outs[s][3 * BLK :, :] = allowed.astype(jnp.bfloat16)


def pack(query, key, value, attn_mask, seq_size):
    rows = 3 * BLK + mask_rows(seq_size)
    return pl.pallas_call(
        functools.partial(pack_kernel, seq_size),
        out_shape=[jax.ShapeDtypeStruct((rows, LANES), jnp.bfloat16)] * QUADS,
        in_specs=[vmem(), vmem(), vmem(), smem()],
        out_specs=[vmem()] * QUADS,
        compiler_params=pltpu.CompilerParams(vmem_limit_bytes=PACK_LIMIT),
        name="pack",
    )(query, key, value, attn_mask)


def attend_kernel(first, last, parts, *refs):
    q_refs, refs = refs[:QUADS], refs[QUADS:]
    if first:
        rows_ref, cols_ref, gain_ref = refs[:3]
        refs = refs[3:]
        refs[3][0:NNZ, :] = rows_ref[...]
        refs[3][NNZ:, :] = cols_ref[...]
        refs[4][...] = gain_ref[...]
    else:
        kv_refs, refs = refs[: QUADS * parts], refs[QUADS * parts :]
        state_refs, refs = refs[:3], refs[3:]
    scale = HD**-0.5 * 1.4426950408889634
    first_head = lax.broadcasted_iota(jnp.int32, (BLK, LANES), 1) < HD
    for s in range(QUADS):
        q = q_refs[s][0:BLK, :]
        zero = jnp.zeros_like(q)
        both = jnp.concatenate(
            [jnp.where(first_head, q, zero), jnp.where(first_head, zero, q)], axis=0
        )
        allowed = q_refs[s][3 * BLK :, :].astype(jnp.float32)
        if first:
            pairs = [(q_refs[u][BLK : 2 * BLK, :], q_refs[u][2 * BLK : 3 * BLK, :]) for u in range(QUADS)]
            base = 0
        else:
            pairs = [(ref[0:BLK, :], ref[BLK : 2 * BLK, :]) for ref in kv_refs]
            base = QUADS
        scores = []
        for row, (key, _) in enumerate(pairs):
            dots = lax.dot_general(both, key, NT, preferred_element_type=jnp.float32)
            scores.append(jnp.where(allowed[base + row : base + row + 1, :] > 0, dots, -1e30))
        top = functools.reduce(jnp.maximum, scores)
        if not first:
            top = jnp.maximum(top, state_refs[0][s])
        top = jnp.max(top, axis=1, keepdims=True)
        if first:
            total = jnp.zeros((2 * BLK, LANES), jnp.float32)
            mixed = jnp.zeros((2 * BLK, LANES), jnp.float32)
        else:
            shrink = jnp.exp2((state_refs[0][s] - top) * scale)
            total = state_refs[1][s] * shrink
            mixed = state_refs[2][s] * shrink
        for score, (_, value) in zip(scores, pairs):
            weight = jnp.exp2((score - top) * scale)
            total = total + weight
            mixed = mixed + jnp.dot(
                weight.astype(jnp.bfloat16), value, preferred_element_type=jnp.float32
            )
        if last:
            mixed = mixed / jnp.sum(total, axis=1, keepdims=True)
            refs[s][...] = jnp.where(first_head, mixed[:BLK], mixed[BLK:]).astype(jnp.bfloat16)
        else:
            refs[0][s] = jnp.broadcast_to(top, (2 * BLK, LANES))
            refs[1][s] = total
            refs[2][s] = mixed


def attend_own(packed, w1_rows, w2_cols, gain):
    return pl.pallas_call(
        functools.partial(attend_kernel, True, False, 1),
        out_shape=[jax.ShapeDtypeStruct((QUADS, 2 * BLK, LANES), jnp.float32)] * 3
        + [
            jax.ShapeDtypeStruct((2 * NNZ, w1_rows.shape[0]), jnp.int32),
            jax.ShapeDtypeStruct((1, gain.shape[0]), jnp.float32),
        ],
        in_specs=[vmem()] * (QUADS + 3),
        out_specs=[vmem()] * 5,
        compiler_params=pltpu.CompilerParams(vmem_limit_bytes=VMEM_LIMIT),
        name="attend_own",
    )(*packed, w1_rows.T, w2_cols.T, gain[None])


def attend_rest(packed, rest, state):
    return pl.pallas_call(
        functools.partial(attend_kernel, False, True, len(rest) // QUADS),
        out_shape=[jax.ShapeDtypeStruct((BLK, LANES), jnp.bfloat16)] * QUADS,
        in_specs=[vmem()] * (QUADS + len(rest) + 3),
        out_specs=[vmem()] * QUADS,
        compiler_params=pltpu.CompilerParams(vmem_limit_bytes=VMEM_LIMIT),
        name="attend_rest",
    )(*packed, *rest, *state)


def block_of(index):
    return pl.ds(pl.multiple_of(index * BLK, BLK), BLK)


def places(table_ref, owner, blocks, i):
    block = owner * blocks + i
    return (
        [block_of(table_ref[n, block]) for n in range(NNZ)],
        [block_of(table_ref[NNZ + n, block]) for n in range(NNZ)],
    )


def tall(ref, i):
    return ref[i].reshape(NNZ * BLK, BLK)


def wide(ref, i):
    return jnp.concatenate([ref[i, n] for n in range(NNZ)], axis=1)


def slope_terms(pre):
    cdf = 0.5 * (1.0 + lax.erf(pre * 0.7071067811865476))
    return pre * cdf, cdf + pre * jnp.exp(-0.5 * pre * pre) * 0.3989422804014327


def dact_of(grad_ref, second_ref, i, cols):
    grads = jnp.concatenate([grad_ref[0, :, c] for c in cols], axis=1)
    return lax.dot_general(grads, wide(second_ref, i), NT, preferred_element_type=jnp.float32)


def hidden_blocks(table_ref, owners, first_refs, second_refs, dact, normed_ref, act_ref, dpre_ref, mlp_ref, back_ref):
    blocks = first_refs[0].shape[0]
    steps = [(s, i) for s in range(len(owners)) for i in range(blocks)]
    for k, (s, i) in enumerate(steps):
        rows, cols = places(table_ref, owners[s], blocks, i)
        picked = jnp.concatenate([normed_ref[:, r] for r in rows], axis=1)
        pre = jnp.dot(picked, tall(first_refs[s], i), preferred_element_type=jnp.float32)
        act, slope = slope_terms(pre)
        act_ref[k] = act.astype(jnp.bfloat16)
        dpre_ref[k] = (dact(k, s, i, cols) * slope).astype(jnp.bfloat16)
    for k, (s, i) in enumerate(steps):
        rows, cols = places(table_ref, owners[s], blocks, i)
        forward = jnp.dot(act_ref[k], wide(second_refs[s], i), preferred_element_type=jnp.float32)
        backward = lax.dot_general(
            dpre_ref[k], tall(first_refs[s], i), NT, preferred_element_type=jnp.float32
        )
        for n in range(NNZ):
            mlp_ref[:, cols[n]] += forward[:, n * BLK : (n + 1) * BLK]
        for n in range(NNZ):
            back_ref[:, rows[n]] += backward[:, n * BLK : (n + 1) * BLK]


def near_kernel(near, table_ref, *refs):
    attn_refs, refs = refs[:QUADS], refs[QUADS:]
    proj_ref, tokens_ref, gain_ref, grad_ref = refs[:4]
    first_refs, second_refs = refs[4 : 4 + near], refs[4 + near : 4 + 3 * near]
    refs = refs[4 + 3 * near :]
    mlp_ref, back_ref, unit_ref, rstd_ref, normed_ref, far_dact_ref, act_ref, dpre_ref = refs
    group = lax.rem(lax.axis_index("seq") // HEAD_BIT, QUADS)
    hidden = tokens_ref[0].astype(jnp.float32)
    for s in range(QUADS):
        hidden = hidden + jnp.dot(
            attn_refs[s][...],
            proj_ref[block_of(lax.bitwise_xor(group, s)), :],
            preferred_element_type=jnp.float32,
        )
    mean = jnp.mean(hidden, axis=1, keepdims=True)
    centred = hidden - mean
    rstd = lax.rsqrt(jnp.mean(centred * centred, axis=1, keepdims=True) + 1e-06)
    unit = centred * rstd
    unit_ref[...] = unit
    rstd_ref[...] = jnp.broadcast_to(rstd, rstd_ref.shape)
    normed_ref[...] = (unit * gain_ref[...]).astype(jnp.bfloat16)
    mlp_ref[...] = hidden
    back_ref[...] = jnp.zeros_like(back_ref)
    me = lax.axis_index("grp")
    owners = [lax.bitwise_xor(me, s) for s in range(2 * near)]
    blocks = first_refs[0].shape[0]
    hidden_blocks(
        table_ref,
        owners[:near],
        first_refs,
        second_refs[:near],
        lambda k, s, i, cols: dact_of(grad_ref, second_refs[s], i, cols),
        normed_ref,
        act_ref,
        dpre_ref,
        mlp_ref,
        back_ref,
    )
    for s in range(near):
        for i in range(blocks):
            _, cols = places(table_ref, owners[near + s], blocks, i)
            far_dact_ref[s * blocks + i] = dact_of(grad_ref, second_refs[near + s], i, cols)


def mlp_near(table, attn, out_proj, tokens, gain, grad_out, firsts, seconds):
    near = len(firsts)
    rows, width = tokens.shape[1:]
    kept = table.shape[1] // 2
    args = (*attn, out_proj, tokens, gain, grad_out, *firsts, *seconds)
    return pl.pallas_call(
        functools.partial(near_kernel, near),
        out_shape=[
            jax.ShapeDtypeStruct((rows, width), jnp.float32),
            jax.ShapeDtypeStruct((rows, width), jnp.float32),
            jax.ShapeDtypeStruct((rows, width), jnp.float32),
            jax.ShapeDtypeStruct((rows, LANES), jnp.float32),
            jax.ShapeDtypeStruct((rows, width), jnp.bfloat16),
            jax.ShapeDtypeStruct((kept, rows, BLK), jnp.float32),
        ],
        in_specs=[smem()] + [vmem()] * len(args),
        out_specs=[vmem()] * 6,
        scratch_shapes=[pltpu.VMEM((kept, rows, BLK), jnp.bfloat16)] * 2,
        compiler_params=pltpu.CompilerParams(vmem_limit_bytes=VMEM_LIMIT),
        name="mlp_near",
    )(table, *args)


def far_kernel(near, table_ref, gain_ref, grad_ref, *refs):
    mlp_in_ref, back_in_ref, unit_ref, rstd_ref, normed_ref, dact_ref = refs[:6]
    first_refs, second_refs = refs[6 : 6 + near], refs[6 + near : 6 + 2 * near]
    out_ref, grad_out_ref, mlp_ref, back_ref, act_ref, dpre_ref = refs[6 + 2 * near :]
    mlp_ref[...] = mlp_in_ref[...]
    back_ref[...] = back_in_ref[...]
    me = lax.axis_index("grp")
    hidden_blocks(
        table_ref,
        [lax.bitwise_xor(me, near + s) for s in range(near)],
        first_refs,
        second_refs,
        lambda k, s, i, cols: dact_ref[k],
        normed_ref,
        act_ref,
        dpre_ref,
        mlp_ref,
        back_ref,
    )
    out_ref[0] = mlp_ref[...].astype(jnp.bfloat16)
    dxhat = back_ref[...] * gain_ref[...]
    unit = unit_ref[...]
    dhidden = (
        dxhat
        - jnp.mean(dxhat, axis=1, keepdims=True)
        - unit * jnp.mean(dxhat * unit, axis=1, keepdims=True)
    )
    rstd = rstd_ref[:, 0:1]
    grad_out_ref[0] = (grad_ref[0].astype(jnp.float32) + rstd * dhidden).astype(jnp.bfloat16)


def mlp_far(table, gain, grad_out, state, firsts, seconds):
    near = len(firsts)
    shape = grad_out.shape
    kept = (table.shape[1] // 2, shape[1], BLK)
    args = (gain, grad_out, *state, *firsts, *seconds)
    return pl.pallas_call(
        functools.partial(far_kernel, near),
        out_shape=[jax.ShapeDtypeStruct(shape, jnp.bfloat16)] * 2,
        in_specs=[smem()] + [vmem()] * len(args),
        out_specs=[vmem()] * 2,
        scratch_shapes=[pltpu.VMEM(shape[1:], jnp.float32)] * 2
        + [pltpu.VMEM(kept, jnp.bfloat16)] * 2,
        compiler_params=pltpu.CompilerParams(vmem_limit_bytes=VMEM_LIMIT),
        name="mlp_far",
    )(table, *args)


def body(
    seq_size,
    grp_size,
    tokens,
    queries,
    keys,
    values,
    attn_mask,
    out_proj,
    norm_gain_vector,
    w1_packed,
    w1_rows,
    w2_packed,
    w2_cols,
    grad_out,
):
    flips = [f for f in flips_of(seq_size) if f and f & (f - 1) == 0]
    across = grp_size // 2
    near_bits = []
    bit = across // 2
    while bit:
        near_bits.append(bit)
        bit //= 2

    def over_seq(x, flip):
        return exchange(x, "seq", seq_size, flip)

    def over_grp(x, flip):
        return exchange(x, "grp", grp_size, flip)

    masks = [0]
    for bit in near_bits:
        masks = masks + [m ^ bit for m in masks]
    order = sorted(range(len(masks)), key=lambda i: masks[i])

    def over_near(x):
        held = butterfly(x, "grp", grp_size, near_bits)
        return [held[i] for i in order]

    far_second = over_grp(w2_packed, across)
    far_first = over_grp(w1_packed, across)
    packed = pack(queries, keys, values, attn_mask, seq_size)
    packed = {0: packed[0], **{s: over_seq(packed[s], s * HEAD_BIT) for s in ORDER}}
    packed = [packed[s] for s in range(QUADS)]
    held = [butterfly(p[BLK : 3 * BLK], "seq", seq_size, flips) for p in packed]
    near_seconds = over_near(after(w2_packed, *packed[1:]))
    near_firsts = over_near(after(w1_packed, *packed[1:]))
    *state, table, gain = attend_own(packed, w1_rows, w2_cols, norm_gain_vector)
    rest = [held[u][t] for t in range(1, len(held[0])) for u in range(QUADS)]
    far_seconds = over_near(after(far_second, state[0]))
    attn = attend_rest(packed, rest, state)
    attn = {0: attn[0], **{s: over_seq(attn[s], s * HEAD_BIT) for s in ORDER}}
    attn = [attn[s] for s in range(QUADS)]
    far_firsts = over_near(after(far_first, *attn[1:]))
    state = mlp_near(
        table, attn, out_proj, tokens, gain, grad_out, near_firsts, near_seconds + far_seconds
    )
    output, grad_tokens = mlp_far(table, gain, grad_out, state, far_firsts, far_seconds)
    return (output, grad_tokens)


def solution(mesh):
    return jax.shard_map(
        functools.partial(body, mesh.shape["seq"], mesh.shape["grp"]),
        mesh=mesh,
        in_specs=(
            P("grp", "seq", None),
            P("grp", "seq", None),
            P("grp", "seq", None),
            P("grp", "seq", None),
            P("grp", "seq", None),
            P(),
            P(),
            P("grp", None, None, None),
            P(),
            P("grp", None, None, None),
            P(),
            P("grp", "seq", None),
        ),
        out_specs=(P("grp", "seq", None), P("grp", "seq", None)),
        check_vma=False,
    )
```

time: 45.1 us -> 41.9 us (0.929)
  waiting for transfers between devices: 6.59 us -> 4.68 us
  Pallas kernels: 12.1 us -> 11.1 us
    ppermute x13 -> x16, waiting for transfers between devices: 6.59 us -> 4.68 us  [exchange(): return lax.ppermute(x, axis, [(i, i ^ flip) for i in range(size)])]
    pallas_call x1, Pallas kernels: 3.37 us -> 1.88 us  [pack(): pl.pallas_call(functools.partial(pack_kernel, seq_size), out_shape=[jax.S...]
    pallas_call x1 -> x2, Pallas kernels: 6.23 us -> 6.76 us  [the longest x1 3.44 us: mlp_near(): pl.pallas_call(functools.partial(near_kernel, near), out_shape=[jax.Shape...]
    ppermute x13 -> x16, starting transfers between devices: 23.6 us -> 23.5 us  [exchange(): return lax.ppermute(x, axis, [(i, i ^ flip) for i in range(size)])]
  transfers between devices with their start and end apart: 13 -> 16, of which waited for: 4 -> 3; matrix products, arithmetic and copies ran while one was open for 2% -> 2% of each run, Pallas kernels for 6% -> 19%
where the time goes in v2:
time: 41.9 us; the launch traced here: 41.6 us
  starting transfers between devices  23.5 us (56%)
  Pallas kernels  11.1 us (26%)
  waiting for transfers between devices  4.68 us (11%)
  local copies, waits for them, and re-layouts  1.56 us (4%)
  between operations  0.74 us (2%)
    ppermute x16, starting transfers between devices, exchange(): return lax.ppermute(x, axis, [(i, i ^ flip) for i in range(size)])  23.5 us
    ppermute x16, waiting for transfers between devices, exchange(): return lax.ppermute(x, axis, [(i, i ^ flip) for i in range(size)])  4.68 us
    pallas_call x1, Pallas kernels, mlp_near(): pl.pallas_call(functools.partial(near_kernel, near), out_shape=[jax.Shape...  3.44 us
    pallas_call x1, Pallas kernels, mlp_far(): pl.pallas_call(functools.partial(far_kernel, near), out_shape=[jax.ShapeD...  3.33 us
    pallas_call x1, Pallas kernels, pack(): pl.pallas_call(functools.partial(pack_kernel, seq_size), out_shape=[jax.S...  1.88 us
    pallas_call x1, Pallas kernels, attend_rest(): pl.pallas_call(functools.partial(attend_kernel, False, True, len(rest) //...  1.37 us
    pallas_call x1, Pallas kernels, attend_own(): pl.pallas_call(functools.partial(attend_kernel, True, False, 1), out_shap...  1.14 us
    slice x4, local copies, waits for them, and re-layouts, body(): held = [butterfly(p[BLK:3 * BLK], 'seq', seq_size, flips) for p in packed]  0.86 us
  transfers between devices with their start and end apart: 16, of which 3 were waited for; matrix products, arithmetic and copies ran while one was open for 2% of the time, Pallas kernels for 19%

profile of v2, /device:TPU:1, one launch (start us, length us, event | category | flops | bytes accessed | tf_op | source)
XLA Modules:
  0.0 41.6 jit_solution(9203082847351412894)
XLA Ops:
  0.6 2.1 %collective-permute-start.12 = (bf16[8,2,128,128]{3,2,1,0:T(8,128)(2,1)}, bf16[8,2,128,128]{3,2,1,0:T(8,128)(2,1)S(1)}, u32[]{:S(2)}, u32[]{:S(2)}) collective-permute-start(bf16[8,2,128,128]{3,2,1,0:T(8,128)(2,1)} %refs_10_), channel_id=1, source_target_pairs={{0,16},{8,24},{16,0},{24,8},{1,17},{9,25},{17,1},{25,9},{2,18},{10... | collective-permute-start | bytes 1572872 | tf_op jit(solution)/shard_map/ppermute | solution.py:45
  2.8 1.9 %pack.1 = (bf16[400,128]{1,0:T(8,128)(2,1)}, bf16[400,128]{1,0:T(8,128)(2,1)}, bf16[400,128]{1,0:T(8,128)(2,1)}, bf16[400,128]{1,0:T(8,128)(2,1)}) custom-call(bf16[1,128,512]{2,1,0:T(8,128)(2,1)} %q_ref.1, bf16[1,128,512]{2,1,0:T(8,128)(2,1)} %k_ref.1, bf16[1,128,512]{2,1,0:T(8,128)(2,1)} %v_ref.1, s32[1,1,8]{2,1,0:T(1,128)} %mask_ref.1), custom_call_target="tpu_custom_call" | custom-call | tf_op jit(solution)/shard_map/pack/pallas_call | solution.py:84
  4.7 1.4 %collective-permute-start = (bf16[400,128]{1,0:T(8,128)(2,1)}, bf16[400,128]{1,0:T(8,128)(2,1)S(1)}, u32[]{:S(2)}, u32[]{:S(2)}) collective-permute-start(bf16[400,128]{1,0:T(8,128)(2,1)} %get-tuple-element.26), channel_id=1, source_target_pairs={{0,2},{1,3},{2,0},{3,1},{4,6},{5,7},{6,4},{7,5},{8,10},{9,11},{10,... | collective-permute-start | bytes 307208 | tf_op jit(solution)/shard_map/ppermute | solution.py:45
  6.2 2.3 %collective-permute-start.1 = (bf16[400,128]{1,0:T(8,128)(2,1)}, bf16[400,128]{1,0:T(8,128)(2,1)S(1)}, u32[]{:S(2)}, u32[]{:S(2)}) collective-permute-start(bf16[400,128]{1,0:T(8,128)(2,1)} %get-tuple-element.27), channel_id=1, source_target_pairs={{0,4},{1,5},{2,6},{3,7},{4,0},{5,1},{6,2},{7,3},{8,12},{9,13},{10,... | collective-permute-start | bytes 307208 | tf_op jit(solution)/shard_map/ppermute | solution.py:45
  8.5 0.8 %slice.12 = bf16[256,128]{1,0:T(8,128)(2,1)S(1)} slice(bf16[400,128]{1,0:T(8,128)(2,1)} %get-tuple-element.25.refs_0_), slice={[128:384], [0:128]} | slice | bytes 131072 | tf_op jit(solution)/shard_map/slice | solution.py:387
  9.3 1.2 %collective-permute-start.3 = (bf16[256,128]{1,0:T(8,128)(2,1)S(1)}, bf16[256,128]{1,0:T(8,128)(2,1)S(1)}, u32[]{:S(2)}, u32[]{:S(2)}) collective-permute-start(bf16[256,128]{1,0:T(8,128)(2,1)S(1)} %slice.12), channel_id=1, source_target_pairs={{0,1},{1,0},{2,3},{3,2},{4,5},{5,4},{6,7},{7,6},{8,9},{9,8},{10,11... | collective-permute-start | bytes 196616 | tf_op jit(solution)/shard_map/ppermute | solution.py:45
  10.5 1.1 %collective-permute-done.1.refs_2_ = bf16[400,128]{1,0:T(8,128)(2,1)S(1)} collective-permute-done((bf16[400,128]{1,0:T(8,128)(2,1)}, bf16[400,128]{1,0:T(8,128)(2,1)S(1)}, u32[]{:S(2)}, u32[]{:S(2)}) %collective-permute-start.1) | collective-permute-done | bytes 102432 | tf_op jit(solution)/shard_map/ppermute | solution.py:45
  11.6 1.2 %collective-permute-start.4 = (bf16[256,128]{1,0:T(8,128)(2,1)S(1)}, bf16[256,128]{1,0:T(8,128)(2,1)S(1)}, u32[]{:S(2)}, u32[]{:S(2)}) collective-permute-start(bf16[256,128]{1,0:T(8,128)(2,1)S(1)} %slice.16), channel_id=1, source_target_pairs={{0,1},{1,0},{2,3},{3,2},{4,5},{5,4},{6,7},{7,6},{8,9},{9,8},{10,11... | collective-permute-start | bytes 196616 | tf_op jit(solution)/shard_map/ppermute | solution.py:45
  12.8 2.3 %collective-permute-done.2.refs_3_ = bf16[400,128]{1,0:T(8,128)(2,1)S(1)} collective-permute-done((bf16[400,128]{1,0:T(8,128)(2,1)}, bf16[400,128]{1,0:T(8,128)(2,1)S(1)}, u32[]{:S(2)}, u32[]{:S(2)}) %collective-permute-start.2) | collective-permute-done | bytes 102432 | tf_op jit(solution)/shard_map/ppermute | solution.py:45
  15.1 1.2 %collective-permute-start.5 = (bf16[256,128]{1,0:T(8,128)(2,1)S(1)}, bf16[256,128]{1,0:T(8,128)(2,1)S(1)}, u32[]{:S(2)}, u32[]{:S(2)}) collective-permute-start(bf16[256,128]{1,0:T(8,128)(2,1)S(1)} %slice.17), channel_id=1, source_target_pairs={{0,1},{1,0},{2,3},{3,2},{4,5},{5,4},{6,7},{7,6},{8,9},{9,8},{10,11... | collective-permute-start | bytes 196616 | tf_op jit(solution)/shard_map/ppermute | solution.py:45
  16.3 0.3 collective-permute-start.6
  16.7 0.3 copy-done.8
  17.0 0.3 copy-done.7
  17.3 1.1 %attend_own.1 = (f32[4,256,128]{2,1,0:T(8,128)S(1)}, f32[4,256,128]{2,1,0:T(8,128)S(1)}, f32[4,256,128]{2,1,0:T(8,128)S(1)}, s32[4,32]{1,0:T(4,128)S(1)}, f32[1,1024]{1,0:T(1,128)S(1)}) custom-call(bf16[400,128]{1,0:T(8,128)(2,1)S(1)} %copy-done.2, bf16[400,128]{1,0:T(8,128)(2,1)S(1)} %collective-permute-done.refs_1_, ...), custom_call_target="tpu_custom_call" | custom-call | tf_op jit(solution)/shard_map/attend_own/pallas_call | solution.py:151
  18.5 1.3 %collective-permute-done.6.refs_7_ = bf16[256,128]{1,0:T(8,128)(2,1)S(1)} collective-permute-done((bf16[256,128]{1,0:T(8,128)(2,1)S(1)}, bf16[256,128]{1,0:T(8,128)(2,1)S(1)}, u32[]{:S(2)}, u32[]{:S(2)}) %collective-permute-start.6) | collective-permute-done | bytes 65568 | tf_op jit(solution)/shard_map/ppermute | solution.py:45
  19.8 1.4 %attend_rest.1 = (bf16[128,128]{1,0:T(8,128)(2,1)S(1)}, bf16[128,128]{1,0:T(8,128)(2,1)S(1)}, bf16[128,128]{1,0:T(8,128)(2,1)S(1)}, bf16[128,128]{1,0:T(8,128)(2,1)S(1)}) custom-call(bf16[400,128]{1,0:T(8,128)(2,1)S(1)} %copy-done.2, bf16[400,128]{1,0:T(8,128)(2,1)S(1)} %collective-permute-done.refs_1_, bf16[400,128]{1,0:T(8,128)(2,1)S(1)} %collective-permute-done.1.refs_2_, ...), custom_call_target="tpu_custom_call" | custom-call | tf_op jit(solution)/shard_map/attend_rest/pallas_call | solution.py:166
  21.2 3.0 %collective-permute-start.7 = (bf16[128,128]{1,0:T(8,128)(2,1)S(1)}, bf16[128,128]{1,0:T(8,128)(2,1)S(1)}, u32[]{:S(2)}, u32[]{:S(2)}) collective-permute-start(bf16[128,128]{1,0:T(8,128)(2,1)S(1)} %get-tuple-element.35), channel_id=1, source_target_pairs={{0,2},{1,3},{2,0},{3,1},{4,6},{5,7},{6,4},{7,5},{8,10},{9,11},{10,... | collective-permute-start | bytes 98312 | tf_op jit(solution)/shard_map/ppermute | solution.py:45
  24.2 0.5 %collective-permute-start.8 = (bf16[128,128]{1,0:T(8,128)(2,1)S(1)}, bf16[128,128]{1,0:T(8,128)(2,1)S(1)}, u32[]{:S(2)}, u32[]{:S(2)}) collective-permute-start(bf16[128,128]{1,0:T(8,128)(2,1)S(1)} %get-tuple-element.36), channel_id=1, source_target_pairs={{0,4},{1,5},{2,6},{3,7},{4,0},{5,1},{6,2},{7,3},{8,12},{9,13},{10,... | collective-permute-start | bytes 98312 | tf_op jit(solution)/shard_map/ppermute | solution.py:45
  24.8 1.6 %collective-permute-start.9 = (bf16[128,128]{1,0:T(8,128)(2,1)S(1)}, bf16[128,128]{1,0:T(8,128)(2,1)S(1)}, u32[]{:S(2)}, u32[]{:S(2)}) collective-permute-start(bf16[128,128]{1,0:T(8,128)(2,1)S(1)} %get-tuple-element.37), channel_id=1, source_target_pairs={{0,6},{1,7},{2,4},{3,5},{4,2},{5,3},{6,0},{7,1},{8,14},{9,15},{10,... | collective-permute-start | bytes 98312 | tf_op jit(solution)/shard_map/ppermute | solution.py:45
  26.4 4.0 %collective-permute-start.10 = (bf16[8,2,128,128]{3,2,1,0:T(8,128)(2,1)S(1)}, bf16[8,2,128,128]{3,2,1,0:T(8,128)(2,1)S(1)}, u32[]{:S(2)}, u32[]{:S(2)}) collective-permute-start(bf16[8,2,128,128]{3,2,1,0:T(8,128)(2,1)S(1)} %copy-done.3), channel_id=1, source_target_pairs={{0,8},{8,0},{16,24},{24,16},{1,9},{9,1},{17,25},{25,17},{2,10},{10... | collective-permute-start | bytes 1572872 | tf_op jit(solution)/shard_map/ppermute | solution.py:45
  30.5 1.3 %collective-permute-start.13 = (bf16[8,2,128,128]{3,2,1,0:T(8,128)(2,1)S(1)}, bf16[8,2,128,128]{3,2,1,0:T(8,128)(2,1)S(1)}, u32[]{:S(2)}, u32[]{:S(2)}) collective-permute-start(bf16[8,2,128,128]{3,2,1,0:T(8,128)(2,1)S(1)} %collective-permute-done.12.refs_12_.refs_8_), channel_id=1, source_target_pairs={{0,8},{8,0},{16,24},{24,16},{1,9},{9,1},{17,25},{25,17},{2,10},{10... | collective-permute-start | bytes 1572872 | tf_op jit(solution)/shard_map/ppermute | solution.py:45
  31.8 3.0 %collective-permute-start.15 = (bf16[8,2,128,128]{3,2,1,0:T(8,128)(2,1)S(1)}, bf16[8,2,128,128]{3,2,1,0:T(8,128)(2,1)S(1)}, u32[]{:S(2)}, u32[]{:S(2)}) collective-permute-start(bf16[8,2,128,128]{3,2,1,0:T(8,128)(2,1)S(1)} %collective-permute-done.14.refs_6_), channel_id=1, source_target_pairs={{0,8},{8,0},{16,24},{24,16},{1,9},{9,1},{17,25},{25,17},{2,10},{10... | collective-permute-start | bytes 1572872 | tf_op jit(solution)/shard_map/ppermute | solution.py:45
  34.8 3.4 %mlp_near.1 = (f32[128,1024]{1,0:T(8,128)S(1)}, f32[128,1024]{1,0:T(8,128)S(1)}, f32[128,1024]{1,0:T(8,128)S(1)}, f32[128,128]{1,0:T(8,128)S(1)}, bf16[128,1024]...) custom-call(s32[4,32]{1,0:T(4,128)S(1)} %get-tuple-element.29.table_ref, bf16[128,128]{1,0:T(8,128)(2,1)S(1)} %get-tuple-element.34.refs_0_, ...), custom_call_target="tpu_custom_call" | custom-call | tf_op jit(solution)/shard_map/mlp_near/pallas_call | solution.py:277
  38.3 3.3 %mlp_far.1 = (bf16[1,128,1024]{2,1,0:T(8,128)(2,1)}, bf16[1,128,1024]{2,1,0:T(8,128)(2,1)}) custom-call(s32[4,32]{1,0:T(4,128)S(1)} %get-tuple-element.29.table_ref, f32[1,1024]{1,0:T(1,128)S(1)} %get-tuple-element.30.refs_6_.gain_ref, bf16[1,128,1024]{2,1,0:T(8,128)(2,1)S(1)} %copy-done.1, f32[128,1024]{1,0:T(8,128)S(1)} %get-tuple-element.41.refs_0_, ...), custom_call_target="tpu_custom_call" | custom-call | tf_op jit(solution)/shard_map/mlp_far/pallas_call | solution.py:331
  (35 shorter events, 0.3 us)
Async XLA Ops:
  0.6 25.8 %collective-permute-start.12 = (bf16[8,2,128,128]{3,2,1,0:T(8,128)(2,1)}, bf16[8,2,128,128]{3,2,1,0:T(8,128)(2,1)S(1)}, u32[]{:S(2)}, u32[]{:S(2)}) collective-permute-start(bf16[8,2,128,128]{3,2,1,0:T(8,128)(2,1)} %refs_10_), channel_id=1, source_target_pairs={{0,16},{8,24},{16,0},{24,8},{1,17},{9,25},{17,1},{25,9},{2,18},{10... | collective-permute-start | bytes 1572872 | tf_op jit(solution)/shard_map/ppermute | solution.py:45
  2.8 29.1 %collective-permute-start.14 = (bf16[8,2,128,128]{3,2,1,0:T(8,128)(2,1)}, bf16[8,2,128,128]{3,2,1,0:T(8,128)(2,1)S(1)}, u32[]{:S(2)}, u32[]{:S(2)}) collective-permute-start(bf16[8,2,128,128]{3,2,1,0:T(8,128)(2,1)} %refs_8_), channel_id=1, source_target_pairs={{0,16},{8,24},{16,0},{24,8},{1,17},{9,25},{17,1},{25,9},{2,18},{10... | collective-permute-start | bytes 1572872 | tf_op jit(solution)/shard_map/ppermute | solution.py:45
  4.7 4.6 %collective-permute-start = (bf16[400,128]{1,0:T(8,128)(2,1)}, bf16[400,128]{1,0:T(8,128)(2,1)S(1)}, u32[]{:S(2)}, u32[]{:S(2)}) collective-permute-start(bf16[400,128]{1,0:T(8,128)(2,1)} %get-tuple-element.26), channel_id=1, source_target_pairs={{0,2},{1,3},{2,0},{3,1},{4,6},{5,7},{6,4},{7,5},{8,10},{9,11},{10,... | collective-permute-start | bytes 307208 | tf_op jit(solution)/shard_map/ppermute | solution.py:45
  6.2 5.5 %collective-permute-start.1 = (bf16[400,128]{1,0:T(8,128)(2,1)}, bf16[400,128]{1,0:T(8,128)(2,1)S(1)}, u32[]{:S(2)}, u32[]{:S(2)}) collective-permute-start(bf16[400,128]{1,0:T(8,128)(2,1)} %get-tuple-element.27), channel_id=1, source_target_pairs={{0,4},{1,5},{2,6},{3,7},{4,0},{5,1},{6,2},{7,3},{8,12},{9,13},{10,... | collective-permute-start | bytes 307208 | tf_op jit(solution)/shard_map/ppermute | solution.py:45
  8.5 6.6 %collective-permute-start.2 = (bf16[400,128]{1,0:T(8,128)(2,1)}, bf16[400,128]{1,0:T(8,128)(2,1)S(1)}, u32[]{:S(2)}, u32[]{:S(2)}) collective-permute-start(bf16[400,128]{1,0:T(8,128)(2,1)} %get-tuple-element.28), channel_id=1, source_target_pairs={{0,6},{1,7},{2,4},{3,5},{4,2},{5,3},{6,0},{7,1},{8,14},{9,15},{10,... | collective-permute-start | bytes 307208 | tf_op jit(solution)/shard_map/ppermute | solution.py:45
  9.3 7.0 %collective-permute-start.3 = (bf16[256,128]{1,0:T(8,128)(2,1)S(1)}, bf16[256,128]{1,0:T(8,128)(2,1)S(1)}, u32[]{:S(2)}, u32[]{:S(2)}) collective-permute-start(bf16[256,128]{1,0:T(8,128)(2,1)S(1)} %slice.12), channel_id=1, source_target_pairs={{0,1},{1,0},{2,3},{3,2},{4,5},{5,4},{6,7},{7,6},{8,9},{9,8},{10,11... | collective-permute-start | bytes 196616 | tf_op jit(solution)/shard_map/ppermute | solution.py:45
  10.5 6.1 %copy-start.2 = (bf16[400,128]{1,0:T(8,128)(2,1)S(1)}, bf16[400,128]{1,0:T(8,128)(2,1)}, u32[]{:S(2)}) copy-start(bf16[400,128]{1,0:T(8,128)(2,1)} %get-tuple-element.25.refs_0_) | copy-start | bytes 307204
  11.6 6.9 %collective-permute-start.4 = (bf16[256,128]{1,0:T(8,128)(2,1)S(1)}, bf16[256,128]{1,0:T(8,128)(2,1)S(1)}, u32[]{:S(2)}, u32[]{:S(2)}) collective-permute-start(bf16[256,128]{1,0:T(8,128)(2,1)S(1)} %slice.16), channel_id=1, source_target_pairs={{0,1},{1,0},{2,3},{3,2},{4,5},{5,4},{6,7},{7,6},{8,9},{9,8},{10,11... | collective-permute-start | bytes 196616 | tf_op jit(solution)/shard_map/ppermute | solution.py:45
  15.1 3.4 %collective-permute-start.5 = (bf16[256,128]{1,0:T(8,128)(2,1)S(1)}, bf16[256,128]{1,0:T(8,128)(2,1)S(1)}, u32[]{:S(2)}, u32[]{:S(2)}) collective-permute-start(bf16[256,128]{1,0:T(8,128)(2,1)S(1)} %slice.17), channel_id=1, source_target_pairs={{0,1},{1,0},{2,3},{3,2},{4,5},{5,4},{6,7},{7,6},{8,9},{9,8},{10,11... | collective-permute-start | bytes 196616 | tf_op jit(solution)/shard_map/ppermute | solution.py:45
  16.3 0.7 %copy-start.8 = (s32[32,2]{0,1:T(2,128)S(1)}, s32[32,2]{0,1:T(2,128)}, u32[]{:S(2)}) copy-start(s32[32,2]{0,1:T(2,128)} %param.22) | copy-start | bytes 772
  16.3 0.7 %copy-start.6 = (f32[1024]{0:T(1024)S(1)}, f32[1024]{0:T(1024)}, u32[]{:S(2)}) copy-start(f32[1024]{0:T(1024)} %param.18) | copy-start | bytes 12292
  16.3 3.5 %collective-permute-start.6 = (bf16[256,128]{1,0:T(8,128)(2,1)S(1)}, bf16[256,128]{1,0:T(8,128)(2,1)S(1)}, u32[]{:S(2)}, u32[]{:S(2)}) collective-permute-start(bf16[256,128]{1,0:T(8,128)(2,1)S(1)} %slice.18), channel_id=1, source_target_pairs={{0,1},{1,0},{2,3},{3,2},{4,5},{5,4},{6,7},{7,6},{8,9},{9,8},{10,11... | collective-permute-start | bytes 196616 | tf_op jit(solution)/shard_map/ppermute | solution.py:45
  17.3 13.1 %copy-start.4 = (bf16[8,2,128,128]{3,2,1,0:T(8,128)(2,1)S(1)}, bf16[8,2,128,128]{3,2,1,0:T(8,128)(2,1)}, u32[]{:S(2)}) copy-start(bf16[8,2,128,128]{3,2,1,0:T(8,128)(2,1)} %refs_10_) | copy-start | bytes 1572868
  19.8 6.6 %copy-start.3 = (bf16[8,2,128,128]{3,2,1,0:T(8,128)(2,1)S(1)}, bf16[8,2,128,128]{3,2,1,0:T(8,128)(2,1)}, u32[]{:S(2)}) copy-start(bf16[8,2,128,128]{3,2,1,0:T(8,128)(2,1)} %refs_8_) | copy-start | bytes 1572868
  19.8 15.0 %copy-start = (bf16[512,1024]{1,0:T(8,128)(2,1)S(1)}, bf16[512,1024]{1,0:T(8,128)(2,1)}, u32[]{:S(2)}) copy-start(bf16[512,1024]{1,0:T(8,128)(2,1)} %refs_4_.1) | copy-start | bytes 3145732
  19.8 15.0 %copy-start.1 = (bf16[1,128,1024]{2,1,0:T(8,128)(2,1)S(1)}, bf16[1,128,1024]{2,1,0:T(8,128)(2,1)}, u32[]{:S(2)}) copy-start(bf16[1,128,1024]{2,1,0:T(8,128)(2,1)} %grad_ref.1) | copy-start | bytes 786436
  19.8 15.0 %copy-start.5 = (bf16[1,128,1024]{2,1,0:T(8,128)(2,1)S(1)}, bf16[1,128,1024]{2,1,0:T(8,128)(2,1)}, u32[]{:S(2)}) copy-start(bf16[1,128,1024]{2,1,0:T(8,128)(2,1)} %refs_5_.1) | copy-start | bytes 786436
  21.2 9.2 %collective-permute-start.7 = (bf16[128,128]{1,0:T(8,128)(2,1)S(1)}, bf16[128,128]{1,0:T(8,128)(2,1)S(1)}, u32[]{:S(2)}, u32[]{:S(2)}) collective-permute-start(bf16[128,128]{1,0:T(8,128)(2,1)S(1)} %get-tuple-element.35), channel_id=1, source_target_pairs={{0,2},{1,3},{2,0},{3,1},{4,6},{5,7},{6,4},{7,5},{8,10},{9,11},{10,... | collective-permute-start | bytes 98312 | tf_op jit(solution)/shard_map/ppermute | solution.py:45
  24.2 6.3 %collective-permute-start.8 = (bf16[128,128]{1,0:T(8,128)(2,1)S(1)}, bf16[128,128]{1,0:T(8,128)(2,1)S(1)}, u32[]{:S(2)}, u32[]{:S(2)}) collective-permute-start(bf16[128,128]{1,0:T(8,128)(2,1)S(1)} %get-tuple-element.36), channel_id=1, source_target_pairs={{0,4},{1,5},{2,6},{3,7},{4,0},{5,1},{6,2},{7,3},{8,12},{9,13},{10,... | collective-permute-start | bytes 98312 | tf_op jit(solution)/shard_map/ppermute | solution.py:45
  24.8 7.1 %collective-permute-start.9 = (bf16[128,128]{1,0:T(8,128)(2,1)S(1)}, bf16[128,128]{1,0:T(8,128)(2,1)S(1)}, u32[]{:S(2)}, u32[]{:S(2)}) collective-permute-start(bf16[128,128]{1,0:T(8,128)(2,1)S(1)} %get-tuple-element.37), channel_id=1, source_target_pairs={{0,6},{1,7},{2,4},{3,5},{4,2},{5,3},{6,0},{7,1},{8,14},{9,15},{10,... | collective-permute-start | bytes 98312 | tf_op jit(solution)/shard_map/ppermute | solution.py:45
  26.4 8.4 %collective-permute-start.10 = (bf16[8,2,128,128]{3,2,1,0:T(8,128)(2,1)S(1)}, bf16[8,2,128,128]{3,2,1,0:T(8,128)(2,1)S(1)}, u32[]{:S(2)}, u32[]{:S(2)}) collective-permute-start(bf16[8,2,128,128]{3,2,1,0:T(8,128)(2,1)S(1)} %copy-done.3), channel_id=1, source_target_pairs={{0,8},{8,0},{16,24},{24,16},{1,9},{9,1},{17,25},{25,17},{2,10},{10... | collective-permute-start | bytes 1572872 | tf_op jit(solution)/shard_map/ppermute | solution.py:45
  30.4 4.4 %collective-permute-start.11 = (bf16[8,2,128,128]{3,2,1,0:T(8,128)(2,1)S(1)}, bf16[8,2,128,128]{3,2,1,0:T(8,128)(2,1)S(1)}, u32[]{:S(2)}, u32[]{:S(2)}) collective-permute-start(bf16[8,2,128,128]{3,2,1,0:T(8,128)(2,1)S(1)} %copy-done.4), channel_id=1, source_target_pairs={{0,8},{8,0},{16,24},{24,16},{1,9},{9,1},{17,25},{25,17},{2,10},{10... | collective-permute-start | bytes 1572872 | tf_op jit(solution)/shard_map/ppermute | solution.py:45
  30.5 4.3 %collective-permute-start.13 = (bf16[8,2,128,128]{3,2,1,0:T(8,128)(2,1)S(1)}, bf16[8,2,128,128]{3,2,1,0:T(8,128)(2,1)S(1)}, u32[]{:S(2)}, u32[]{:S(2)}) collective-permute-start(bf16[8,2,128,128]{3,2,1,0:T(8,128)(2,1)S(1)} %collective-permute-done.12.refs_12_.refs_8_), channel_id=1, source_target_pairs={{0,8},{8,0},{16,24},{24,16},{1,9},{9,1},{17,25},{25,17},{2,10},{10... | collective-permute-start | bytes 1572872 | tf_op jit(solution)/shard_map/ppermute | solution.py:45
  31.8 6.5 %collective-permute-start.15 = (bf16[8,2,128,128]{3,2,1,0:T(8,128)(2,1)S(1)}, bf16[8,2,128,128]{3,2,1,0:T(8,128)(2,1)S(1)}, u32[]{:S(2)}, u32[]{:S(2)}) collective-permute-start(bf16[8,2,128,128]{3,2,1,0:T(8,128)(2,1)S(1)} %collective-permute-done.14.refs_6_), channel_id=1, source_target_pairs={{0,8},{8,0},{16,24},{24,16},{1,9},{9,1},{17,25},{25,17},{2,10},{10... | collective-permute-start | bytes 1572872 | tf_op jit(solution)/shard_map/ppermute | solution.py:45
  (1 other events, 0.7 us)

commit v3 on v2

--- a/solution.py
+++ b/solution.py
@@ -225,7 +225,10 @@
             back_ref[:, rows[n]] += backward[:, n * BLK : (n + 1) * BLK]
 
 
-def near_kernel(near, table_ref, *refs):
+def near_kernel(near, table_in_ref, *refs):
+    refs, (table_ref, table_sem) = refs[:-2], refs[-2:]
+    table_copy = pltpu.make_async_copy(table_in_ref, table_ref, table_sem)
+    table_copy.start()
     attn_refs, refs = refs[:QUADS], refs[QUADS:]
     proj_ref, tokens_ref, gain_ref, grad_ref = refs[:4]
     first_refs, second_refs = refs[4 : 4 + near], refs[4 + near : 4 + 3 * near]
@@ -248,6 +251,7 @@
     normed_ref[...] = (unit * gain_ref[...]).astype(jnp.bfloat16)
     mlp_ref[...] = hidden
     back_ref[...] = jnp.zeros_like(back_ref)
+    table_copy.wait()
     me = lax.axis_index("grp")
     owners = [lax.bitwise_xor(me, s) for s in range(2 * near)]
     blocks = first_refs[0].shape[0]
@@ -284,20 +288,25 @@
             jax.ShapeDtypeStruct((rows, width), jnp.bfloat16),
             jax.ShapeDtypeStruct((kept, rows, BLK), jnp.float32),
         ],
-        in_specs=[smem()] + [vmem()] * len(args),
+        in_specs=[vmem()] * (1 + len(args)),
         out_specs=[vmem()] * 6,
-        scratch_shapes=[pltpu.VMEM((kept, rows, BLK), jnp.bfloat16)] * 2,
+        scratch_shapes=[pltpu.VMEM((kept, rows, BLK), jnp.bfloat16)] * 2
+        + [pltpu.SMEM(table.shape, jnp.int32), pltpu.SemaphoreType.DMA],
         compiler_params=pltpu.CompilerParams(vmem_limit_bytes=VMEM_LIMIT),
         name="mlp_near",
     )(table, *args)
 
 
-def far_kernel(near, table_ref, gain_ref, grad_ref, *refs):
+def far_kernel(near, table_in_ref, gain_ref, grad_ref, *refs):
+    refs, (table_ref, table_sem) = refs[:-2], refs[-2:]
+    table_copy = pltpu.make_async_copy(table_in_ref, table_ref, table_sem)
+    table_copy.start()
     mlp_in_ref, back_in_ref, unit_ref, rstd_ref, normed_ref, dact_ref = refs[:6]
     first_refs, second_refs = refs[6 : 6 + near], refs[6 + near : 6 + 2 * near]
     out_ref, grad_out_ref, mlp_ref, back_ref, act_ref, dpre_ref = refs[6 + 2 * near :]
     mlp_ref[...] = mlp_in_ref[...]
     back_ref[...] = back_in_ref[...]
+    table_copy.wait()
     me = lax.axis_index("grp")
     hidden_blocks(
         table_ref,
@@ -331,10 +340,11 @@
     return pl.pallas_call(
         functools.partial(far_kernel, near),
         out_shape=[jax.ShapeDtypeStruct(shape, jnp.bfloat16)] * 2,
-        in_specs=[smem()] + [vmem()] * len(args),
+        in_specs=[vmem()] * (1 + len(args)),
         out_specs=[vmem()] * 2,
         scratch_shapes=[pltpu.VMEM(shape[1:], jnp.float32)] * 2
-        + [pltpu.VMEM(kept, jnp.bfloat16)] * 2,
+        + [pltpu.VMEM(kept, jnp.bfloat16)] * 2
+        + [pltpu.SMEM(table.shape, jnp.int32), pltpu.SemaphoreType.DMA],
         compiler_params=pltpu.CompilerParams(vmem_limit_bytes=VMEM_LIMIT),
         name="mlp_far",
     )(table, *args)

time: 41.9 us -> 41.2 us (0.983)
  Pallas kernels: 11.1 us -> 10.4 us
    pallas_call x1, Pallas kernels: 3.44 us -> 2.73 us  [mlp_near(): pl.pallas_call(functools.partial(near_kernel, near), out_shape=[jax.Shape...]
  transfers between devices with their start and end apart: 16 -> 16, of which waited for: 3 -> 3; matrix products, arithmetic and copies ran while one was open for 2% -> 2% of each run, Pallas kernels for 19% -> 17%
where the time goes in v3:
time: 41.2 us; the launch traced here: 40.9 us
  starting transfers between devices  23.5 us (57%)
  Pallas kernels  10.4 us (25%)
  waiting for transfers between devices  4.68 us (11%)
  local copies, waits for them, and re-layouts  1.56 us (4%)
  between operations  0.74 us (2%)
    ppermute x16, starting transfers between devices, exchange(): return lax.ppermute(x, axis, [(i, i ^ flip) for i in range(size)])  23.5 us
    ppermute x16, waiting for transfers between devices, exchange(): return lax.ppermute(x, axis, [(i, i ^ flip) for i in range(size)])  4.68 us
    pallas_call x1, Pallas kernels, mlp_far(): pl.pallas_call(functools.partial(far_kernel, near), out_shape=[jax.ShapeD...  3.32 us
    pallas_call x1, Pallas kernels, mlp_near(): pl.pallas_call(functools.partial(near_kernel, near), out_shape=[jax.Shape...  2.73 us
    pallas_call x1, Pallas kernels, pack(): pl.pallas_call(functools.partial(pack_kernel, seq_size), out_shape=[jax.S...  1.88 us
    pallas_call x1, Pallas kernels, attend_rest(): pl.pallas_call(functools.partial(attend_kernel, False, True, len(rest) //...  1.37 us
    pallas_call x1, Pallas kernels, attend_own(): pl.pallas_call(functools.partial(attend_kernel, True, False, 1), out_shap...  1.14 us
    slice x4, local copies, waits for them, and re-layouts, body(): held = [butterfly(p[BLK:3 * BLK], 'seq', seq_size, flips) for p in packed]  0.86 us
  transfers between devices with their start and end apart: 16, of which 3 were waited for; matrix products, arithmetic and copies ran while one was open for 2% of the time, Pallas kernels for 17%

profile of v3, /device:TPU:1, one launch (start us, length us, event | category | flops | bytes accessed | tf_op | source)
XLA Modules:
  0.0 40.9 jit_solution(11512714149407465809)
XLA Ops:
  0.6 2.1 %collective-permute-start.12 = (bf16[8,2,128,128]{3,2,1,0:T(8,128)(2,1)}, bf16[8,2,128,128]{3,2,1,0:T(8,128)(2,1)S(1)}, u32[]{:S(2)}, u32[]{:S(2)}) collective-permute-start(bf16[8,2,128,128]{3,2,1,0:T(8,128)(2,1)} %refs_10_), channel_id=1, source_target_pairs={{0,16},{8,24},{16,0},{24,8},{1,17},{9,25},{17,1},{25,9},{2,18},{10... | collective-permute-start | bytes 1572872 | tf_op jit(solution)/shard_map/ppermute | solution.py:45
  2.8 1.9 %pack.1 = (bf16[400,128]{1,0:T(8,128)(2,1)}, bf16[400,128]{1,0:T(8,128)(2,1)}, bf16[400,128]{1,0:T(8,128)(2,1)}, bf16[400,128]{1,0:T(8,128)(2,1)}) custom-call(bf16[1,128,512]{2,1,0:T(8,128)(2,1)} %q_ref.1, bf16[1,128,512]{2,1,0:T(8,128)(2,1)} %k_ref.1, bf16[1,128,512]{2,1,0:T(8,128)(2,1)} %v_ref.1, s32[1,1,8]{2,1,0:T(1,128)} %mask_ref.1), custom_call_target="tpu_custom_call" | custom-call | tf_op jit(solution)/shard_map/pack/pallas_call | solution.py:84
  4.7 1.4 %collective-permute-start = (bf16[400,128]{1,0:T(8,128)(2,1)}, bf16[400,128]{1,0:T(8,128)(2,1)S(1)}, u32[]{:S(2)}, u32[]{:S(2)}) collective-permute-start(bf16[400,128]{1,0:T(8,128)(2,1)} %get-tuple-element.26), channel_id=1, source_target_pairs={{0,2},{1,3},{2,0},{3,1},{4,6},{5,7},{6,4},{7,5},{8,10},{9,11},{10,... | collective-permute-start | bytes 307208 | tf_op jit(solution)/shard_map/ppermute | solution.py:45
  6.2 2.3 %collective-permute-start.1 = (bf16[400,128]{1,0:T(8,128)(2,1)}, bf16[400,128]{1,0:T(8,128)(2,1)S(1)}, u32[]{:S(2)}, u32[]{:S(2)}) collective-permute-start(bf16[400,128]{1,0:T(8,128)(2,1)} %get-tuple-element.27), channel_id=1, source_target_pairs={{0,4},{1,5},{2,6},{3,7},{4,0},{5,1},{6,2},{7,3},{8,12},{9,13},{10,... | collective-permute-start | bytes 307208 | tf_op jit(solution)/shard_map/ppermute | solution.py:45
  8.5 0.8 %slice.12 = bf16[256,128]{1,0:T(8,128)(2,1)S(1)} slice(bf16[400,128]{1,0:T(8,128)(2,1)} %get-tuple-element.25.refs_0_), slice={[128:384], [0:128]} | slice | bytes 131072 | tf_op jit(solution)/shard_map/slice | solution.py:397
  9.3 1.2 %collective-permute-start.3 = (bf16[256,128]{1,0:T(8,128)(2,1)S(1)}, bf16[256,128]{1,0:T(8,128)(2,1)S(1)}, u32[]{:S(2)}, u32[]{:S(2)}) collective-permute-start(bf16[256,128]{1,0:T(8,128)(2,1)S(1)} %slice.12), channel_id=1, source_target_pairs={{0,1},{1,0},{2,3},{3,2},{4,5},{5,4},{6,7},{7,6},{8,9},{9,8},{10,11... | collective-permute-start | bytes 196616 | tf_op jit(solution)/shard_map/ppermute | solution.py:45
  10.5 1.1 %collective-permute-done.1.refs_2_ = bf16[400,128]{1,0:T(8,128)(2,1)S(1)} collective-permute-done((bf16[400,128]{1,0:T(8,128)(2,1)}, bf16[400,128]{1,0:T(8,128)(2,1)S(1)}, u32[]{:S(2)}, u32[]{:S(2)}) %collective-permute-start.1) | collective-permute-done | bytes 102432 | tf_op jit(solution)/shard_map/ppermute | solution.py:45
  11.6 1.2 %collective-permute-start.4 = (bf16[256,128]{1,0:T(8,128)(2,1)S(1)}, bf16[256,128]{1,0:T(8,128)(2,1)S(1)}, u32[]{:S(2)}, u32[]{:S(2)}) collective-permute-start(bf16[256,128]{1,0:T(8,128)(2,1)S(1)} %slice.16), channel_id=1, source_target_pairs={{0,1},{1,0},{2,3},{3,2},{4,5},{5,4},{6,7},{7,6},{8,9},{9,8},{10,11... | collective-permute-start | bytes 196616 | tf_op jit(solution)/shard_map/ppermute | solution.py:45
  12.8 2.3 %collective-permute-done.2.refs_3_ = bf16[400,128]{1,0:T(8,128)(2,1)S(1)} collective-permute-done((bf16[400,128]{1,0:T(8,128)(2,1)}, bf16[400,128]{1,0:T(8,128)(2,1)S(1)}, u32[]{:S(2)}, u32[]{:S(2)}) %collective-permute-start.2) | collective-permute-done | bytes 102432 | tf_op jit(solution)/shard_map/ppermute | solution.py:45
  15.1 1.2 %collective-permute-start.5 = (bf16[256,128]{1,0:T(8,128)(2,1)S(1)}, bf16[256,128]{1,0:T(8,128)(2,1)S(1)}, u32[]{:S(2)}, u32[]{:S(2)}) collective-permute-start(bf16[256,128]{1,0:T(8,128)(2,1)S(1)} %slice.17), channel_id=1, source_target_pairs={{0,1},{1,0},{2,3},{3,2},{4,5},{5,4},{6,7},{7,6},{8,9},{9,8},{10,11... | collective-permute-start | bytes 196616 | tf_op jit(solution)/shard_map/ppermute | solution.py:45
  16.3 0.3 collective-permute-start.6
  16.7 0.3 copy-done.8
  17.0 0.3 copy-done.7
  17.3 1.1 %attend_own.1 = (f32[4,256,128]{2,1,0:T(8,128)S(1)}, f32[4,256,128]{2,1,0:T(8,128)S(1)}, f32[4,256,128]{2,1,0:T(8,128)S(1)}, s32[4,32]{1,0:T(4,128)S(1)}, f32[1,1024]{1,0:T(1,128)S(1)}) custom-call(bf16[400,128]{1,0:T(8,128)(2,1)S(1)} %copy-done.2, bf16[400,128]{1,0:T(8,128)(2,1)S(1)} %collective-permute-done.refs_1_, ...), custom_call_target="tpu_custom_call" | custom-call | tf_op jit(solution)/shard_map/attend_own/pallas_call | solution.py:151
  18.5 1.3 %collective-permute-done.6.refs_7_ = bf16[256,128]{1,0:T(8,128)(2,1)S(1)} collective-permute-done((bf16[256,128]{1,0:T(8,128)(2,1)S(1)}, bf16[256,128]{1,0:T(8,128)(2,1)S(1)}, u32[]{:S(2)}, u32[]{:S(2)}) %collective-permute-start.6) | collective-permute-done | bytes 65568 | tf_op jit(solution)/shard_map/ppermute | solution.py:45
  19.8 1.4 %attend_rest.1 = (bf16[128,128]{1,0:T(8,128)(2,1)S(1)}, bf16[128,128]{1,0:T(8,128)(2,1)S(1)}, bf16[128,128]{1,0:T(8,128)(2,1)S(1)}, bf16[128,128]{1,0:T(8,128)(2,1)S(1)}) custom-call(bf16[400,128]{1,0:T(8,128)(2,1)S(1)} %copy-done.2, bf16[400,128]{1,0:T(8,128)(2,1)S(1)} %collective-permute-done.refs_1_, bf16[400,128]{1,0:T(8,128)(2,1)S(1)} %collective-permute-done.1.refs_2_, ...), custom_call_target="tpu_custom_call" | custom-call | tf_op jit(solution)/shard_map/attend_rest/pallas_call | solution.py:166
  21.2 3.0 %collective-permute-start.7 = (bf16[128,128]{1,0:T(8,128)(2,1)S(1)}, bf16[128,128]{1,0:T(8,128)(2,1)S(1)}, u32[]{:S(2)}, u32[]{:S(2)}) collective-permute-start(bf16[128,128]{1,0:T(8,128)(2,1)S(1)} %get-tuple-element.35), channel_id=1, source_target_pairs={{0,2},{1,3},{2,0},{3,1},{4,6},{5,7},{6,4},{7,5},{8,10},{9,11},{10,... | collective-permute-start | bytes 98312 | tf_op jit(solution)/shard_map/ppermute | solution.py:45
  24.2 0.5 %collective-permute-start.8 = (bf16[128,128]{1,0:T(8,128)(2,1)S(1)}, bf16[128,128]{1,0:T(8,128)(2,1)S(1)}, u32[]{:S(2)}, u32[]{:S(2)}) collective-permute-start(bf16[128,128]{1,0:T(8,128)(2,1)S(1)} %get-tuple-element.36), channel_id=1, source_target_pairs={{0,4},{1,5},{2,6},{3,7},{4,0},{5,1},{6,2},{7,3},{8,12},{9,13},{10,... | collective-permute-start | bytes 98312 | tf_op jit(solution)/shard_map/ppermute | solution.py:45
  24.8 1.6 %collective-permute-start.9 = (bf16[128,128]{1,0:T(8,128)(2,1)S(1)}, bf16[128,128]{1,0:T(8,128)(2,1)S(1)}, u32[]{:S(2)}, u32[]{:S(2)}) collective-permute-start(bf16[128,128]{1,0:T(8,128)(2,1)S(1)} %get-tuple-element.37), channel_id=1, source_target_pairs={{0,6},{1,7},{2,4},{3,5},{4,2},{5,3},{6,0},{7,1},{8,14},{9,15},{10,... | collective-permute-start | bytes 98312 | tf_op jit(solution)/shard_map/ppermute | solution.py:45
  26.4 4.0 %collective-permute-start.10 = (bf16[8,2,128,128]{3,2,1,0:T(8,128)(2,1)S(1)}, bf16[8,2,128,128]{3,2,1,0:T(8,128)(2,1)S(1)}, u32[]{:S(2)}, u32[]{:S(2)}) collective-permute-start(bf16[8,2,128,128]{3,2,1,0:T(8,128)(2,1)S(1)} %copy-done.3), channel_id=1, source_target_pairs={{0,8},{8,0},{16,24},{24,16},{1,9},{9,1},{17,25},{25,17},{2,10},{10... | collective-permute-start | bytes 1572872 | tf_op jit(solution)/shard_map/ppermute | solution.py:45
  30.5 1.3 %collective-permute-start.13 = (bf16[8,2,128,128]{3,2,1,0:T(8,128)(2,1)S(1)}, bf16[8,2,128,128]{3,2,1,0:T(8,128)(2,1)S(1)}, u32[]{:S(2)}, u32[]{:S(2)}) collective-permute-start(bf16[8,2,128,128]{3,2,1,0:T(8,128)(2,1)S(1)} %collective-permute-done.12.refs_12_.refs_8_), channel_id=1, source_target_pairs={{0,8},{8,0},{16,24},{24,16},{1,9},{9,1},{17,25},{25,17},{2,10},{10... | collective-permute-start | bytes 1572872 | tf_op jit(solution)/shard_map/ppermute | solution.py:45
  31.8 3.0 %collective-permute-start.15 = (bf16[8,2,128,128]{3,2,1,0:T(8,128)(2,1)S(1)}, bf16[8,2,128,128]{3,2,1,0:T(8,128)(2,1)S(1)}, u32[]{:S(2)}, u32[]{:S(2)}) collective-permute-start(bf16[8,2,128,128]{3,2,1,0:T(8,128)(2,1)S(1)} %collective-permute-done.14.refs_6_), channel_id=1, source_target_pairs={{0,8},{8,0},{16,24},{24,16},{1,9},{9,1},{17,25},{25,17},{2,10},{10... | collective-permute-start | bytes 1572872 | tf_op jit(solution)/shard_map/ppermute | solution.py:45
  34.8 2.7 %mlp_near.1 = (f32[128,1024]{1,0:T(8,128)S(1)}, f32[128,1024]{1,0:T(8,128)S(1)}, f32[128,1024]{1,0:T(8,128)S(1)}, f32[128,128]{1,0:T(8,128)S(1)}, bf16[128,1024]...) custom-call(s32[4,32]{1,0:T(4,128)S(1)} %get-tuple-element.29.table_in_ref, bf16[128,128]{1,0:T(8,128)(2,1)S(1)} %get-tuple-element.34.refs_0_, ...), custom_call_target="tpu_custom_call" | custom-call | tf_op jit(solution)/shard_map/mlp_near/pallas_call | solution.py:281
  37.6 3.3 %mlp_far.1 = (bf16[1,128,1024]{2,1,0:T(8,128)(2,1)}, bf16[1,128,1024]{2,1,0:T(8,128)(2,1)}) custom-call(s32[4,32]{1,0:T(4,128)S(1)} %get-tuple-element.29.table_in_ref, f32[1,1024]{1,0:T(1,128)S(1)} %get-tuple-element.30.refs_6_.gain_ref, bf16[1,128,1024]{2,1,0:T(8,128)(2,1)S(1)} %copy-done.1, f32[128,1024]{1,0:T(8,128)S(1)} %get-tuple-element.41.refs_0_, ...), custom_call_target="tpu_custom_call" | custom-call | tf_op jit(solution)/shard_map/mlp_far/pallas_call | solution.py:340
  (35 shorter events, 0.3 us)
Async XLA Ops:
  0.6 25.8 %collective-permute-start.12 = (bf16[8,2,128,128]{3,2,1,0:T(8,128)(2,1)}, bf16[8,2,128,128]{3,2,1,0:T(8,128)(2,1)S(1)}, u32[]{:S(2)}, u32[]{:S(2)}) collective-permute-start(bf16[8,2,128,128]{3,2,1,0:T(8,128)(2,1)} %refs_10_), channel_id=1, source_target_pairs={{0,16},{8,24},{16,0},{24,8},{1,17},{9,25},{17,1},{25,9},{2,18},{10... | collective-permute-start | bytes 1572872 | tf_op jit(solution)/shard_map/ppermute | solution.py:45
  2.8 29.1 %collective-permute-start.14 = (bf16[8,2,128,128]{3,2,1,0:T(8,128)(2,1)}, bf16[8,2,128,128]{3,2,1,0:T(8,128)(2,1)S(1)}, u32[]{:S(2)}, u32[]{:S(2)}) collective-permute-start(bf16[8,2,128,128]{3,2,1,0:T(8,128)(2,1)} %refs_8_), channel_id=1, source_target_pairs={{0,16},{8,24},{16,0},{24,8},{1,17},{9,25},{17,1},{25,9},{2,18},{10... | collective-permute-start | bytes 1572872 | tf_op jit(solution)/shard_map/ppermute | solution.py:45
  4.7 4.6 %collective-permute-start = (bf16[400,128]{1,0:T(8,128)(2,1)}, bf16[400,128]{1,0:T(8,128)(2,1)S(1)}, u32[]{:S(2)}, u32[]{:S(2)}) collective-permute-start(bf16[400,128]{1,0:T(8,128)(2,1)} %get-tuple-element.26), channel_id=1, source_target_pairs={{0,2},{1,3},{2,0},{3,1},{4,6},{5,7},{6,4},{7,5},{8,10},{9,11},{10,... | collective-permute-start | bytes 307208 | tf_op jit(solution)/shard_map/ppermute | solution.py:45
  6.2 5.5 %collective-permute-start.1 = (bf16[400,128]{1,0:T(8,128)(2,1)}, bf16[400,128]{1,0:T(8,128)(2,1)S(1)}, u32[]{:S(2)}, u32[]{:S(2)}) collective-permute-start(bf16[400,128]{1,0:T(8,128)(2,1)} %get-tuple-element.27), channel_id=1, source_target_pairs={{0,4},{1,5},{2,6},{3,7},{4,0},{5,1},{6,2},{7,3},{8,12},{9,13},{10,... | collective-permute-start | bytes 307208 | tf_op jit(solution)/shard_map/ppermute | solution.py:45
  8.5 6.6 %collective-permute-start.2 = (bf16[400,128]{1,0:T(8,128)(2,1)}, bf16[400,128]{1,0:T(8,128)(2,1)S(1)}, u32[]{:S(2)}, u32[]{:S(2)}) collective-permute-start(bf16[400,128]{1,0:T(8,128)(2,1)} %get-tuple-element.28), channel_id=1, source_target_pairs={{0,6},{1,7},{2,4},{3,5},{4,2},{5,3},{6,0},{7,1},{8,14},{9,15},{10,... | collective-permute-start | bytes 307208 | tf_op jit(solution)/shard_map/ppermute | solution.py:45
  9.3 7.0 %collective-permute-start.3 = (bf16[256,128]{1,0:T(8,128)(2,1)S(1)}, bf16[256,128]{1,0:T(8,128)(2,1)S(1)}, u32[]{:S(2)}, u32[]{:S(2)}) collective-permute-start(bf16[256,128]{1,0:T(8,128)(2,1)S(1)} %slice.12), channel_id=1, source_target_pairs={{0,1},{1,0},{2,3},{3,2},{4,5},{5,4},{6,7},{7,6},{8,9},{9,8},{10,11... | collective-permute-start | bytes 196616 | tf_op jit(solution)/shard_map/ppermute | solution.py:45
  10.5 6.1 %copy-start.2 = (bf16[400,128]{1,0:T(8,128)(2,1)S(1)}, bf16[400,128]{1,0:T(8,128)(2,1)}, u32[]{:S(2)}) copy-start(bf16[400,128]{1,0:T(8,128)(2,1)} %get-tuple-element.25.refs_0_) | copy-start | bytes 307204
  11.6 6.9 %collective-permute-start.4 = (bf16[256,128]{1,0:T(8,128)(2,1)S(1)}, bf16[256,128]{1,0:T(8,128)(2,1)S(1)}, u32[]{:S(2)}, u32[]{:S(2)}) collective-permute-start(bf16[256,128]{1,0:T(8,128)(2,1)S(1)} %slice.16), channel_id=1, source_target_pairs={{0,1},{1,0},{2,3},{3,2},{4,5},{5,4},{6,7},{7,6},{8,9},{9,8},{10,11... | collective-permute-start | bytes 196616 | tf_op jit(solution)/shard_map/ppermute | solution.py:45
  15.1 3.4 %collective-permute-start.5 = (bf16[256,128]{1,0:T(8,128)(2,1)S(1)}, bf16[256,128]{1,0:T(8,128)(2,1)S(1)}, u32[]{:S(2)}, u32[]{:S(2)}) collective-permute-start(bf16[256,128]{1,0:T(8,128)(2,1)S(1)} %slice.17), channel_id=1, source_target_pairs={{0,1},{1,0},{2,3},{3,2},{4,5},{5,4},{6,7},{7,6},{8,9},{9,8},{10,11... | collective-permute-start | bytes 196616 | tf_op jit(solution)/shard_map/ppermute | solution.py:45
  16.3 0.7 %copy-start.8 = (s32[32,2]{0,1:T(2,128)S(1)}, s32[32,2]{0,1:T(2,128)}, u32[]{:S(2)}) copy-start(s32[32,2]{0,1:T(2,128)} %param.22) | copy-start | bytes 772
  16.3 0.7 %copy-start.6 = (f32[1024]{0:T(1024)S(1)}, f32[1024]{0:T(1024)}, u32[]{:S(2)}) copy-start(f32[1024]{0:T(1024)} %param.18) | copy-start | bytes 12292
  16.3 3.5 %collective-permute-start.6 = (bf16[256,128]{1,0:T(8,128)(2,1)S(1)}, bf16[256,128]{1,0:T(8,128)(2,1)S(1)}, u32[]{:S(2)}, u32[]{:S(2)}) collective-permute-start(bf16[256,128]{1,0:T(8,128)(2,1)S(1)} %slice.18), channel_id=1, source_target_pairs={{0,1},{1,0},{2,3},{3,2},{4,5},{5,4},{6,7},{7,6},{8,9},{9,8},{10,11... | collective-permute-start | bytes 196616 | tf_op jit(solution)/shard_map/ppermute | solution.py:45
  17.3 13.1 %copy-start.4 = (bf16[8,2,128,128]{3,2,1,0:T(8,128)(2,1)S(1)}, bf16[8,2,128,128]{3,2,1,0:T(8,128)(2,1)}, u32[]{:S(2)}) copy-start(bf16[8,2,128,128]{3,2,1,0:T(8,128)(2,1)} %refs_10_) | copy-start | bytes 1572868
  19.8 6.6 %copy-start.3 = (bf16[8,2,128,128]{3,2,1,0:T(8,128)(2,1)S(1)}, bf16[8,2,128,128]{3,2,1,0:T(8,128)(2,1)}, u32[]{:S(2)}) copy-start(bf16[8,2,128,128]{3,2,1,0:T(8,128)(2,1)} %refs_8_) | copy-start | bytes 1572868
  19.8 15.0 %copy-start = (bf16[512,1024]{1,0:T(8,128)(2,1)S(1)}, bf16[512,1024]{1,0:T(8,128)(2,1)}, u32[]{:S(2)}) copy-start(bf16[512,1024]{1,0:T(8,128)(2,1)} %refs_4_.1) | copy-start | bytes 3145732
  19.8 15.0 %copy-start.1 = (bf16[1,128,1024]{2,1,0:T(8,128)(2,1)S(1)}, bf16[1,128,1024]{2,1,0:T(8,128)(2,1)}, u32[]{:S(2)}) copy-start(bf16[1,128,1024]{2,1,0:T(8,128)(2,1)} %grad_ref.1) | copy-start | bytes 786436
  19.8 15.0 %copy-start.5 = (bf16[1,128,1024]{2,1,0:T(8,128)(2,1)S(1)}, bf16[1,128,1024]{2,1,0:T(8,128)(2,1)}, u32[]{:S(2)}) copy-start(bf16[1,128,1024]{2,1,0:T(8,128)(2,1)} %refs_5_.1) | copy-start | bytes 786436
  21.2 9.2 %collective-permute-start.7 = (bf16[128,128]{1,0:T(8,128)(2,1)S(1)}, bf16[128,128]{1,0:T(8,128)(2,1)S(1)}, u32[]{:S(2)}, u32[]{:S(2)}) collective-permute-start(bf16[128,128]{1,0:T(8,128)(2,1)S(1)} %get-tuple-element.35), channel_id=1, source_target_pairs={{0,2},{1,3},{2,0},{3,1},{4,6},{5,7},{6,4},{7,5},{8,10},{9,11},{10,... | collective-permute-start | bytes 98312 | tf_op jit(solution)/shard_map/ppermute | solution.py:45
  24.2 6.3 %collective-permute-start.8 = (bf16[128,128]{1,0:T(8,128)(2,1)S(1)}, bf16[128,128]{1,0:T(8,128)(2,1)S(1)}, u32[]{:S(2)}, u32[]{:S(2)}) collective-permute-start(bf16[128,128]{1,0:T(8,128)(2,1)S(1)} %get-tuple-element.36), channel_id=1, source_target_pairs={{0,4},{1,5},{2,6},{3,7},{4,0},{5,1},{6,2},{7,3},{8,12},{9,13},{10,... | collective-permute-start | bytes 98312 | tf_op jit(solution)/shard_map/ppermute | solution.py:45
  24.8 7.1 %collective-permute-start.9 = (bf16[128,128]{1,0:T(8,128)(2,1)S(1)}, bf16[128,128]{1,0:T(8,128)(2,1)S(1)}, u32[]{:S(2)}, u32[]{:S(2)}) collective-permute-start(bf16[128,128]{1,0:T(8,128)(2,1)S(1)} %get-tuple-element.37), channel_id=1, source_target_pairs={{0,6},{1,7},{2,4},{3,5},{4,2},{5,3},{6,0},{7,1},{8,14},{9,15},{10,... | collective-permute-start | bytes 98312 | tf_op jit(solution)/shard_map/ppermute | solution.py:45
  26.4 8.4 %collective-permute-start.10 = (bf16[8,2,128,128]{3,2,1,0:T(8,128)(2,1)S(1)}, bf16[8,2,128,128]{3,2,1,0:T(8,128)(2,1)S(1)}, u32[]{:S(2)}, u32[]{:S(2)}) collective-permute-start(bf16[8,2,128,128]{3,2,1,0:T(8,128)(2,1)S(1)} %copy-done.3), channel_id=1, source_target_pairs={{0,8},{8,0},{16,24},{24,16},{1,9},{9,1},{17,25},{25,17},{2,10},{10... | collective-permute-start | bytes 1572872 | tf_op jit(solution)/shard_map/ppermute | solution.py:45
  30.4 4.4 %collective-permute-start.11 = (bf16[8,2,128,128]{3,2,1,0:T(8,128)(2,1)S(1)}, bf16[8,2,128,128]{3,2,1,0:T(8,128)(2,1)S(1)}, u32[]{:S(2)}, u32[]{:S(2)}) collective-permute-start(bf16[8,2,128,128]{3,2,1,0:T(8,128)(2,1)S(1)} %copy-done.4), channel_id=1, source_target_pairs={{0,8},{8,0},{16,24},{24,16},{1,9},{9,1},{17,25},{25,17},{2,10},{10... | collective-permute-start | bytes 1572872 | tf_op jit(solution)/shard_map/ppermute | solution.py:45
  30.5 4.3 %collective-permute-start.13 = (bf16[8,2,128,128]{3,2,1,0:T(8,128)(2,1)S(1)}, bf16[8,2,128,128]{3,2,1,0:T(8,128)(2,1)S(1)}, u32[]{:S(2)}, u32[]{:S(2)}) collective-permute-start(bf16[8,2,128,128]{3,2,1,0:T(8,128)(2,1)S(1)} %collective-permute-done.12.refs_12_.refs_8_), channel_id=1, source_target_pairs={{0,8},{8,0},{16,24},{24,16},{1,9},{9,1},{17,25},{25,17},{2,10},{10... | collective-permute-start | bytes 1572872 | tf_op jit(solution)/shard_map/ppermute | solution.py:45
  31.8 5.7 %collective-permute-start.15 = (bf16[8,2,128,128]{3,2,1,0:T(8,128)(2,1)S(1)}, bf16[8,2,128,128]{3,2,1,0:T(8,128)(2,1)S(1)}, u32[]{:S(2)}, u32[]{:S(2)}) collective-permute-start(bf16[8,2,128,128]{3,2,1,0:T(8,128)(2,1)S(1)} %collective-permute-done.14.refs_6_), channel_id=1, source_target_pairs={{0,8},{8,0},{16,24},{24,16},{1,9},{9,1},{17,25},{25,17},{2,10},{10... | collective-permute-start | bytes 1572872 | tf_op jit(solution)/shard_map/ppermute | solution.py:45
  (1 other events, 0.7 us)

commit v4 on v3

--- a/solution.py
+++ b/solution.py
@@ -180,9 +180,14 @@
 def places(table_ref, owner, blocks, i):
     block = owner * blocks + i
     return (
-        [block_of(table_ref[n, block]) for n in range(NNZ)],
-        [block_of(table_ref[NNZ + n, block]) for n in range(NNZ)],
+        [table_ref[n, block] for n in range(NNZ)],
+        [table_ref[NNZ + n, block] for n in range(NNZ)],
     )
+
+
+def split_blocks(ref, blocks_ref):
+    for d in range(blocks_ref.shape[0]):
+        blocks_ref[d] = ref[0, :, d * BLK : (d + 1) * BLK]
 
 
 def tall(ref, i):
@@ -199,30 +204,31 @@
 
 
 def dact_of(grad_ref, second_ref, i, cols):
-    grads = jnp.concatenate([grad_ref[0, :, c] for c in cols], axis=1)
+    grads = jnp.concatenate([grad_ref[c] for c in cols], axis=1)
     return lax.dot_general(grads, wide(second_ref, i), NT, preferred_element_type=jnp.float32)
 
 
-def hidden_blocks(table_ref, owners, first_refs, second_refs, dact, normed_ref, act_ref, dpre_ref, mlp_ref, back_ref):
-    blocks = first_refs[0].shape[0]
+def hidden_blocks(table_ref, owners, weight_refs, grad_ref, normed_ref, act_ref, dpre_ref, mlp_ref, back_ref):
+    blocks = weight_refs[0].shape[0] // 2
     steps = [(s, i) for s in range(len(owners)) for i in range(blocks)]
     for k, (s, i) in enumerate(steps):
         rows, cols = places(table_ref, owners[s], blocks, i)
-        picked = jnp.concatenate([normed_ref[:, r] for r in rows], axis=1)
-        pre = jnp.dot(picked, tall(first_refs[s], i), preferred_element_type=jnp.float32)
+        dact = dact_of(grad_ref, weight_refs[s], blocks + i, cols)
+        picked = jnp.concatenate([normed_ref[r] for r in rows], axis=1)
+        pre = jnp.dot(picked, tall(weight_refs[s], i), preferred_element_type=jnp.float32)
         act, slope = slope_terms(pre)
         act_ref[k] = act.astype(jnp.bfloat16)
-        dpre_ref[k] = (dact(k, s, i, cols) * slope).astype(jnp.bfloat16)
+        dpre_ref[k] = (dact * slope).astype(jnp.bfloat16)
     for k, (s, i) in enumerate(steps):
         rows, cols = places(table_ref, owners[s], blocks, i)
-        forward = jnp.dot(act_ref[k], wide(second_refs[s], i), preferred_element_type=jnp.float32)
+        forward = jnp.dot(act_ref[k], wide(weight_refs[s], blocks + i), preferred_element_type=jnp.float32)
         backward = lax.dot_general(
-            dpre_ref[k], tall(first_refs[s], i), NT, preferred_element_type=jnp.float32
+            dpre_ref[k], tall(weight_refs[s], i), NT, preferred_element_type=jnp.float32
         )
         for n in range(NNZ):
-            mlp_ref[:, cols[n]] += forward[:, n * BLK : (n + 1) * BLK]
+            mlp_ref[cols[n]] += forward[:, n * BLK : (n + 1) * BLK]
         for n in range(NNZ):
-            back_ref[:, rows[n]] += backward[:, n * BLK : (n + 1) * BLK]
+            back_ref[rows[n]] += backward[:, n * BLK : (n + 1) * BLK]
 
 
 def near_kernel(near, table_in_ref, *refs):
@@ -231,9 +237,9 @@
     table_copy.start()
     attn_refs, refs = refs[:QUADS], refs[QUADS:]
     proj_ref, tokens_ref, gain_ref, grad_ref = refs[:4]
-    first_refs, second_refs = refs[4 : 4 + near], refs[4 + near : 4 + 3 * near]
-    refs = refs[4 + 3 * near :]
-    mlp_ref, back_ref, unit_ref, rstd_ref, normed_ref, far_dact_ref, act_ref, dpre_ref = refs
+    weight_refs, refs = refs[4 : 4 + near], refs[4 + near :]
+    mlp_ref, back_ref, unit_ref, rstd_ref, normed_ref, act_ref, dpre_ref, grads_ref = refs
+    split_blocks(grad_ref, grads_ref)
     group = lax.rem(lax.axis_index("seq") // HEAD_BIT, QUADS)
     hidden = tokens_ref[0].astype(jnp.float32)
     for s in range(QUADS):
@@ -248,49 +254,45 @@
     unit = centred * rstd
     unit_ref[...] = unit
     rstd_ref[...] = jnp.broadcast_to(rstd, rstd_ref.shape)
-    normed_ref[...] = (unit * gain_ref[...]).astype(jnp.bfloat16)
-    mlp_ref[...] = hidden
+    normed = (unit * gain_ref[...]).astype(jnp.bfloat16)
+    for d in range(mlp_ref.shape[0]):
+        normed_ref[d] = normed[:, d * BLK : (d + 1) * BLK]
+        mlp_ref[d] = hidden[:, d * BLK : (d + 1) * BLK]
     back_ref[...] = jnp.zeros_like(back_ref)
     table_copy.wait()
     me = lax.axis_index("grp")
-    owners = [lax.bitwise_xor(me, s) for s in range(2 * near)]
-    blocks = first_refs[0].shape[0]
+    owners = [lax.bitwise_xor(me, s) for s in range(near)]
     hidden_blocks(
         table_ref,
-        owners[:near],
-        first_refs,
-        second_refs[:near],
-        lambda k, s, i, cols: dact_of(grad_ref, second_refs[s], i, cols),
+        owners,
+        weight_refs,
+        grads_ref,
         normed_ref,
         act_ref,
         dpre_ref,
         mlp_ref,
         back_ref,
     )
-    for s in range(near):
-        for i in range(blocks):
-            _, cols = places(table_ref, owners[near + s], blocks, i)
-            far_dact_ref[s * blocks + i] = dact_of(grad_ref, second_refs[near + s], i, cols)
-
-
-def mlp_near(table, attn, out_proj, tokens, gain, grad_out, firsts, seconds):
-    near = len(firsts)
+
+
+def mlp_near(table, attn, out_proj, tokens, gain, grad_out, weights):
+    near = len(weights)
     rows, width = tokens.shape[1:]
     kept = table.shape[1] // 2
-    args = (*attn, out_proj, tokens, gain, grad_out, *firsts, *seconds)
+    args = (*attn, out_proj, tokens, gain, grad_out, *weights)
     return pl.pallas_call(
         functools.partial(near_kernel, near),
         out_shape=[
-            jax.ShapeDtypeStruct((rows, width), jnp.float32),
-            jax.ShapeDtypeStruct((rows, width), jnp.float32),
+            jax.ShapeDtypeStruct((width // BLK, rows, BLK), jnp.float32),
+            jax.ShapeDtypeStruct((width // BLK, rows, BLK), jnp.float32),
             jax.ShapeDtypeStruct((rows, width), jnp.float32),
             jax.ShapeDtypeStruct((rows, LANES), jnp.float32),
-            jax.ShapeDtypeStruct((rows, width), jnp.bfloat16),
-            jax.ShapeDtypeStruct((kept, rows, BLK), jnp.float32),
+            jax.ShapeDtypeStruct((width // BLK, rows, BLK), jnp.bfloat16),
         ],
         in_specs=[vmem()] * (1 + len(args)),
-        out_specs=[vmem()] * 6,
+        out_specs=[vmem()] * 5,
         scratch_shapes=[pltpu.VMEM((kept, rows, BLK), jnp.bfloat16)] * 2
+        + [pltpu.VMEM((width // BLK, rows, BLK), jnp.bfloat16)]
         + [pltpu.SMEM(table.shape, jnp.int32), pltpu.SemaphoreType.DMA],
         compiler_params=pltpu.CompilerParams(vmem_limit_bytes=VMEM_LIMIT),
         name="mlp_near",
@@ -301,9 +303,10 @@
     refs, (table_ref, table_sem) = refs[:-2], refs[-2:]
     table_copy = pltpu.make_async_copy(table_in_ref, table_ref, table_sem)
     table_copy.start()
-    mlp_in_ref, back_in_ref, unit_ref, rstd_ref, normed_ref, dact_ref = refs[:6]
-    first_refs, second_refs = refs[6 : 6 + near], refs[6 + near : 6 + 2 * near]
-    out_ref, grad_out_ref, mlp_ref, back_ref, act_ref, dpre_ref = refs[6 + 2 * near :]
+    mlp_in_ref, back_in_ref, unit_ref, rstd_ref, normed_ref = refs[:5]
+    weight_refs = refs[5 : 5 + near]
+    out_ref, grad_out_ref, mlp_ref, back_ref, act_ref, dpre_ref, grads_ref = refs[5 + near :]
+    split_blocks(grad_ref, grads_ref)
     mlp_ref[...] = mlp_in_ref[...]
     back_ref[...] = back_in_ref[...]
     table_copy.wait()
@@ -311,17 +314,18 @@
     hidden_blocks(
         table_ref,
         [lax.bitwise_xor(me, near + s) for s in range(near)],
-        first_refs,
-        second_refs,
-        lambda k, s, i, cols: dact_ref[k],
+        weight_refs,
+        grads_ref,
         normed_ref,
         act_ref,
         dpre_ref,
         mlp_ref,
         back_ref,
     )
-    out_ref[0] = mlp_ref[...].astype(jnp.bfloat16)
-    dxhat = back_ref[...] * gain_ref[...]
+    width_blocks = range(mlp_ref.shape[0])
+    for d in width_blocks:
+        out_ref[0, :, d * BLK : (d + 1) * BLK] = mlp_ref[d].astype(jnp.bfloat16)
+    dxhat = jnp.concatenate([back_ref[d] for d in width_blocks], axis=1) * gain_ref[...]
     unit = unit_ref[...]
     dhidden = (
         dxhat
@@ -332,18 +336,19 @@
     grad_out_ref[0] = (grad_ref[0].astype(jnp.float32) + rstd * dhidden).astype(jnp.bfloat16)
 
 
-def mlp_far(table, gain, grad_out, state, firsts, seconds):
-    near = len(firsts)
+def mlp_far(table, gain, grad_out, state, weights):
+    near = len(weights)
     shape = grad_out.shape
     kept = (table.shape[1] // 2, shape[1], BLK)
-    args = (gain, grad_out, *state, *firsts, *seconds)
+    args = (gain, grad_out, *state, *weights)
     return pl.pallas_call(
         functools.partial(far_kernel, near),
         out_shape=[jax.ShapeDtypeStruct(shape, jnp.bfloat16)] * 2,
         in_specs=[vmem()] * (1 + len(args)),
         out_specs=[vmem()] * 2,
-        scratch_shapes=[pltpu.VMEM(shape[1:], jnp.float32)] * 2
+        scratch_shapes=[pltpu.VMEM(state[0].shape, jnp.float32)] * 2
         + [pltpu.VMEM(kept, jnp.bfloat16)] * 2
+        + [pltpu.VMEM(state[4].shape, jnp.bfloat16)]
         + [pltpu.SMEM(table.shape, jnp.int32), pltpu.SemaphoreType.DMA],
         compiler_params=pltpu.CompilerParams(vmem_limit_bytes=VMEM_LIMIT),
         name="mlp_far",
@@ -389,25 +394,21 @@
         held = butterfly(x, "grp", grp_size, near_bits)
         return [held[i] for i in order]
 
-    far_second = over_grp(w2_packed, across)
-    far_first = over_grp(w1_packed, across)
+    weights = jnp.concatenate([w1_packed, w2_packed])
+    far_weights = over_grp(weights, across)
     packed = pack(queries, keys, values, attn_mask, seq_size)
     packed = {0: packed[0], **{s: over_seq(packed[s], s * HEAD_BIT) for s in ORDER}}
     packed = [packed[s] for s in range(QUADS)]
     held = [butterfly(p[BLK : 3 * BLK], "seq", seq_size, flips) for p in packed]
-    near_seconds = over_near(after(w2_packed, *packed[1:]))
-    near_firsts = over_near(after(w1_packed, *packed[1:]))
+    near_weights = over_near(after(weights, *packed[1:]))
     *state, table, gain = attend_own(packed, w1_rows, w2_cols, norm_gain_vector)
     rest = [held[u][t] for t in range(1, len(held[0])) for u in range(QUADS)]
-    far_seconds = over_near(after(far_second, state[0]))
     attn = attend_rest(packed, rest, state)
     attn = {0: attn[0], **{s: over_seq(attn[s], s * HEAD_BIT) for s in ORDER}}
     attn = [attn[s] for s in range(QUADS)]
-    far_firsts = over_near(after(far_first, *attn[1:]))
-    state = mlp_near(
-        table, attn, out_proj, tokens, gain, grad_out, near_firsts, near_seconds + far_seconds
-    )
-    output, grad_tokens = mlp_far(table, gain, grad_out, state, far_firsts, far_seconds)
+    far_weights = over_near(after(far_weights, *attn[1:]))
+    state = mlp_near(table, attn, out_proj, tokens, gain, grad_out, near_weights)
+    output, grad_tokens = mlp_far(table, gain, grad_out, state, far_weights)
     return (output, grad_tokens)
 
 

time: 41.2 us -> 40.9 us (level)
  local copies, waits for them, and re-layouts: 1.56 us -> 2.81 us
  waiting for transfers between devices: 4.68 us -> 3.73 us
  Pallas kernels: 10.4 us -> 9.46 us
    unnamed x18 -> x17, local copies, waits for them, and re-layouts: 0.7 us -> 1.88 us
    ppermute x16 -> x13, waiting for transfers between devices: 4.68 us -> 3.73 us  [exchange(): return lax.ppermute(x, axis, [(i, i ^ flip) for i in range(size)])]
    pallas_call x1, Pallas kernels: 2.73 us -> 2.16 us  [mlp_near(): pl.pallas_call(functools.partial(near_kernel, near), out_shape=[jax.Shape...]
    ppermute x16 -> x13, starting transfers between devices: 23.5 us -> 23.6 us  [exchange(): return lax.ppermute(x, axis, [(i, i ^ flip) for i in range(size)])]
  transfers between devices with their start and end apart: 16 -> 13, of which waited for: 3 -> 4; matrix products, arithmetic and copies ran while one was open for 2% -> 2% of each run, Pallas kernels for 17% -> 16%
where the time goes in v4:
time: 40.9 us; the launch traced here: 40.4 us
  starting transfers between devices  23.6 us (58%)
  Pallas kernels  9.46 us (23%)
  waiting for transfers between devices  3.73 us (9%)
  local copies, waits for them, and re-layouts  2.81 us (7%)
  between operations  0.76 us (2%)
    ppermute x13, starting transfers between devices, exchange(): return lax.ppermute(x, axis, [(i, i ^ flip) for i in range(size)])  23.6 us
    ppermute x13, waiting for transfers between devices, exchange(): return lax.ppermute(x, axis, [(i, i ^ flip) for i in range(size)])  3.73 us
    pallas_call x1, Pallas kernels, mlp_far(): pl.pallas_call(functools.partial(far_kernel, near), out_shape=[jax.ShapeD...  2.93 us
    pallas_call x1, Pallas kernels, mlp_near(): pl.pallas_call(functools.partial(near_kernel, near), out_shape=[jax.Shape...  2.16 us
    unnamed x17, local copies, waits for them, and re-layouts  1.88 us
    pallas_call x1, Pallas kernels, pack(): pl.pallas_call(functools.partial(pack_kernel, seq_size), out_shape=[jax.S...  1.88 us
    pallas_call x1, Pallas kernels, attend_rest(): pl.pallas_call(functools.partial(attend_kernel, False, True, len(rest) //...  1.35 us
    pallas_call x1, Pallas kernels, attend_own(): pl.pallas_call(functools.partial(attend_kernel, True, False, 1), out_shap...  1.14 us
  transfers between devices with their start and end apart: 13, of which 4 were waited for; matrix products, arithmetic and copies ran while one was open for 2% of the time, Pallas kernels for 16%

profile of v4, /device:TPU:1, one launch (start us, length us, event | category | flops | bytes accessed | tf_op | source)
XLA Modules:
  0.0 40.4 jit_solution(6263804765324622787)
XLA Ops:
  0.6 1.1 %constant_dynamic-update-slice_fusion.1 = bf16[16,2,128,128]{3,2,1,0:T(8,128)(2,1)S(1)} fusion(bf16[8,2,128,128]{3,2,1,0:T(8,128)(2,1)} %param.19), kind=kLoop, calls=%fused_computation.1 | loop fusion | bytes 1048576
  1.9 2.1 %collective-permute-start.11 = (bf16[16,2,128,128]{3,2,1,0:T(8,128)(2,1)S(1)}, bf16[16,2,128,128]{3,2,1,0:T(8,128)(2,1)S(1)}, u32[]{:S(2)}, u32[]{:S(2)}) collective-permute-start(bf16[16,2,128,128]{3,2,1,0:T(8,128)(2,1)S(1)} %constant_dynamic-update-slice_fusion.refs_8_), channel_id=1, source_target_pairs={{0,16},{8,24},{16,0},{24,8},{1,17},{9,25},{17,1},{25,9},{2,18},{10... | collective-permute-start | bytes 3145736 | tf_op jit(solution)/shard_map/ppermute | solution.py:45
  4.0 1.9 %pack.1 = (bf16[400,128]{1,0:T(8,128)(2,1)}, bf16[400,128]{1,0:T(8,128)(2,1)}, bf16[400,128]{1,0:T(8,128)(2,1)}, bf16[400,128]{1,0:T(8,128)(2,1)}) custom-call(bf16[1,128,512]{2,1,0:T(8,128)(2,1)} %q_ref.1, bf16[1,128,512]{2,1,0:T(8,128)(2,1)} %k_ref.1, bf16[1,128,512]{2,1,0:T(8,128)(2,1)} %v_ref.1, s32[1,1,8]{2,1,0:T(1,128)} %mask_ref.1), custom_call_target="tpu_custom_call" | custom-call | tf_op jit(solution)/shard_map/pack/pallas_call | solution.py:84
  5.9 1.3 %collective-permute-start = (bf16[400,128]{1,0:T(8,128)(2,1)}, bf16[400,128]{1,0:T(8,128)(2,1)S(1)}, u32[]{:S(2)}, u32[]{:S(2)}) collective-permute-start(bf16[400,128]{1,0:T(8,128)(2,1)} %get-tuple-element.23), channel_id=1, source_target_pairs={{0,2},{1,3},{2,0},{3,1},{4,6},{5,7},{6,4},{7,5},{8,10},{9,11},{10,... | collective-permute-start | bytes 307208 | tf_op jit(solution)/shard_map/ppermute | solution.py:45
  7.2 2.3 %collective-permute-start.1 = (bf16[400,128]{1,0:T(8,128)(2,1)}, bf16[400,128]{1,0:T(8,128)(2,1)S(1)}, u32[]{:S(2)}, u32[]{:S(2)}) collective-permute-start(bf16[400,128]{1,0:T(8,128)(2,1)} %get-tuple-element.24), channel_id=1, source_target_pairs={{0,4},{1,5},{2,6},{3,7},{4,0},{5,1},{6,2},{7,3},{8,12},{9,13},{10,... | collective-permute-start | bytes 307208 | tf_op jit(solution)/shard_map/ppermute | solution.py:45
  9.5 0.8 %slice.12 = bf16[256,128]{1,0:T(8,128)(2,1)S(1)} slice(bf16[400,128]{1,0:T(8,128)(2,1)} %get-tuple-element.22.refs_0_), slice={[128:384], [0:128]} | slice | bytes 131072 | tf_op jit(solution)/shard_map/slice | solution.py:402
  10.4 1.2 %collective-permute-start.3 = (bf16[256,128]{1,0:T(8,128)(2,1)S(1)}, bf16[256,128]{1,0:T(8,128)(2,1)S(1)}, u32[]{:S(2)}, u32[]{:S(2)}) collective-permute-start(bf16[256,128]{1,0:T(8,128)(2,1)S(1)} %slice.12), channel_id=1, source_target_pairs={{0,1},{1,0},{2,3},{3,2},{4,5},{5,4},{6,7},{7,6},{8,9},{9,8},{10,11... | collective-permute-start | bytes 196616 | tf_op jit(solution)/shard_map/ppermute | solution.py:45
  11.6 0.3 collective-permute-start.4
  11.9 0.4 %collective-permute-done.1.refs_2_ = bf16[400,128]{1,0:T(8,128)(2,1)S(1)} collective-permute-done((bf16[400,128]{1,0:T(8,128)(2,1)}, bf16[400,128]{1,0:T(8,128)(2,1)S(1)}, u32[]{:S(2)}, u32[]{:S(2)}) %collective-permute-start.1) | collective-permute-done | bytes 102432 | tf_op jit(solution)/shard_map/ppermute | solution.py:45
  12.4 1.2 %collective-permute-start.5 = (bf16[256,128]{1,0:T(8,128)(2,1)S(1)}, bf16[256,128]{1,0:T(8,128)(2,1)S(1)}, u32[]{:S(2)}, u32[]{:S(2)}) collective-permute-start(bf16[256,128]{1,0:T(8,128)(2,1)S(1)} %slice.17), channel_id=1, source_target_pairs={{0,1},{1,0},{2,3},{3,2},{4,5},{5,4},{6,7},{7,6},{8,9},{9,8},{10,11... | collective-permute-start | bytes 196616 | tf_op jit(solution)/shard_map/ppermute | solution.py:45
  13.6 2.8 %collective-permute-done.2.refs_3_ = bf16[400,128]{1,0:T(8,128)(2,1)S(1)} collective-permute-done((bf16[400,128]{1,0:T(8,128)(2,1)}, bf16[400,128]{1,0:T(8,128)(2,1)S(1)}, u32[]{:S(2)}, u32[]{:S(2)}) %collective-permute-start.2) | collective-permute-done | bytes 102432 | tf_op jit(solution)/shard_map/ppermute | solution.py:45
  16.4 1.3 %collective-permute-start.6 = (bf16[256,128]{1,0:T(8,128)(2,1)S(1)}, bf16[256,128]{1,0:T(8,128)(2,1)S(1)}, u32[]{:S(2)}, u32[]{:S(2)}) collective-permute-start(bf16[256,128]{1,0:T(8,128)(2,1)S(1)} %slice.18), channel_id=1, source_target_pairs={{0,1},{1,0},{2,3},{3,2},{4,5},{5,4},{6,7},{7,6},{8,9},{9,8},{10,11... | collective-permute-start | bytes 196616 | tf_op jit(solution)/shard_map/ppermute | solution.py:45
  17.7 0.7 %copy-done.5 = s32[32,2]{0,1:T(2,128)S(1)} copy-done((s32[32,2]{0,1:T(2,128)S(1)}, s32[32,2]{0,1:T(2,128)}, u32[]{:S(2)}) %copy-start.5) | copy-done | bytes 280
  18.4 1.1 %attend_own.1 = (f32[4,256,128]{2,1,0:T(8,128)S(1)}, f32[4,256,128]{2,1,0:T(8,128)S(1)}, f32[4,256,128]{2,1,0:T(8,128)S(1)}, s32[4,32]{1,0:T(4,128)S(1)}, f32[1,1024]{1,0:T(1,128)S(1)}) custom-call(bf16[400,128]{1,0:T(8,128)(2,1)S(1)} %copy-done.2, bf16[400,128]{1,0:T(8,128)(2,1)S(1)} %collective-permute-done.refs_1_, ...), custom_call_target="tpu_custom_call" | custom-call | tf_op jit(solution)/shard_map/attend_own/pallas_call | solution.py:151
  19.6 0.3 collective-permute-done.6.refs_7_
  19.9 1.4 %attend_rest.1 = (bf16[128,128]{1,0:T(8,128)(2,1)S(1)}, bf16[128,128]{1,0:T(8,128)(2,1)S(1)}, bf16[128,128]{1,0:T(8,128)(2,1)S(1)}, bf16[128,128]{1,0:T(8,128)(2,1)S(1)}) custom-call(bf16[400,128]{1,0:T(8,128)(2,1)S(1)} %copy-done.2, bf16[400,128]{1,0:T(8,128)(2,1)S(1)} %collective-permute-done.refs_1_, bf16[400,128]{1,0:T(8,128)(2,1)S(1)} %collective-permute-done.1.refs_2_, ...), custom_call_target="tpu_custom_call" | custom-call | tf_op jit(solution)/shard_map/attend_rest/pallas_call | solution.py:166
  21.3 3.2 %collective-permute-start.7 = (bf16[128,128]{1,0:T(8,128)(2,1)S(1)}, bf16[128,128]{1,0:T(8,128)(2,1)S(1)}, u32[]{:S(2)}, u32[]{:S(2)}) collective-permute-start(bf16[128,128]{1,0:T(8,128)(2,1)S(1)} %get-tuple-element.32), channel_id=1, source_target_pairs={{0,2},{1,3},{2,0},{3,1},{4,6},{5,7},{6,4},{7,5},{8,10},{9,11},{10,... | collective-permute-start | bytes 98312 | tf_op jit(solution)/shard_map/ppermute | solution.py:45
  24.5 0.3 collective-permute-start.8
  24.8 1.8 %collective-permute-start.9 = (bf16[128,128]{1,0:T(8,128)(2,1)S(1)}, bf16[128,128]{1,0:T(8,128)(2,1)S(1)}, u32[]{:S(2)}, u32[]{:S(2)}) collective-permute-start(bf16[128,128]{1,0:T(8,128)(2,1)S(1)} %get-tuple-element.34), channel_id=1, source_target_pairs={{0,6},{1,7},{2,4},{3,5},{4,2},{5,3},{6,0},{7,1},{8,14},{9,15},{10,... | collective-permute-start | bytes 98312 | tf_op jit(solution)/shard_map/ppermute | solution.py:45
  26.6 4.2 %collective-permute-start.10 = (bf16[16,2,128,128]{3,2,1,0:T(8,128)(2,1)S(1)}, bf16[16,2,128,128]{3,2,1,0:T(8,128)(2,1)S(1)}, u32[]{:S(2)}, u32[]{:S(2)}) collective-permute-start(bf16[16,2,128,128]{3,2,1,0:T(8,128)(2,1)S(1)} %constant_dynamic-update-slice_fusion.refs_8_), channel_id=1, source_target_pairs={{0,8},{8,0},{16,24},{24,16},{1,9},{9,1},{17,25},{25,17},{2,10},{10... | collective-permute-start | bytes 3145736 | tf_op jit(solution)/shard_map/ppermute | solution.py:45
  30.8 4.3 %collective-permute-start.12 = (bf16[16,2,128,128]{3,2,1,0:T(8,128)(2,1)S(1)}, bf16[16,2,128,128]{3,2,1,0:T(8,128)(2,1)S(1)}, u32[]{:S(2)}, u32[]{:S(2)}) collective-permute-start(bf16[16,2,128,128]{3,2,1,0:T(8,128)(2,1)S(1)} %collective-permute-done.11.refs_5_), channel_id=1, source_target_pairs={{0,8},{8,0},{16,24},{24,16},{1,9},{9,1},{17,25},{25,17},{2,10},{10... | collective-permute-start | bytes 3145736 | tf_op jit(solution)/shard_map/ppermute | solution.py:45
  35.2 2.2 %mlp_near.1 = (f32[8,128,128]{2,1,0:T(8,128)S(1)}, f32[8,128,128]{2,1,0:T(8,128)S(1)}, f32[128,1024]{1,0:T(8,128)S(1)}, f32[128,128]{1,0:T(8,128)S(1)}, bf16[8,128,128]{2,1,0:T(8,128)(2,1)S(1)}) custom-call(s32[4,32]{1,0:T(4,128)S(1)} %get-tuple-element.26.table_in_ref, bf16[128,128]{1,0:T(8,128)(2,1)S(1)} %get-tuple-element.31.refs_0_, ...), custom_call_target="tpu_custom_call" | custom-call | tf_op jit(solution)/shard_map/mlp_near/pallas_call | solution.py:283
  37.3 0.1 collective-permute-done.12.refs_6_
  37.4 2.9 %mlp_far.1 = (bf16[1,128,1024]{2,1,0:T(8,128)(2,1)}, bf16[1,128,1024]{2,1,0:T(8,128)(2,1)}) custom-call(s32[4,32]{1,0:T(4,128)S(1)} %get-tuple-element.26.table_in_ref, f32[1,1024]{1,0:T(1,128)S(1)} %get-tuple-element.27.refs_6_.gain_ref, bf16[1,128,1024]{2,1,0:T(8,128)(2,1)S(1)} %copy-done, f32[8,128,128]{2,1,0:T(8,128)S(1)} %get-tuple-element.36.refs_0_, ...), custom_call_target="tpu_custom_call" | custom-call | tf_op jit(solution)/shard_map/mlp_far/pallas_call | solution.py:344
  (29 shorter events, 0.2 us)
Async XLA Ops:
  0.6 1.2 %copy-start.7 = (bf16[8,2,128,128]{3,2,1,0:T(8,128)(2,1)S(1)}, bf16[8,2,128,128]{3,2,1,0:T(8,128)(2,1)}, u32[]{:S(2)}) copy-start(bf16[8,2,128,128]{3,2,1,0:T(8,128)(2,1)} %param.21) | copy-start | bytes 1572868
  1.9 28.9 %collective-permute-start.11 = (bf16[16,2,128,128]{3,2,1,0:T(8,128)(2,1)S(1)}, bf16[16,2,128,128]{3,2,1,0:T(8,128)(2,1)S(1)}, u32[]{:S(2)}, u32[]{:S(2)}) collective-permute-start(bf16[16,2,128,128]{3,2,1,0:T(8,128)(2,1)S(1)} %constant_dynamic-update-slice_fusion.refs_8_), channel_id=1, source_target_pairs={{0,16},{8,24},{16,0},{24,8},{1,17},{9,25},{17,1},{25,9},{2,18},{10... | collective-permute-start | bytes 3145736 | tf_op jit(solution)/shard_map/ppermute | solution.py:45
  5.9 5.7 %collective-permute-start = (bf16[400,128]{1,0:T(8,128)(2,1)}, bf16[400,128]{1,0:T(8,128)(2,1)S(1)}, u32[]{:S(2)}, u32[]{:S(2)}) collective-permute-start(bf16[400,128]{1,0:T(8,128)(2,1)} %get-tuple-element.23), channel_id=1, source_target_pairs={{0,2},{1,3},{2,0},{3,1},{4,6},{5,7},{6,4},{7,5},{8,10},{9,11},{10,... | collective-permute-start | bytes 307208 | tf_op jit(solution)/shard_map/ppermute | solution.py:45
  7.2 5.2 %collective-permute-start.1 = (bf16[400,128]{1,0:T(8,128)(2,1)}, bf16[400,128]{1,0:T(8,128)(2,1)S(1)}, u32[]{:S(2)}, u32[]{:S(2)}) collective-permute-start(bf16[400,128]{1,0:T(8,128)(2,1)} %get-tuple-element.24), channel_id=1, source_target_pairs={{0,4},{1,5},{2,6},{3,7},{4,0},{5,1},{6,2},{7,3},{8,12},{9,13},{10,... | collective-permute-start | bytes 307208 | tf_op jit(solution)/shard_map/ppermute | solution.py:45
  9.5 6.9 %collective-permute-start.2 = (bf16[400,128]{1,0:T(8,128)(2,1)}, bf16[400,128]{1,0:T(8,128)(2,1)S(1)}, u32[]{:S(2)}, u32[]{:S(2)}) collective-permute-start(bf16[400,128]{1,0:T(8,128)(2,1)} %get-tuple-element.25), channel_id=1, source_target_pairs={{0,6},{1,7},{2,4},{3,5},{4,2},{5,3},{6,0},{7,1},{8,14},{9,15},{10,... | collective-permute-start | bytes 307208 | tf_op jit(solution)/shard_map/ppermute | solution.py:45
  10.4 9.2 %collective-permute-start.3 = (bf16[256,128]{1,0:T(8,128)(2,1)S(1)}, bf16[256,128]{1,0:T(8,128)(2,1)S(1)}, u32[]{:S(2)}, u32[]{:S(2)}) collective-permute-start(bf16[256,128]{1,0:T(8,128)(2,1)S(1)} %slice.12), channel_id=1, source_target_pairs={{0,1},{1,0},{2,3},{3,2},{4,5},{5,4},{6,7},{7,6},{8,9},{9,8},{10,11... | collective-permute-start | bytes 196616 | tf_op jit(solution)/shard_map/ppermute | solution.py:45
  11.6 6.1 %copy-start.2 = (bf16[400,128]{1,0:T(8,128)(2,1)S(1)}, bf16[400,128]{1,0:T(8,128)(2,1)}, u32[]{:S(2)}) copy-start(bf16[400,128]{1,0:T(8,128)(2,1)} %get-tuple-element.22.refs_0_) | copy-start | bytes 307204
  11.6 7.9 %collective-permute-start.4 = (bf16[256,128]{1,0:T(8,128)(2,1)S(1)}, bf16[256,128]{1,0:T(8,128)(2,1)S(1)}, u32[]{:S(2)}, u32[]{:S(2)}) collective-permute-start(bf16[256,128]{1,0:T(8,128)(2,1)S(1)} %slice.16), channel_id=1, source_target_pairs={{0,1},{1,0},{2,3},{3,2},{4,5},{5,4},{6,7},{7,6},{8,9},{9,8},{10,11... | collective-permute-start | bytes 196616 | tf_op jit(solution)/shard_map/ppermute | solution.py:45
  12.4 7.2 %collective-permute-start.5 = (bf16[256,128]{1,0:T(8,128)(2,1)S(1)}, bf16[256,128]{1,0:T(8,128)(2,1)S(1)}, u32[]{:S(2)}, u32[]{:S(2)}) collective-permute-start(bf16[256,128]{1,0:T(8,128)(2,1)S(1)} %slice.17), channel_id=1, source_target_pairs={{0,1},{1,0},{2,3},{3,2},{4,5},{5,4},{6,7},{7,6},{8,9},{9,8},{10,11... | collective-permute-start | bytes 196616 | tf_op jit(solution)/shard_map/ppermute | solution.py:45
  16.4 1.3 %copy-start.6 = (s32[32,2]{0,1:T(2,128)S(1)}, s32[32,2]{0,1:T(2,128)}, u32[]{:S(2)}) copy-start(s32[32,2]{0,1:T(2,128)} %param.22) | copy-start | bytes 772
  16.4 1.3 %copy-start.4 = (f32[1024]{0:T(1024)S(1)}, f32[1024]{0:T(1024)}, u32[]{:S(2)}) copy-start(f32[1024]{0:T(1024)} %param.18) | copy-start | bytes 12292
  16.4 3.5 %collective-permute-start.6 = (bf16[256,128]{1,0:T(8,128)(2,1)S(1)}, bf16[256,128]{1,0:T(8,128)(2,1)S(1)}, u32[]{:S(2)}, u32[]{:S(2)}) collective-permute-start(bf16[256,128]{1,0:T(8,128)(2,1)S(1)} %slice.18), channel_id=1, source_target_pairs={{0,1},{1,0},{2,3},{3,2},{4,5},{5,4},{6,7},{7,6},{8,9},{9,8},{10,11... | collective-permute-start | bytes 196616 | tf_op jit(solution)/shard_map/ppermute | solution.py:45
  17.7 0.7 %copy-start.5 = (s32[32,2]{0,1:T(2,128)S(1)}, s32[32,2]{0,1:T(2,128)}, u32[]{:S(2)}) copy-start(s32[32,2]{0,1:T(2,128)} %param.20) | copy-start | bytes 772
  19.9 15.2 %copy-start = (bf16[1,128,1024]{2,1,0:T(8,128)(2,1)S(1)}, bf16[1,128,1024]{2,1,0:T(8,128)(2,1)}, u32[]{:S(2)}) copy-start(bf16[1,128,1024]{2,1,0:T(8,128)(2,1)} %grad_ref.1) | copy-start | bytes 786436
  19.9 15.2 %copy-start.1 = (bf16[512,1024]{1,0:T(8,128)(2,1)S(1)}, bf16[512,1024]{1,0:T(8,128)(2,1)}, u32[]{:S(2)}) copy-start(bf16[512,1024]{1,0:T(8,128)(2,1)} %refs_4_.1) | copy-start | bytes 3145732
  19.9 15.2 %copy-start.3 = (bf16[1,128,1024]{2,1,0:T(8,128)(2,1)S(1)}, bf16[1,128,1024]{2,1,0:T(8,128)(2,1)}, u32[]{:S(2)}) copy-start(bf16[1,128,1024]{2,1,0:T(8,128)(2,1)} %refs_5_.1) | copy-start | bytes 786436
  21.3 9.5 %collective-permute-start.7 = (bf16[128,128]{1,0:T(8,128)(2,1)S(1)}, bf16[128,128]{1,0:T(8,128)(2,1)S(1)}, u32[]{:S(2)}, u32[]{:S(2)}) collective-permute-start(bf16[128,128]{1,0:T(8,128)(2,1)S(1)} %get-tuple-element.32), channel_id=1, source_target_pairs={{0,2},{1,3},{2,0},{3,1},{4,6},{5,7},{6,4},{7,5},{8,10},{9,11},{10,... | collective-permute-start | bytes 98312 | tf_op jit(solution)/shard_map/ppermute | solution.py:45
  24.5 6.3 %collective-permute-start.8 = (bf16[128,128]{1,0:T(8,128)(2,1)S(1)}, bf16[128,128]{1,0:T(8,128)(2,1)S(1)}, u32[]{:S(2)}, u32[]{:S(2)}) collective-permute-start(bf16[128,128]{1,0:T(8,128)(2,1)S(1)} %get-tuple-element.33), channel_id=1, source_target_pairs={{0,4},{1,5},{2,6},{3,7},{4,0},{5,1},{6,2},{7,3},{8,12},{9,13},{10,... | collective-permute-start | bytes 98312 | tf_op jit(solution)/shard_map/ppermute | solution.py:45
  24.8 6.0 %collective-permute-start.9 = (bf16[128,128]{1,0:T(8,128)(2,1)S(1)}, bf16[128,128]{1,0:T(8,128)(2,1)S(1)}, u32[]{:S(2)}, u32[]{:S(2)}) collective-permute-start(bf16[128,128]{1,0:T(8,128)(2,1)S(1)} %get-tuple-element.34), channel_id=1, source_target_pairs={{0,6},{1,7},{2,4},{3,5},{4,2},{5,3},{6,0},{7,1},{8,14},{9,15},{10,... | collective-permute-start | bytes 98312 | tf_op jit(solution)/shard_map/ppermute | solution.py:45
  26.6 8.5 %collective-permute-start.10 = (bf16[16,2,128,128]{3,2,1,0:T(8,128)(2,1)S(1)}, bf16[16,2,128,128]{3,2,1,0:T(8,128)(2,1)S(1)}, u32[]{:S(2)}, u32[]{:S(2)}) collective-permute-start(bf16[16,2,128,128]{3,2,1,0:T(8,128)(2,1)S(1)} %constant_dynamic-update-slice_fusion.refs_8_), channel_id=1, source_target_pairs={{0,8},{8,0},{16,24},{24,16},{1,9},{9,1},{17,25},{25,17},{2,10},{10... | collective-permute-start | bytes 3145736 | tf_op jit(solution)/shard_map/ppermute | solution.py:45
  30.8 6.6 %collective-permute-start.12 = (bf16[16,2,128,128]{3,2,1,0:T(8,128)(2,1)S(1)}, bf16[16,2,128,128]{3,2,1,0:T(8,128)(2,1)S(1)}, u32[]{:S(2)}, u32[]{:S(2)}) collective-permute-start(bf16[16,2,128,128]{3,2,1,0:T(8,128)(2,1)S(1)} %collective-permute-done.11.refs_5_), channel_id=1, source_target_pairs={{0,8},{8,0},{16,24},{24,16},{1,9},{9,1},{17,25},{25,17},{2,10},{10... | collective-permute-start | bytes 3145736 | tf_op jit(solution)/shard_map/ppermute | solution.py:45

commit v5 on v3

--- a/solution.py
+++ b/solution.py
@@ -158,6 +158,7 @@
         in_specs=[vmem()] * (QUADS + 3),
         out_specs=[vmem()] * 5,
         compiler_params=pltpu.CompilerParams(vmem_limit_bytes=VMEM_LIMIT),
+        cost_estimate=pl.CostEstimate(flops=2150000000, bytes_accessed=0, transcendentals=0),
         name="attend_own",
     )(*packed, w1_rows.T, w2_cols.T, gain[None])
 
@@ -169,6 +170,7 @@
         in_specs=[vmem()] * (QUADS + len(rest) + 3),
         out_specs=[vmem()] * QUADS,
         compiler_params=pltpu.CompilerParams(vmem_limit_bytes=VMEM_LIMIT),
+        cost_estimate=pl.CostEstimate(flops=2150000000, bytes_accessed=0, transcendentals=0),
         name="attend_rest",
     )(*packed, *rest, *state)
 
@@ -180,9 +182,14 @@
 def places(table_ref, owner, blocks, i):
     block = owner * blocks + i
     return (
-        [block_of(table_ref[n, block]) for n in range(NNZ)],
-        [block_of(table_ref[NNZ + n, block]) for n in range(NNZ)],
-    )
+        [table_ref[n, block] for n in range(NNZ)],
+        [table_ref[NNZ + n, block] for n in range(NNZ)],
+    )
+
+
+def split_blocks(ref, blocks_ref):
+    for d in range(blocks_ref.shape[0]):
+        blocks_ref[d] = ref[0, :, d * BLK : (d + 1) * BLK]
 
 
 def tall(ref, i):
@@ -198,8 +205,8 @@
     return pre * cdf, cdf + pre * jnp.exp(-0.5 * pre * pre) * 0.3989422804014327
 
 
-def dact_of(grad_ref, second_ref, i, cols):
-    grads = jnp.concatenate([grad_ref[0, :, c] for c in cols], axis=1)
+def dact_of(grads_ref, second_ref, i, cols):
+    grads = jnp.concatenate([grads_ref[c] for c in cols], axis=1)
     return lax.dot_general(grads, wide(second_ref, i), NT, preferred_element_type=jnp.float32)
 
 
@@ -208,7 +215,7 @@
     steps = [(s, i) for s in range(len(owners)) for i in range(blocks)]
     for k, (s, i) in enumerate(steps):
         rows, cols = places(table_ref, owners[s], blocks, i)
-        picked = jnp.concatenate([normed_ref[:, r] for r in rows], axis=1)
+        picked = jnp.concatenate([normed_ref[r] for r in rows], axis=1)
         pre = jnp.dot(picked, tall(first_refs[s], i), preferred_element_type=jnp.float32)
         act, slope = slope_terms(pre)
         act_ref[k] = act.astype(jnp.bfloat16)
@@ -220,9 +227,9 @@
             dpre_ref[k], tall(first_refs[s], i), NT, preferred_element_type=jnp.float32
         )
         for n in range(NNZ):
-            mlp_ref[:, cols[n]] += forward[:, n * BLK : (n + 1) * BLK]
+            mlp_ref[cols[n]] += forward[:, n * BLK : (n + 1) * BLK]
         for n in range(NNZ):
-            back_ref[:, rows[n]] += backward[:, n * BLK : (n + 1) * BLK]
+            back_ref[rows[n]] += backward[:, n * BLK : (n + 1) * BLK]
 
 
 def near_kernel(near, table_in_ref, *refs):
@@ -233,7 +240,8 @@
     proj_ref, tokens_ref, gain_ref, grad_ref = refs[:4]
     first_refs, second_refs = refs[4 : 4 + near], refs[4 + near : 4 + 3 * near]
     refs = refs[4 + 3 * near :]
-    mlp_ref, back_ref, unit_ref, rstd_ref, normed_ref, far_dact_ref, act_ref, dpre_ref = refs
+    mlp_ref, back_ref, unit_ref, rstd_ref, normed_ref, far_dact_ref, act_ref, dpre_ref, grads_ref = refs
+    split_blocks(grad_ref, grads_ref)
     group = lax.rem(lax.axis_index("seq") // HEAD_BIT, QUADS)
     hidden = tokens_ref[0].astype(jnp.float32)
     for s in range(QUADS):
@@ -248,8 +256,10 @@
     unit = centred * rstd
     unit_ref[...] = unit
     rstd_ref[...] = jnp.broadcast_to(rstd, rstd_ref.shape)
-    normed_ref[...] = (unit * gain_ref[...]).astype(jnp.bfloat16)
-    mlp_ref[...] = hidden
+    normed = (unit * gain_ref[...]).astype(jnp.bfloat16)
+    for d in range(mlp_ref.shape[0]):
+        normed_ref[d] = normed[:, d * BLK : (d + 1) * BLK]
+        mlp_ref[d] = hidden[:, d * BLK : (d + 1) * BLK]
     back_ref[...] = jnp.zeros_like(back_ref)
     table_copy.wait()
     me = lax.axis_index("grp")
@@ -260,7 +270,7 @@
         owners[:near],
         first_refs,
         second_refs[:near],
-        lambda k, s, i, cols: dact_of(grad_ref, second_refs[s], i, cols),
+        lambda k, s, i, cols: dact_of(grads_ref, second_refs[s], i, cols),
         normed_ref,
         act_ref,
         dpre_ref,
@@ -270,7 +280,7 @@
     for s in range(near):
         for i in range(blocks):
             _, cols = places(table_ref, owners[near + s], blocks, i)
-            far_dact_ref[s * blocks + i] = dact_of(grad_ref, second_refs[near + s], i, cols)
+            far_dact_ref[s * blocks + i] = dact_of(grads_ref, second_refs[near + s], i, cols)
 
 
 def mlp_near(table, attn, out_proj, tokens, gain, grad_out, firsts, seconds):
@@ -281,16 +291,17 @@
     return pl.pallas_call(
         functools.partial(near_kernel, near),
         out_shape=[
-            jax.ShapeDtypeStruct((rows, width), jnp.float32),
-            jax.ShapeDtypeStruct((rows, width), jnp.float32),
+            jax.ShapeDtypeStruct((width // BLK, rows, BLK), jnp.float32),
+            jax.ShapeDtypeStruct((width // BLK, rows, BLK), jnp.float32),
             jax.ShapeDtypeStruct((rows, width), jnp.float32),
             jax.ShapeDtypeStruct((rows, LANES), jnp.float32),
-            jax.ShapeDtypeStruct((rows, width), jnp.bfloat16),
+            jax.ShapeDtypeStruct((width // BLK, rows, BLK), jnp.bfloat16),
             jax.ShapeDtypeStruct((kept, rows, BLK), jnp.float32),
         ],
         in_specs=[vmem()] * (1 + len(args)),
         out_specs=[vmem()] * 6,
         scratch_shapes=[pltpu.VMEM((kept, rows, BLK), jnp.bfloat16)] * 2
+        + [pltpu.VMEM((width // BLK, rows, BLK), jnp.bfloat16)]
         + [pltpu.SMEM(table.shape, jnp.int32), pltpu.SemaphoreType.DMA],
         compiler_params=pltpu.CompilerParams(vmem_limit_bytes=VMEM_LIMIT),
         name="mlp_near",
@@ -320,8 +331,10 @@
         mlp_ref,
         back_ref,
     )
-    out_ref[0] = mlp_ref[...].astype(jnp.bfloat16)
-    dxhat = back_ref[...] * gain_ref[...]
+    width_blocks = range(mlp_ref.shape[0])
+    for d in width_blocks:
+        out_ref[0, :, d * BLK : (d + 1) * BLK] = mlp_ref[d].astype(jnp.bfloat16)
+    dxhat = jnp.concatenate([back_ref[d] for d in width_blocks], axis=1) * gain_ref[...]
     unit = unit_ref[...]
     dhidden = (
         dxhat
@@ -342,7 +355,7 @@
         out_shape=[jax.ShapeDtypeStruct(shape, jnp.bfloat16)] * 2,
         in_specs=[vmem()] * (1 + len(args)),
         out_specs=[vmem()] * 2,
-        scratch_shapes=[pltpu.VMEM(shape[1:], jnp.float32)] * 2
+        scratch_shapes=[pltpu.VMEM(state[0].shape, jnp.float32)] * 2
         + [pltpu.VMEM(kept, jnp.bfloat16)] * 2
         + [pltpu.SMEM(table.shape, jnp.int32), pltpu.SemaphoreType.DMA],
         compiler_params=pltpu.CompilerParams(vmem_limit_bytes=VMEM_LIMIT),

time: 41.2 us -> 38.9 us (0.944)
  starting transfers between devices: 23.5 us -> 21.9 us
  Pallas kernels: 10.4 us -> 9.74 us
    ppermute x16, starting transfers between devices: 23.5 us -> 21.9 us  [exchange(): return lax.ppermute(x, axis, [(i, i ^ flip) for i in range(size)])]
  transfers between devices with their start and end apart: 16 -> 16, of which waited for: 3 -> 3; matrix products, arithmetic and copies ran while one was open for 2% -> 2% of each run, Pallas kernels for 17% -> 13%
where the time goes in v5:
time: 38.9 us; the launch traced here: 38.7 us
  starting transfers between devices  21.9 us (56%)
  Pallas kernels  9.74 us (25%)
  waiting for transfers between devices  4.71 us (12%)
  local copies, waits for them, and re-layouts  1.56 us (4%)
  between operations  0.75 us (2%)
    ppermute x16, starting transfers between devices, exchange(): return lax.ppermute(x, axis, [(i, i ^ flip) for i in range(size)])  21.9 us
    ppermute x16, waiting for transfers between devices, exchange(): return lax.ppermute(x, axis, [(i, i ^ flip) for i in range(size)])  4.71 us
    pallas_call x1, Pallas kernels, mlp_far(): pl.pallas_call(functools.partial(far_kernel, near), out_shape=[jax.ShapeD...  3 us
    pallas_call x1, Pallas kernels, mlp_near(): pl.pallas_call(functools.partial(near_kernel, near), out_shape=[jax.Shape...  2.35 us
    pallas_call x1, Pallas kernels, pack(): pl.pallas_call(functools.partial(pack_kernel, seq_size), out_shape=[jax.S...  1.88 us
    pallas_call x1, Pallas kernels, attend_rest(): pl.pallas_call(functools.partial(attend_kernel, False, True, len(rest) //...  1.35 us
    pallas_call x1, Pallas kernels, attend_own(): pl.pallas_call(functools.partial(attend_kernel, True, False, 1), out_shap...  1.15 us
    slice x4, local copies, waits for them, and re-layouts, body(): held = [butterfly(p[BLK:3 * BLK], 'seq', seq_size, flips) for p in packed]  0.86 us
  transfers between devices with their start and end apart: 16, of which 3 were waited for; matrix products, arithmetic and copies ran while one was open for 2% of the time, Pallas kernels for 13%

profile of v5, /device:TPU:1, one launch (start us, length us, event | category | flops | bytes accessed | tf_op | source)
XLA Modules:
  0.0 38.7 jit_solution(15468222257048836065)
XLA Ops:
  0.6 1.9 %pack.1 = (bf16[400,128]{1,0:T(8,128)(2,1)}, bf16[400,128]{1,0:T(8,128)(2,1)}, bf16[400,128]{1,0:T(8,128)(2,1)}, bf16[400,128]{1,0:T(8,128)(2,1)}) custom-call(bf16[1,128,512]{2,1,0:T(8,128)(2,1)} %q_ref.1, bf16[1,128,512]{2,1,0:T(8,128)(2,1)} %k_ref.1, bf16[1,128,512]{2,1,0:T(8,128)(2,1)} %v_ref.1, s32[1,1,8]{2,1,0:T(1,128)} %mask_ref.1), custom_call_target="tpu_custom_call" | custom-call | tf_op jit(solution)/shard_map/pack/pallas_call | solution.py:84
  2.5 2.1 %collective-permute-start = (bf16[400,128]{1,0:T(8,128)(2,1)}, bf16[400,128]{1,0:T(8,128)(2,1)S(1)}, u32[]{:S(2)}, u32[]{:S(2)}) collective-permute-start(bf16[400,128]{1,0:T(8,128)(2,1)} %get-tuple-element.26), channel_id=1, source_target_pairs={{0,2},{1,3},{2,0},{3,1},{4,6},{5,7},{6,4},{7,5},{8,10},{9,11},{10,... | collective-permute-start | bytes 307208 | tf_op jit(solution)/shard_map/ppermute | solution.py:45
  4.6 2.3 %collective-permute-start.1 = (bf16[400,128]{1,0:T(8,128)(2,1)}, bf16[400,128]{1,0:T(8,128)(2,1)S(1)}, u32[]{:S(2)}, u32[]{:S(2)}) collective-permute-start(bf16[400,128]{1,0:T(8,128)(2,1)} %get-tuple-element.27), channel_id=1, source_target_pairs={{0,4},{1,5},{2,6},{3,7},{4,0},{5,1},{6,2},{7,3},{8,12},{9,13},{10,... | collective-permute-start | bytes 307208 | tf_op jit(solution)/shard_map/ppermute | solution.py:45
  6.9 1.2 %collective-permute-start.12 = (bf16[8,2,128,128]{3,2,1,0:T(8,128)(2,1)}, bf16[8,2,128,128]{3,2,1,0:T(8,128)(2,1)S(1)}, u32[]{:S(2)}, u32[]{:S(2)}) collective-permute-start(bf16[8,2,128,128]{3,2,1,0:T(8,128)(2,1)} %refs_10_), channel_id=1, source_target_pairs={{0,16},{8,24},{16,0},{24,8},{1,17},{9,25},{17,1},{25,9},{2,18},{10... | collective-permute-start | bytes 1572872 | tf_op jit(solution)/shard_map/ppermute | solution.py:45
  8.4 0.8 %slice.12 = bf16[256,128]{1,0:T(8,128)(2,1)S(1)} slice(bf16[400,128]{1,0:T(8,128)(2,1)} %get-tuple-element.25.refs_0_), slice={[128:384], [0:128]} | slice | bytes 131072 | tf_op jit(solution)/shard_map/slice | solution.py:410
  9.3 1.2 %collective-permute-start.3 = (bf16[256,128]{1,0:T(8,128)(2,1)S(1)}, bf16[256,128]{1,0:T(8,128)(2,1)S(1)}, u32[]{:S(2)}, u32[]{:S(2)}) collective-permute-start(bf16[256,128]{1,0:T(8,128)(2,1)S(1)} %slice.12), channel_id=1, source_target_pairs={{0,1},{1,0},{2,3},{3,2},{4,5},{5,4},{6,7},{7,6},{8,9},{9,8},{10,11... | collective-permute-start | bytes 196616 | tf_op jit(solution)/shard_map/ppermute | solution.py:45
  10.5 0.3 collective-permute-start.4
  10.8 3.1 %collective-permute-done.2.refs_3_ = bf16[400,128]{1,0:T(8,128)(2,1)S(1)} collective-permute-done((bf16[400,128]{1,0:T(8,128)(2,1)}, bf16[400,128]{1,0:T(8,128)(2,1)S(1)}, u32[]{:S(2)}, u32[]{:S(2)}) %collective-permute-start.2) | collective-permute-done | bytes 102432 | tf_op jit(solution)/shard_map/ppermute | solution.py:45
  13.9 1.2 %collective-permute-start.5 = (bf16[256,128]{1,0:T(8,128)(2,1)S(1)}, bf16[256,128]{1,0:T(8,128)(2,1)S(1)}, u32[]{:S(2)}, u32[]{:S(2)}) collective-permute-start(bf16[256,128]{1,0:T(8,128)(2,1)S(1)} %slice.17), channel_id=1, source_target_pairs={{0,1},{1,0},{2,3},{3,2},{4,5},{5,4},{6,7},{7,6},{8,9},{9,8},{10,11... | collective-permute-start | bytes 196616 | tf_op jit(solution)/shard_map/ppermute | solution.py:45
  15.2 0.3 collective-permute-start.6
  15.5 0.3 copy-done.8
  15.8 0.3 copy-done.7
  16.2 1.1 %attend_own.1 = (f32[4,256,128]{2,1,0:T(8,128)S(1)}, f32[4,256,128]{2,1,0:T(8,128)S(1)}, f32[4,256,128]{2,1,0:T(8,128)S(1)}, s32[4,32]{1,0:T(4,128)S(1)}, f32[1,1024]{1,0:T(1,128)S(1)}) custom-call(bf16[400,128]{1,0:T(8,128)(2,1)S(1)} %copy-done.5, bf16[400,128]{1,0:T(8,128)(2,1)S(1)} %collective-permute-done.refs_1_, ...), custom_call_target="tpu_custom_call" | custom-call | flops 2150000128 | tf_op jit(solution)/shard_map/attend_own/pallas_call | solution.py:151
  17.3 1.3 %collective-permute-done.6.refs_7_ = bf16[256,128]{1,0:T(8,128)(2,1)S(1)} collective-permute-done((bf16[256,128]{1,0:T(8,128)(2,1)S(1)}, bf16[256,128]{1,0:T(8,128)(2,1)S(1)}, u32[]{:S(2)}, u32[]{:S(2)}) %collective-permute-start.6) | collective-permute-done | bytes 65568 | tf_op jit(solution)/shard_map/ppermute | solution.py:45
  18.7 1.4 %attend_rest.1 = (bf16[128,128]{1,0:T(8,128)(2,1)S(1)}, bf16[128,128]{1,0:T(8,128)(2,1)S(1)}, bf16[128,128]{1,0:T(8,128)(2,1)S(1)}, bf16[128,128]{1,0:T(8,128)(2,1)S(1)}) custom-call(bf16[400,128]{1,0:T(8,128)(2,1)S(1)} %copy-done.5, bf16[400,128]{1,0:T(8,128)(2,1)S(1)} %collective-permute-done.refs_1_, bf16[400,128]{1,0:T(8,128)(2,1)S(1)} %collective-permute-done.1.refs_2_, ...), custom_call_target="tpu_custom_call" | custom-call | flops 2150000128 | tf_op jit(solution)/shard_map/attend_rest/pallas_call | solution.py:167
  20.0 2.7 %collective-permute-start.7 = (bf16[128,128]{1,0:T(8,128)(2,1)S(1)}, bf16[128,128]{1,0:T(8,128)(2,1)S(1)}, u32[]{:S(2)}, u32[]{:S(2)}) collective-permute-start(bf16[128,128]{1,0:T(8,128)(2,1)S(1)} %get-tuple-element.35), channel_id=1, source_target_pairs={{0,2},{1,3},{2,0},{3,1},{4,6},{5,7},{6,4},{7,5},{8,10},{9,11},{10,... | collective-permute-start | bytes 98312 | tf_op jit(solution)/shard_map/ppermute | solution.py:45
  22.7 0.9 %collective-permute-start.8 = (bf16[128,128]{1,0:T(8,128)(2,1)S(1)}, bf16[128,128]{1,0:T(8,128)(2,1)S(1)}, u32[]{:S(2)}, u32[]{:S(2)}) collective-permute-start(bf16[128,128]{1,0:T(8,128)(2,1)S(1)} %get-tuple-element.36), channel_id=1, source_target_pairs={{0,4},{1,5},{2,6},{3,7},{4,0},{5,1},{6,2},{7,3},{8,12},{9,13},{10,... | collective-permute-start | bytes 98312 | tf_op jit(solution)/shard_map/ppermute | solution.py:45
  23.6 1.2 %collective-permute-start.9 = (bf16[128,128]{1,0:T(8,128)(2,1)S(1)}, bf16[128,128]{1,0:T(8,128)(2,1)S(1)}, u32[]{:S(2)}, u32[]{:S(2)}) collective-permute-start(bf16[128,128]{1,0:T(8,128)(2,1)S(1)} %get-tuple-element.37), channel_id=1, source_target_pairs={{0,6},{1,7},{2,4},{3,5},{4,2},{5,3},{6,0},{7,1},{8,14},{9,15},{10,... | collective-permute-start | bytes 98312 | tf_op jit(solution)/shard_map/ppermute | solution.py:45
  24.8 4.1 %collective-permute-start.10 = (bf16[8,2,128,128]{3,2,1,0:T(8,128)(2,1)S(1)}, bf16[8,2,128,128]{3,2,1,0:T(8,128)(2,1)S(1)}, u32[]{:S(2)}, u32[]{:S(2)}) collective-permute-start(bf16[8,2,128,128]{3,2,1,0:T(8,128)(2,1)S(1)} %copy-done.2), channel_id=1, source_target_pairs={{0,8},{8,0},{16,24},{24,16},{1,9},{9,1},{17,25},{25,17},{2,10},{10... | collective-permute-start | bytes 1572872 | tf_op jit(solution)/shard_map/ppermute | solution.py:45
  29.0 1.3 %collective-permute-start.13 = (bf16[8,2,128,128]{3,2,1,0:T(8,128)(2,1)S(1)}, bf16[8,2,128,128]{3,2,1,0:T(8,128)(2,1)S(1)}, u32[]{:S(2)}, u32[]{:S(2)}) collective-permute-start(bf16[8,2,128,128]{3,2,1,0:T(8,128)(2,1)S(1)} %collective-permute-done.12.refs_12_.refs_8_), channel_id=1, source_target_pairs={{0,8},{8,0},{16,24},{24,16},{1,9},{9,1},{17,25},{25,17},{2,10},{10... | collective-permute-start | bytes 1572872 | tf_op jit(solution)/shard_map/ppermute | solution.py:45
  30.3 0.3 collective-permute-done.14.refs_6_
  30.6 2.7 %collective-permute-start.15 = (bf16[8,2,128,128]{3,2,1,0:T(8,128)(2,1)S(1)}, bf16[8,2,128,128]{3,2,1,0:T(8,128)(2,1)S(1)}, u32[]{:S(2)}, u32[]{:S(2)}) collective-permute-start(bf16[8,2,128,128]{3,2,1,0:T(8,128)(2,1)S(1)} %collective-permute-done.14.refs_6_), channel_id=1, source_target_pairs={{0,8},{8,0},{16,24},{24,16},{1,9},{9,1},{17,25},{25,17},{2,10},{10... | collective-permute-start | bytes 1572872 | tf_op jit(solution)/shard_map/ppermute | solution.py:45
  33.3 2.4 %mlp_near.1 = (f32[8,128,128]{2,1,0:T(8,128)S(1)}, f32[8,128,128]{2,1,0:T(8,128)S(1)}, f32[128,1024]{1,0:T(8,128)S(1)}, f32[128,128]{1,0:T(8,128)S(1)}, bf16[8,1...) custom-call(s32[4,32]{1,0:T(4,128)S(1)} %get-tuple-element.29.table_in_ref, ...), custom_call_target="tpu_custom_call" | custom-call | tf_op jit(solution)/shard_map/mlp_near/pallas_call | solution.py:291
  35.7 3.0 %mlp_far.1 = (bf16[1,128,1024]{2,1,0:T(8,128)(2,1)}, bf16[1,128,1024]{2,1,0:T(8,128)(2,1)}) custom-call(s32[4,32]{1,0:T(4,128)S(1)} %get-tuple-element.29.table_in_ref, f32[1,1024]{1,0:T(1,128)S(1)} %get-tuple-element.30.refs_6_.gain_ref, bf16[1,128,1024]{2,1,0:T(8,128)(2,1)S(1)} %copy-done.1, f32[8,128,128]{2,1,0:T(8,128)S(1)} %get-tuple-element.41.refs_0_, ...), custom_call_target="tpu_custom_call" | custom-call | tf_op jit(solution)/shard_map/mlp_far/pallas_call | solution.py:353
  (35 shorter events, 0.4 us)
Async XLA Ops:
  2.5 6.8 %collective-permute-start = (bf16[400,128]{1,0:T(8,128)(2,1)}, bf16[400,128]{1,0:T(8,128)(2,1)S(1)}, u32[]{:S(2)}, u32[]{:S(2)}) collective-permute-start(bf16[400,128]{1,0:T(8,128)(2,1)} %get-tuple-element.26), channel_id=1, source_target_pairs={{0,2},{1,3},{2,0},{3,1},{4,6},{5,7},{6,4},{7,5},{8,10},{9,11},{10,... | collective-permute-start | bytes 307208 | tf_op jit(solution)/shard_map/ppermute | solution.py:45
  4.6 5.8 %collective-permute-start.1 = (bf16[400,128]{1,0:T(8,128)(2,1)}, bf16[400,128]{1,0:T(8,128)(2,1)S(1)}, u32[]{:S(2)}, u32[]{:S(2)}) collective-permute-start(bf16[400,128]{1,0:T(8,128)(2,1)} %get-tuple-element.27), channel_id=1, source_target_pairs={{0,4},{1,5},{2,6},{3,7},{4,0},{5,1},{6,2},{7,3},{8,12},{9,13},{10,... | collective-permute-start | bytes 307208 | tf_op jit(solution)/shard_map/ppermute | solution.py:45
  6.9 7.0 %collective-permute-start.2 = (bf16[400,128]{1,0:T(8,128)(2,1)}, bf16[400,128]{1,0:T(8,128)(2,1)S(1)}, u32[]{:S(2)}, u32[]{:S(2)}) collective-permute-start(bf16[400,128]{1,0:T(8,128)(2,1)} %get-tuple-element.28), channel_id=1, source_target_pairs={{0,6},{1,7},{2,4},{3,5},{4,2},{5,3},{6,0},{7,1},{8,14},{9,15},{10,... | collective-permute-start | bytes 307208 | tf_op jit(solution)/shard_map/ppermute | solution.py:45
  6.9 17.9 %collective-permute-start.12 = (bf16[8,2,128,128]{3,2,1,0:T(8,128)(2,1)}, bf16[8,2,128,128]{3,2,1,0:T(8,128)(2,1)S(1)}, u32[]{:S(2)}, u32[]{:S(2)}) collective-permute-start(bf16[8,2,128,128]{3,2,1,0:T(8,128)(2,1)} %refs_10_), channel_id=1, source_target_pairs={{0,16},{8,24},{16,0},{24,8},{1,17},{9,25},{17,1},{25,9},{2,18},{10... | collective-permute-start | bytes 1572872 | tf_op jit(solution)/shard_map/ppermute | solution.py:45
  8.2 22.4 %collective-permute-start.14 = (bf16[8,2,128,128]{3,2,1,0:T(8,128)(2,1)}, bf16[8,2,128,128]{3,2,1,0:T(8,128)(2,1)S(1)}, u32[]{:S(2)}, u32[]{:S(2)}) collective-permute-start(bf16[8,2,128,128]{3,2,1,0:T(8,128)(2,1)} %refs_8_), channel_id=1, source_target_pairs={{0,16},{8,24},{16,0},{24,8},{1,17},{9,25},{17,1},{25,9},{2,18},{10... | collective-permute-start | bytes 1572872 | tf_op jit(solution)/shard_map/ppermute | solution.py:45
  9.3 5.9 %collective-permute-start.3 = (bf16[256,128]{1,0:T(8,128)(2,1)S(1)}, bf16[256,128]{1,0:T(8,128)(2,1)S(1)}, u32[]{:S(2)}, u32[]{:S(2)}) collective-permute-start(bf16[256,128]{1,0:T(8,128)(2,1)S(1)} %slice.12), channel_id=1, source_target_pairs={{0,1},{1,0},{2,3},{3,2},{4,5},{5,4},{6,7},{7,6},{8,9},{9,8},{10,11... | collective-permute-start | bytes 196616 | tf_op jit(solution)/shard_map/ppermute | solution.py:45
  10.5 5.0 %copy-start.5 = (bf16[400,128]{1,0:T(8,128)(2,1)S(1)}, bf16[400,128]{1,0:T(8,128)(2,1)}, u32[]{:S(2)}) copy-start(bf16[400,128]{1,0:T(8,128)(2,1)} %get-tuple-element.25.refs_0_) | copy-start | bytes 307204
  10.5 6.8 %collective-permute-start.4 = (bf16[256,128]{1,0:T(8,128)(2,1)S(1)}, bf16[256,128]{1,0:T(8,128)(2,1)S(1)}, u32[]{:S(2)}, u32[]{:S(2)}) collective-permute-start(bf16[256,128]{1,0:T(8,128)(2,1)S(1)} %slice.16), channel_id=1, source_target_pairs={{0,1},{1,0},{2,3},{3,2},{4,5},{5,4},{6,7},{7,6},{8,9},{9,8},{10,11... | collective-permute-start | bytes 196616 | tf_op jit(solution)/shard_map/ppermute | solution.py:45
  13.9 3.4 %collective-permute-start.5 = (bf16[256,128]{1,0:T(8,128)(2,1)S(1)}, bf16[256,128]{1,0:T(8,128)(2,1)S(1)}, u32[]{:S(2)}, u32[]{:S(2)}) collective-permute-start(bf16[256,128]{1,0:T(8,128)(2,1)S(1)} %slice.17), channel_id=1, source_target_pairs={{0,1},{1,0},{2,3},{3,2},{4,5},{5,4},{6,7},{7,6},{8,9},{9,8},{10,11... | collective-permute-start | bytes 196616 | tf_op jit(solution)/shard_map/ppermute | solution.py:45
  15.1 0.7 %copy-start.6 = (f32[1024]{0:T(1024)S(1)}, f32[1024]{0:T(1024)}, u32[]{:S(2)}) copy-start(f32[1024]{0:T(1024)} %param.18) | copy-start | bytes 12292
  15.2 3.5 %collective-permute-start.6 = (bf16[256,128]{1,0:T(8,128)(2,1)S(1)}, bf16[256,128]{1,0:T(8,128)(2,1)S(1)}, u32[]{:S(2)}, u32[]{:S(2)}) collective-permute-start(bf16[256,128]{1,0:T(8,128)(2,1)S(1)} %slice.18), channel_id=1, source_target_pairs={{0,1},{1,0},{2,3},{3,2},{4,5},{5,4},{6,7},{7,6},{8,9},{9,8},{10,11... | collective-permute-start | bytes 196616 | tf_op jit(solution)/shard_map/ppermute | solution.py:45
  15.5 0.7 %copy-start.7 = (s32[32,2]{0,1:T(2,128)S(1)}, s32[32,2]{0,1:T(2,128)}, u32[]{:S(2)}) copy-start(s32[32,2]{0,1:T(2,128)} %param.20) | copy-start | bytes 772
  18.6 6.2 %copy-start.2 = (bf16[8,2,128,128]{3,2,1,0:T(8,128)(2,1)S(1)}, bf16[8,2,128,128]{3,2,1,0:T(8,128)(2,1)}, u32[]{:S(2)}) copy-start(bf16[8,2,128,128]{3,2,1,0:T(8,128)(2,1)} %refs_8_) | copy-start | bytes 1572868
  18.6 10.3 %copy-start.3 = (bf16[8,2,128,128]{3,2,1,0:T(8,128)(2,1)S(1)}, bf16[8,2,128,128]{3,2,1,0:T(8,128)(2,1)}, u32[]{:S(2)}) copy-start(bf16[8,2,128,128]{3,2,1,0:T(8,128)(2,1)} %refs_10_) | copy-start | bytes 1572868
  18.6 14.7 %copy-start = (bf16[512,1024]{1,0:T(8,128)(2,1)S(1)}, bf16[512,1024]{1,0:T(8,128)(2,1)}, u32[]{:S(2)}) copy-start(bf16[512,1024]{1,0:T(8,128)(2,1)} %refs_4_.1) | copy-start | bytes 3145732
  18.6 14.7 %copy-start.1 = (bf16[1,128,1024]{2,1,0:T(8,128)(2,1)S(1)}, bf16[1,128,1024]{2,1,0:T(8,128)(2,1)}, u32[]{:S(2)}) copy-start(bf16[1,128,1024]{2,1,0:T(8,128)(2,1)} %grad_ref.1) | copy-start | bytes 786436
  18.6 14.7 %copy-start.4 = (bf16[1,128,1024]{2,1,0:T(8,128)(2,1)S(1)}, bf16[1,128,1024]{2,1,0:T(8,128)(2,1)}, u32[]{:S(2)}) copy-start(bf16[1,128,1024]{2,1,0:T(8,128)(2,1)} %refs_5_.1) | copy-start | bytes 786436
  20.0 8.9 %collective-permute-start.7 = (bf16[128,128]{1,0:T(8,128)(2,1)S(1)}, bf16[128,128]{1,0:T(8,128)(2,1)S(1)}, u32[]{:S(2)}, u32[]{:S(2)}) collective-permute-start(bf16[128,128]{1,0:T(8,128)(2,1)S(1)} %get-tuple-element.35), channel_id=1, source_target_pairs={{0,2},{1,3},{2,0},{3,1},{4,6},{5,7},{6,4},{7,5},{8,10},{9,11},{10,... | collective-permute-start | bytes 98312 | tf_op jit(solution)/shard_map/ppermute | solution.py:45
  22.7 6.3 %collective-permute-start.8 = (bf16[128,128]{1,0:T(8,128)(2,1)S(1)}, bf16[128,128]{1,0:T(8,128)(2,1)S(1)}, u32[]{:S(2)}, u32[]{:S(2)}) collective-permute-start(bf16[128,128]{1,0:T(8,128)(2,1)S(1)} %get-tuple-element.36), channel_id=1, source_target_pairs={{0,4},{1,5},{2,6},{3,7},{4,0},{5,1},{6,2},{7,3},{8,12},{9,13},{10,... | collective-permute-start | bytes 98312 | tf_op jit(solution)/shard_map/ppermute | solution.py:45
  23.6 6.7 %collective-permute-start.9 = (bf16[128,128]{1,0:T(8,128)(2,1)S(1)}, bf16[128,128]{1,0:T(8,128)(2,1)S(1)}, u32[]{:S(2)}, u32[]{:S(2)}) collective-permute-start(bf16[128,128]{1,0:T(8,128)(2,1)S(1)} %get-tuple-element.37), channel_id=1, source_target_pairs={{0,6},{1,7},{2,4},{3,5},{4,2},{5,3},{6,0},{7,1},{8,14},{9,15},{10,... | collective-permute-start | bytes 98312 | tf_op jit(solution)/shard_map/ppermute | solution.py:45
  24.8 8.4 %collective-permute-start.10 = (bf16[8,2,128,128]{3,2,1,0:T(8,128)(2,1)S(1)}, bf16[8,2,128,128]{3,2,1,0:T(8,128)(2,1)S(1)}, u32[]{:S(2)}, u32[]{:S(2)}) collective-permute-start(bf16[8,2,128,128]{3,2,1,0:T(8,128)(2,1)S(1)} %copy-done.2), channel_id=1, source_target_pairs={{0,8},{8,0},{16,24},{24,16},{1,9},{9,1},{17,25},{25,17},{2,10},{10... | collective-permute-start | bytes 1572872 | tf_op jit(solution)/shard_map/ppermute | solution.py:45
  28.9 4.4 %collective-permute-start.11 = (bf16[8,2,128,128]{3,2,1,0:T(8,128)(2,1)S(1)}, bf16[8,2,128,128]{3,2,1,0:T(8,128)(2,1)S(1)}, u32[]{:S(2)}, u32[]{:S(2)}) collective-permute-start(bf16[8,2,128,128]{3,2,1,0:T(8,128)(2,1)S(1)} %copy-done.3), channel_id=1, source_target_pairs={{0,8},{8,0},{16,24},{24,16},{1,9},{9,1},{17,25},{25,17},{2,10},{10... | collective-permute-start | bytes 1572872 | tf_op jit(solution)/shard_map/ppermute | solution.py:45
  29.0 4.3 %collective-permute-start.13 = (bf16[8,2,128,128]{3,2,1,0:T(8,128)(2,1)S(1)}, bf16[8,2,128,128]{3,2,1,0:T(8,128)(2,1)S(1)}, u32[]{:S(2)}, u32[]{:S(2)}) collective-permute-start(bf16[8,2,128,128]{3,2,1,0:T(8,128)(2,1)S(1)} %collective-permute-done.12.refs_12_.refs_8_), channel_id=1, source_target_pairs={{0,8},{8,0},{16,24},{24,16},{1,9},{9,1},{17,25},{25,17},{2,10},{10... | collective-permute-start | bytes 1572872 | tf_op jit(solution)/shard_map/ppermute | solution.py:45
  30.6 5.1 %collective-permute-start.15 = (bf16[8,2,128,128]{3,2,1,0:T(8,128)(2,1)S(1)}, bf16[8,2,128,128]{3,2,1,0:T(8,128)(2,1)S(1)}, u32[]{:S(2)}, u32[]{:S(2)}) collective-permute-start(bf16[8,2,128,128]{3,2,1,0:T(8,128)(2,1)S(1)} %collective-permute-done.14.refs_6_), channel_id=1, source_target_pairs={{0,8},{8,0},{16,24},{24,16},{1,9},{9,1},{17,25},{25,17},{2,10},{10... | collective-permute-start | bytes 1572872 | tf_op jit(solution)/shard_map/ppermute | solution.py:45
  (1 other events, 0.7 us)

commit v6 on v5

--- a/solution.py
+++ b/solution.py
@@ -16,7 +16,7 @@
 NT = (((1,), (1,)), ((), ()))
 ORDER = (2, 3, 1)
 VMEM_LIMIT = 24 * 1024 * 1024
-PACK_LIMIT = 60 * 1024 * 1024
+PACK_LIMIT = int(53.5 * 1024 * 1024)
 
 
 def vmem():

time: 38.9 us -> 38.6 us (level)
  Pallas kernels: 9.74 us -> 9 us
  starting transfers between devices: 21.9 us -> 22.3 us
    slice x4, local copies, waits for them, and re-layouts: 0.86 us -> 0.02 us  [body(): held = [butterfly(p[BLK:3 * BLK], 'seq', seq_size, flips) for p in packed]]
    pallas_call x1, Pallas kernels: 1.88 us -> 1.14 us  [pack(): pl.pallas_call(functools.partial(pack_kernel, seq_size), out_shape=[jax.S...]
    unnamed x18, local copies, waits for them, and re-layouts: 0.7 us -> 1.35 us
  transfers between devices with their start and end apart: 16 -> 16, of which waited for: 3 -> 3; matrix products, arithmetic and copies ran while one was open for 2% -> 0% of each run, Pallas kernels for 13% -> 13%
where the time goes in v6:
time: 38.6 us; the launch traced here: 38.5 us
  starting transfers between devices  22.3 us (58%)
  Pallas kernels  9 us (23%)
  waiting for transfers between devices  5.04 us (13%)
  local copies, waits for them, and re-layouts  1.37 us (4%)
  between operations  0.76 us (2%)
    ppermute x16, starting transfers between devices, exchange(): return lax.ppermute(x, axis, [(i, i ^ flip) for i in range(size)])  22.3 us
    ppermute x16, waiting for transfers between devices, exchange(): return lax.ppermute(x, axis, [(i, i ^ flip) for i in range(size)])  5.04 us
    pallas_call x1, Pallas kernels, mlp_far(): pl.pallas_call(functools.partial(far_kernel, near), out_shape=[jax.ShapeD...  3.01 us
    pallas_call x1, Pallas kernels, mlp_near(): pl.pallas_call(functools.partial(near_kernel, near), out_shape=[jax.Shape...  2.35 us
    pallas_call x1, Pallas kernels, attend_rest(): pl.pallas_call(functools.partial(attend_kernel, False, True, len(rest) //...  1.35 us
    unnamed x18, local copies, waits for them, and re-layouts  1.35 us
    pallas_call x1, Pallas kernels, attend_own(): pl.pallas_call(functools.partial(attend_kernel, True, False, 1), out_shap...  1.15 us
    pallas_call x1, Pallas kernels, pack(): pl.pallas_call(functools.partial(pack_kernel, seq_size), out_shape=[jax.S...  1.14 us
  transfers between devices with their start and end apart: 16, of which 3 were waited for; matrix products, arithmetic and copies ran while one was open for 0% of the time, Pallas kernels for 13%

profile of v6, /device:TPU:1, one launch (start us, length us, event | category | flops | bytes accessed | tf_op | source)
XLA Modules:
  0.0 38.5 jit_solution(11527828155606565678)
XLA Ops:
  0.6 0.6 %copy-done.5 = s32[1,1,8]{2,1,0:T(1,128)S(1)} copy-done((s32[1,1,8]{2,1,0:T(1,128)S(1)}, s32[1,1,8]{2,1,0:T(1,128)}, u32[]{:S(2)}) %copy-start.5) | copy-done | bytes 56
  1.3 1.1 %pack.1 = (bf16[400,128]{1,0:T(8,128)(2,1)S(1)}, bf16[400,128]{1,0:T(8,128)(2,1)S(1)}, bf16[400,128]{1,0:T(8,128)(2,1)S(1)}, bf16[400,128]{1,0:T(8,128)(2,1)S(1)}) custom-call(bf16[1,128,512]{2,1,0:T(8,128)(2,1)} %q_ref.1, bf16[1,128,512]{2,1,0:T(8,128)(2,1)} %k_ref.1, bf16[1,128,512]{2,1,0:T(8,128)(2,1)} %v_ref.1, s32[1,1,8]{2,1,0:T(1,128)S(1)} %copy-done.5), custom_call_target="tpu_custom_call" | custom-call | tf_op jit(solution)/shard_map/pack/pallas_call | solution.py:84
  2.4 2.2 %collective-permute-start = (bf16[400,128]{1,0:T(8,128)(2,1)S(1)}, bf16[400,128]{1,0:T(8,128)(2,1)S(1)}, u32[]{:S(2)}, u32[]{:S(2)}) collective-permute-start(bf16[400,128]{1,0:T(8,128)(2,1)S(1)} %get-tuple-element.26), channel_id=1, source_target_pairs={{0,2},{1,3},{2,0},{3,1},{4,6},{5,7},{6,4},{7,5},{8,10},{9,11},{10,... | collective-permute-start | bytes 307208 | tf_op jit(solution)/shard_map/ppermute | solution.py:45
  4.6 2.3 %collective-permute-start.1 = (bf16[400,128]{1,0:T(8,128)(2,1)S(1)}, bf16[400,128]{1,0:T(8,128)(2,1)S(1)}, u32[]{:S(2)}, u32[]{:S(2)}) collective-permute-start(bf16[400,128]{1,0:T(8,128)(2,1)S(1)} %get-tuple-element.27), channel_id=1, source_target_pairs={{0,4},{1,5},{2,6},{3,7},{4,0},{5,1},{6,2},{7,3},{8,12},{9,13},{10,... | collective-permute-start | bytes 307208 | tf_op jit(solution)/shard_map/ppermute | solution.py:45
  6.9 1.2 %collective-permute-start.12 = (bf16[8,2,128,128]{3,2,1,0:T(8,128)(2,1)}, bf16[8,2,128,128]{3,2,1,0:T(8,128)(2,1)S(1)}, u32[]{:S(2)}, u32[]{:S(2)}) collective-permute-start(bf16[8,2,128,128]{3,2,1,0:T(8,128)(2,1)} %refs_10_), channel_id=1, source_target_pairs={{0,16},{8,24},{16,0},{24,8},{1,17},{9,25},{17,1},{25,9},{2,18},{10... | collective-permute-start | bytes 1572872 | tf_op jit(solution)/shard_map/ppermute | solution.py:45
  8.4 1.3 %collective-permute-start.3 = (bf16[256,128]{1,0:T(8,128)(2,1)S(1)}, bf16[256,128]{1,0:T(8,128)(2,1)S(1)}, u32[]{:S(2)}, u32[]{:S(2)}) collective-permute-start(bf16[256,128]{1,0:T(8,128)(2,1)S(1)} %slice.12), channel_id=1, source_target_pairs={{0,1},{1,0},{2,3},{3,2},{4,5},{5,4},{6,7},{7,6},{8,9},{9,8},{10,11... | collective-permute-start | bytes 196616 | tf_op jit(solution)/shard_map/ppermute | solution.py:45
  9.7 0.8 %collective-permute-start.4 = (bf16[256,128]{1,0:T(8,128)(2,1)S(1)}, bf16[256,128]{1,0:T(8,128)(2,1)S(1)}, u32[]{:S(2)}, u32[]{:S(2)}) collective-permute-start(bf16[256,128]{1,0:T(8,128)(2,1)S(1)} %slice.16), channel_id=1, source_target_pairs={{0,1},{1,0},{2,3},{3,2},{4,5},{5,4},{6,7},{7,6},{8,9},{9,8},{10,11... | collective-permute-start | bytes 196616 | tf_op jit(solution)/shard_map/ppermute | solution.py:45
  10.5 3.2 %collective-permute-done.2.refs_3_ = bf16[400,128]{1,0:T(8,128)(2,1)S(1)} collective-permute-done((bf16[400,128]{1,0:T(8,128)(2,1)S(1)}, bf16[400,128]{1,0:T(8,128)(2,1)S(1)}, u32[]{:S(2)}, u32[]{:S(2)}) %collective-permute-start.2) | collective-permute-done | bytes 102432 | tf_op jit(solution)/shard_map/ppermute | solution.py:45
  13.7 1.2 %collective-permute-start.5 = (bf16[256,128]{1,0:T(8,128)(2,1)S(1)}, bf16[256,128]{1,0:T(8,128)(2,1)S(1)}, u32[]{:S(2)}, u32[]{:S(2)}) collective-permute-start(bf16[256,128]{1,0:T(8,128)(2,1)S(1)} %slice.17), channel_id=1, source_target_pairs={{0,1},{1,0},{2,3},{3,2},{4,5},{5,4},{6,7},{7,6},{8,9},{9,8},{10,11... | collective-permute-start | bytes 196616 | tf_op jit(solution)/shard_map/ppermute | solution.py:45
  14.9 0.3 collective-permute-start.6
  15.3 0.3 copy-done.8
  15.6 0.3 copy-done.7
  15.9 1.1 %attend_own.1 = (f32[4,256,128]{2,1,0:T(8,128)S(1)}, f32[4,256,128]{2,1,0:T(8,128)S(1)}, f32[4,256,128]{2,1,0:T(8,128)S(1)}, s32[4,32]{1,0:T(4,128)S(1)}, f32[1,1024]{1,0:T(1,128)S(1)}) custom-call(bf16[400,128]{1,0:T(8,128)(2,1)S(1)} %get-tuple-element.25.refs_0_, bf16[400,128]{1,0:T(8,128)(2,1)S(1)} %collective-permute-done.refs_1_, ...), custom_call_target="tpu_custom_call" | custom-call | flops 2150000128 | tf_op jit(solution)/shard_map/attend_own/pallas_call | solution.py:151
  17.1 1.3 %collective-permute-done.6.refs_7_ = bf16[256,128]{1,0:T(8,128)(2,1)S(1)} collective-permute-done((bf16[256,128]{1,0:T(8,128)(2,1)S(1)}, bf16[256,128]{1,0:T(8,128)(2,1)S(1)}, u32[]{:S(2)}, u32[]{:S(2)}) %collective-permute-start.6) | collective-permute-done | bytes 65568 | tf_op jit(solution)/shard_map/ppermute | solution.py:45
  18.4 1.4 %attend_rest.1 = (bf16[128,128]{1,0:T(8,128)(2,1)S(1)}, bf16[128,128]{1,0:T(8,128)(2,1)S(1)}, bf16[128,128]{1,0:T(8,128)(2,1)S(1)}, bf16[128,128]{1,0:T(8,128)(2,1)S(1)}) custom-call(bf16[400,128]{1,0:T(8,128)(2,1)S(1)} %get-tuple-element.25.refs_0_, bf16[400,128]{1,0:T(8,128)(2,1)S(1)} %collective-permute-done.refs_1_, ...), custom_call_target="tpu_custom_call" | custom-call | flops 2150000128 | tf_op jit(solution)/shard_map/attend_rest/pallas_call | solution.py:167
  19.8 2.6 %collective-permute-start.7 = (bf16[128,128]{1,0:T(8,128)(2,1)S(1)}, bf16[128,128]{1,0:T(8,128)(2,1)S(1)}, u32[]{:S(2)}, u32[]{:S(2)}) collective-permute-start(bf16[128,128]{1,0:T(8,128)(2,1)S(1)} %get-tuple-element.35), channel_id=1, source_target_pairs={{0,2},{1,3},{2,0},{3,1},{4,6},{5,7},{6,4},{7,5},{8,10},{9,11},{10,... | collective-permute-start | bytes 98312 | tf_op jit(solution)/shard_map/ppermute | solution.py:45
  22.4 1.0 %collective-permute-start.8 = (bf16[128,128]{1,0:T(8,128)(2,1)S(1)}, bf16[128,128]{1,0:T(8,128)(2,1)S(1)}, u32[]{:S(2)}, u32[]{:S(2)}) collective-permute-start(bf16[128,128]{1,0:T(8,128)(2,1)S(1)} %get-tuple-element.36), channel_id=1, source_target_pairs={{0,4},{1,5},{2,6},{3,7},{4,0},{5,1},{6,2},{7,3},{8,12},{9,13},{10,... | collective-permute-start | bytes 98312 | tf_op jit(solution)/shard_map/ppermute | solution.py:45
  23.4 1.1 %collective-permute-start.9 = (bf16[128,128]{1,0:T(8,128)(2,1)S(1)}, bf16[128,128]{1,0:T(8,128)(2,1)S(1)}, u32[]{:S(2)}, u32[]{:S(2)}) collective-permute-start(bf16[128,128]{1,0:T(8,128)(2,1)S(1)} %get-tuple-element.37), channel_id=1, source_target_pairs={{0,6},{1,7},{2,4},{3,5},{4,2},{5,3},{6,0},{7,1},{8,14},{9,15},{10,... | collective-permute-start | bytes 98312 | tf_op jit(solution)/shard_map/ppermute | solution.py:45
  24.5 4.2 %collective-permute-start.10 = (bf16[8,2,128,128]{3,2,1,0:T(8,128)(2,1)S(1)}, bf16[8,2,128,128]{3,2,1,0:T(8,128)(2,1)S(1)}, u32[]{:S(2)}, u32[]{:S(2)}) collective-permute-start(bf16[8,2,128,128]{3,2,1,0:T(8,128)(2,1)S(1)} %copy-done.2), channel_id=1, source_target_pairs={{0,8},{8,0},{16,24},{24,16},{1,9},{9,1},{17,25},{25,17},{2,10},{10... | collective-permute-start | bytes 1572872 | tf_op jit(solution)/shard_map/ppermute | solution.py:45
  28.8 1.3 %collective-permute-start.13 = (bf16[8,2,128,128]{3,2,1,0:T(8,128)(2,1)S(1)}, bf16[8,2,128,128]{3,2,1,0:T(8,128)(2,1)S(1)}, u32[]{:S(2)}, u32[]{:S(2)}) collective-permute-start(bf16[8,2,128,128]{3,2,1,0:T(8,128)(2,1)S(1)} %collective-permute-done.12.refs_12_.refs_8_), channel_id=1, source_target_pairs={{0,8},{8,0},{16,24},{24,16},{1,9},{9,1},{17,25},{25,17},{2,10},{10... | collective-permute-start | bytes 1572872 | tf_op jit(solution)/shard_map/ppermute | solution.py:45
  30.1 0.5 %collective-permute-done.14.refs_6_ = bf16[8,2,128,128]{3,2,1,0:T(8,128)(2,1)S(1)} collective-permute-done((bf16[8,2,128,128]{3,2,1,0:T(8,128)(2,1)}, bf16[8,2,128,128]{3,2,1,0:T(8,128)(2,1)S(1)}, u32[]{:S(2)}, u32[]{:S(2)}) %collective-permute-start.14) | collective-permute-done | bytes 524320 | tf_op jit(solution)/shard_map/ppermute | solution.py:45
  30.6 2.5 %collective-permute-start.15 = (bf16[8,2,128,128]{3,2,1,0:T(8,128)(2,1)S(1)}, bf16[8,2,128,128]{3,2,1,0:T(8,128)(2,1)S(1)}, u32[]{:S(2)}, u32[]{:S(2)}) collective-permute-start(bf16[8,2,128,128]{3,2,1,0:T(8,128)(2,1)S(1)} %collective-permute-done.14.refs_6_), channel_id=1, source_target_pairs={{0,8},{8,0},{16,24},{24,16},{1,9},{9,1},{17,25},{25,17},{2,10},{10... | collective-permute-start | bytes 1572872 | tf_op jit(solution)/shard_map/ppermute | solution.py:45
  33.1 2.3 %mlp_near.1 = (f32[8,128,128]{2,1,0:T(8,128)S(1)}, f32[8,128,128]{2,1,0:T(8,128)S(1)}, f32[128,1024]{1,0:T(8,128)S(1)}, f32[128,128]{1,0:T(8,128)S(1)}, bf16[8,1...) custom-call(s32[4,32]{1,0:T(4,128)S(1)} %get-tuple-element.29.table_in_ref, ...), custom_call_target="tpu_custom_call" | custom-call | tf_op jit(solution)/shard_map/mlp_near/pallas_call | solution.py:291
  35.5 3.0 %mlp_far.1 = (bf16[1,128,1024]{2,1,0:T(8,128)(2,1)}, bf16[1,128,1024]{2,1,0:T(8,128)(2,1)}) custom-call(s32[4,32]{1,0:T(4,128)S(1)} %get-tuple-element.29.table_in_ref, f32[1,1024]{1,0:T(1,128)S(1)} %get-tuple-element.30.refs_6_.gain_ref, bf16[1,128,1024]{2,1,0:T(8,128)(2,1)S(1)} %copy-done.1, f32[8,128,128]{2,1,0:T(8,128)S(1)} %get-tuple-element.41.refs_0_, ...), custom_call_target="tpu_custom_call" | custom-call | tf_op jit(solution)/shard_map/mlp_far/pallas_call | solution.py:353
  (35 shorter events, 0.4 us)
Async XLA Ops:
  2.4 6.0 %collective-permute-start = (bf16[400,128]{1,0:T(8,128)(2,1)S(1)}, bf16[400,128]{1,0:T(8,128)(2,1)S(1)}, u32[]{:S(2)}, u32[]{:S(2)}) collective-permute-start(bf16[400,128]{1,0:T(8,128)(2,1)S(1)} %get-tuple-element.26), channel_id=1, source_target_pairs={{0,2},{1,3},{2,0},{3,1},{4,6},{5,7},{6,4},{7,5},{8,10},{9,11},{10,... | collective-permute-start | bytes 307208 | tf_op jit(solution)/shard_map/ppermute | solution.py:45
  4.6 5.1 %collective-permute-start.1 = (bf16[400,128]{1,0:T(8,128)(2,1)S(1)}, bf16[400,128]{1,0:T(8,128)(2,1)S(1)}, u32[]{:S(2)}, u32[]{:S(2)}) collective-permute-start(bf16[400,128]{1,0:T(8,128)(2,1)S(1)} %get-tuple-element.27), channel_id=1, source_target_pairs={{0,4},{1,5},{2,6},{3,7},{4,0},{5,1},{6,2},{7,3},{8,12},{9,13},{10,... | collective-permute-start | bytes 307208 | tf_op jit(solution)/shard_map/ppermute | solution.py:45
  6.9 6.8 %collective-permute-start.2 = (bf16[400,128]{1,0:T(8,128)(2,1)S(1)}, bf16[400,128]{1,0:T(8,128)(2,1)S(1)}, u32[]{:S(2)}, u32[]{:S(2)}) collective-permute-start(bf16[400,128]{1,0:T(8,128)(2,1)S(1)} %get-tuple-element.28), channel_id=1, source_target_pairs={{0,6},{1,7},{2,4},{3,5},{4,2},{5,3},{6,0},{7,1},{8,14},{9,15},{10,... | collective-permute-start | bytes 307208 | tf_op jit(solution)/shard_map/ppermute | solution.py:45
  6.9 17.6 %collective-permute-start.12 = (bf16[8,2,128,128]{3,2,1,0:T(8,128)(2,1)}, bf16[8,2,128,128]{3,2,1,0:T(8,128)(2,1)S(1)}, u32[]{:S(2)}, u32[]{:S(2)}) collective-permute-start(bf16[8,2,128,128]{3,2,1,0:T(8,128)(2,1)} %refs_10_), channel_id=1, source_target_pairs={{0,16},{8,24},{16,0},{24,8},{1,17},{9,25},{17,1},{25,9},{2,18},{10... | collective-permute-start | bytes 1572872 | tf_op jit(solution)/shard_map/ppermute | solution.py:45
  8.2 22.4 %collective-permute-start.14 = (bf16[8,2,128,128]{3,2,1,0:T(8,128)(2,1)}, bf16[8,2,128,128]{3,2,1,0:T(8,128)(2,1)S(1)}, u32[]{:S(2)}, u32[]{:S(2)}) collective-permute-start(bf16[8,2,128,128]{3,2,1,0:T(8,128)(2,1)} %refs_8_), channel_id=1, source_target_pairs={{0,16},{8,24},{16,0},{24,8},{1,17},{9,25},{17,1},{25,9},{2,18},{10... | collective-permute-start | bytes 1572872 | tf_op jit(solution)/shard_map/ppermute | solution.py:45
  8.4 6.5 %collective-permute-start.3 = (bf16[256,128]{1,0:T(8,128)(2,1)S(1)}, bf16[256,128]{1,0:T(8,128)(2,1)S(1)}, u32[]{:S(2)}, u32[]{:S(2)}) collective-permute-start(bf16[256,128]{1,0:T(8,128)(2,1)S(1)} %slice.12), channel_id=1, source_target_pairs={{0,1},{1,0},{2,3},{3,2},{4,5},{5,4},{6,7},{7,6},{8,9},{9,8},{10,11... | collective-permute-start | bytes 196616 | tf_op jit(solution)/shard_map/ppermute | solution.py:45
  9.7 7.4 %collective-permute-start.4 = (bf16[256,128]{1,0:T(8,128)(2,1)S(1)}, bf16[256,128]{1,0:T(8,128)(2,1)S(1)}, u32[]{:S(2)}, u32[]{:S(2)}) collective-permute-start(bf16[256,128]{1,0:T(8,128)(2,1)S(1)} %slice.16), channel_id=1, source_target_pairs={{0,1},{1,0},{2,3},{3,2},{4,5},{5,4},{6,7},{7,6},{8,9},{9,8},{10,11... | collective-permute-start | bytes 196616 | tf_op jit(solution)/shard_map/ppermute | solution.py:45
  13.7 3.4 %collective-permute-start.5 = (bf16[256,128]{1,0:T(8,128)(2,1)S(1)}, bf16[256,128]{1,0:T(8,128)(2,1)S(1)}, u32[]{:S(2)}, u32[]{:S(2)}) collective-permute-start(bf16[256,128]{1,0:T(8,128)(2,1)S(1)} %slice.17), channel_id=1, source_target_pairs={{0,1},{1,0},{2,3},{3,2},{4,5},{5,4},{6,7},{7,6},{8,9},{9,8},{10,11... | collective-permute-start | bytes 196616 | tf_op jit(solution)/shard_map/ppermute | solution.py:45
  14.9 0.7 %copy-start.8 = (s32[32,2]{0,1:T(2,128)S(1)}, s32[32,2]{0,1:T(2,128)}, u32[]{:S(2)}) copy-start(s32[32,2]{0,1:T(2,128)} %param.22) | copy-start | bytes 772
  14.9 0.7 %copy-start.6 = (f32[1024]{0:T(1024)S(1)}, f32[1024]{0:T(1024)}, u32[]{:S(2)}) copy-start(f32[1024]{0:T(1024)} %param.18) | copy-start | bytes 12292
  14.9 3.5 %collective-permute-start.6 = (bf16[256,128]{1,0:T(8,128)(2,1)S(1)}, bf16[256,128]{1,0:T(8,128)(2,1)S(1)}, u32[]{:S(2)}, u32[]{:S(2)}) collective-permute-start(bf16[256,128]{1,0:T(8,128)(2,1)S(1)} %slice.18), channel_id=1, source_target_pairs={{0,1},{1,0},{2,3},{3,2},{4,5},{5,4},{6,7},{7,6},{8,9},{9,8},{10,11... | collective-permute-start | bytes 196616 | tf_op jit(solution)/shard_map/ppermute | solution.py:45
  15.3 0.7 %copy-start.7 = (s32[32,2]{0,1:T(2,128)S(1)}, s32[32,2]{0,1:T(2,128)}, u32[]{:S(2)}) copy-start(s32[32,2]{0,1:T(2,128)} %param.20) | copy-start | bytes 772
  18.4 6.1 %copy-start.2 = (bf16[8,2,128,128]{3,2,1,0:T(8,128)(2,1)S(1)}, bf16[8,2,128,128]{3,2,1,0:T(8,128)(2,1)}, u32[]{:S(2)}) copy-start(bf16[8,2,128,128]{3,2,1,0:T(8,128)(2,1)} %refs_8_) | copy-start | bytes 1572868
  18.4 10.3 %copy-start.3 = (bf16[8,2,128,128]{3,2,1,0:T(8,128)(2,1)S(1)}, bf16[8,2,128,128]{3,2,1,0:T(8,128)(2,1)}, u32[]{:S(2)}) copy-start(bf16[8,2,128,128]{3,2,1,0:T(8,128)(2,1)} %refs_10_) | copy-start | bytes 1572868
  18.4 14.7 %copy-start = (bf16[512,1024]{1,0:T(8,128)(2,1)S(1)}, bf16[512,1024]{1,0:T(8,128)(2,1)}, u32[]{:S(2)}) copy-start(bf16[512,1024]{1,0:T(8,128)(2,1)} %refs_4_.1) | copy-start | bytes 3145732
  18.4 14.7 %copy-start.1 = (bf16[1,128,1024]{2,1,0:T(8,128)(2,1)S(1)}, bf16[1,128,1024]{2,1,0:T(8,128)(2,1)}, u32[]{:S(2)}) copy-start(bf16[1,128,1024]{2,1,0:T(8,128)(2,1)} %grad_ref.1) | copy-start | bytes 786436
  18.4 14.7 %copy-start.4 = (bf16[1,128,1024]{2,1,0:T(8,128)(2,1)S(1)}, bf16[1,128,1024]{2,1,0:T(8,128)(2,1)}, u32[]{:S(2)}) copy-start(bf16[1,128,1024]{2,1,0:T(8,128)(2,1)} %refs_5_.1) | copy-start | bytes 786436
  19.8 8.9 %collective-permute-start.7 = (bf16[128,128]{1,0:T(8,128)(2,1)S(1)}, bf16[128,128]{1,0:T(8,128)(2,1)S(1)}, u32[]{:S(2)}, u32[]{:S(2)}) collective-permute-start(bf16[128,128]{1,0:T(8,128)(2,1)S(1)} %get-tuple-element.35), channel_id=1, source_target_pairs={{0,2},{1,3},{2,0},{3,1},{4,6},{5,7},{6,4},{7,5},{8,10},{9,11},{10,... | collective-permute-start | bytes 98312 | tf_op jit(solution)/shard_map/ppermute | solution.py:45
  22.4 6.4 %collective-permute-start.8 = (bf16[128,128]{1,0:T(8,128)(2,1)S(1)}, bf16[128,128]{1,0:T(8,128)(2,1)S(1)}, u32[]{:S(2)}, u32[]{:S(2)}) collective-permute-start(bf16[128,128]{1,0:T(8,128)(2,1)S(1)} %get-tuple-element.36), channel_id=1, source_target_pairs={{0,4},{1,5},{2,6},{3,7},{4,0},{5,1},{6,2},{7,3},{8,12},{9,13},{10,... | collective-permute-start | bytes 98312 | tf_op jit(solution)/shard_map/ppermute | solution.py:45
  23.4 6.7 %collective-permute-start.9 = (bf16[128,128]{1,0:T(8,128)(2,1)S(1)}, bf16[128,128]{1,0:T(8,128)(2,1)S(1)}, u32[]{:S(2)}, u32[]{:S(2)}) collective-permute-start(bf16[128,128]{1,0:T(8,128)(2,1)S(1)} %get-tuple-element.37), channel_id=1, source_target_pairs={{0,6},{1,7},{2,4},{3,5},{4,2},{5,3},{6,0},{7,1},{8,14},{9,15},{10,... | collective-permute-start | bytes 98312 | tf_op jit(solution)/shard_map/ppermute | solution.py:45
  24.5 8.5 %collective-permute-start.10 = (bf16[8,2,128,128]{3,2,1,0:T(8,128)(2,1)S(1)}, bf16[8,2,128,128]{3,2,1,0:T(8,128)(2,1)S(1)}, u32[]{:S(2)}, u32[]{:S(2)}) collective-permute-start(bf16[8,2,128,128]{3,2,1,0:T(8,128)(2,1)S(1)} %copy-done.2), channel_id=1, source_target_pairs={{0,8},{8,0},{16,24},{24,16},{1,9},{9,1},{17,25},{25,17},{2,10},{10... | collective-permute-start | bytes 1572872 | tf_op jit(solution)/shard_map/ppermute | solution.py:45
  28.7 4.4 %collective-permute-start.11 = (bf16[8,2,128,128]{3,2,1,0:T(8,128)(2,1)S(1)}, bf16[8,2,128,128]{3,2,1,0:T(8,128)(2,1)S(1)}, u32[]{:S(2)}, u32[]{:S(2)}) collective-permute-start(bf16[8,2,128,128]{3,2,1,0:T(8,128)(2,1)S(1)} %copy-done.3), channel_id=1, source_target_pairs={{0,8},{8,0},{16,24},{24,16},{1,9},{9,1},{17,25},{25,17},{2,10},{10... | collective-permute-start | bytes 1572872 | tf_op jit(solution)/shard_map/ppermute | solution.py:45
  28.8 4.3 %collective-permute-start.13 = (bf16[8,2,128,128]{3,2,1,0:T(8,128)(2,1)S(1)}, bf16[8,2,128,128]{3,2,1,0:T(8,128)(2,1)S(1)}, u32[]{:S(2)}, u32[]{:S(2)}) collective-permute-start(bf16[8,2,128,128]{3,2,1,0:T(8,128)(2,1)S(1)} %collective-permute-done.12.refs_12_.refs_8_), channel_id=1, source_target_pairs={{0,8},{8,0},{16,24},{24,16},{1,9},{9,1},{17,25},{25,17},{2,10},{10... | collective-permute-start | bytes 1572872 | tf_op jit(solution)/shard_map/ppermute | solution.py:45
  30.6 4.9 %collective-permute-start.15 = (bf16[8,2,128,128]{3,2,1,0:T(8,128)(2,1)S(1)}, bf16[8,2,128,128]{3,2,1,0:T(8,128)(2,1)S(1)}, u32[]{:S(2)}, u32[]{:S(2)}) collective-permute-start(bf16[8,2,128,128]{3,2,1,0:T(8,128)(2,1)S(1)} %collective-permute-done.14.refs_6_), channel_id=1, source_target_pairs={{0,8},{8,0},{16,24},{24,16},{1,9},{9,1},{17,25},{25,17},{2,10},{10... | collective-permute-start | bytes 1572872 | tf_op jit(solution)/shard_map/ppermute | solution.py:45
  (1 other events, 0.7 us)

commit v7 on v6

--- a/solution.py
+++ b/solution.py
@@ -210,16 +210,18 @@
     return lax.dot_general(grads, wide(second_ref, i), NT, preferred_element_type=jnp.float32)
 
 
-def hidden_blocks(table_ref, owners, first_refs, second_refs, dact, normed_ref, act_ref, dpre_ref, mlp_ref, back_ref):
+def hidden_blocks(table_ref, owners, first_refs, second_refs, dact, pick, act_ref, dpre_ref, mlp_ref, back_ref, table_ready=None):
     blocks = first_refs[0].shape[0]
     steps = [(s, i) for s in range(len(owners)) for i in range(blocks)]
     for k, (s, i) in enumerate(steps):
-        rows, cols = places(table_ref, owners[s], blocks, i)
-        picked = jnp.concatenate([normed_ref[r] for r in rows], axis=1)
+        rows, cols = places(table_ref, owners[s], blocks, i) if table_ready is None else (None, None)
+        picked = pick(k, rows)
         pre = jnp.dot(picked, tall(first_refs[s], i), preferred_element_type=jnp.float32)
         act, slope = slope_terms(pre)
         act_ref[k] = act.astype(jnp.bfloat16)
         dpre_ref[k] = (dact(k, s, i, cols) * slope).astype(jnp.bfloat16)
+    if table_ready is not None:
+        table_ready()
     for k, (s, i) in enumerate(steps):
         rows, cols = places(table_ref, owners[s], blocks, i)
         forward = jnp.dot(act_ref[k], wide(second_refs[s], i), preferred_element_type=jnp.float32)
@@ -240,7 +242,7 @@
     proj_ref, tokens_ref, gain_ref, grad_ref = refs[:4]
     first_refs, second_refs = refs[4 : 4 + near], refs[4 + near : 4 + 3 * near]
     refs = refs[4 + 3 * near :]
-    mlp_ref, back_ref, unit_ref, rstd_ref, normed_ref, far_dact_ref, act_ref, dpre_ref, grads_ref = refs
+    mlp_ref, back_ref, unit_ref, rstd_ref, far_picked_ref, far_dact_ref, normed_ref, act_ref, dpre_ref, grads_ref = refs
     split_blocks(grad_ref, grads_ref)
     group = lax.rem(lax.axis_index("seq") // HEAD_BIT, QUADS)
     hidden = tokens_ref[0].astype(jnp.float32)
@@ -271,7 +273,7 @@
         first_refs,
         second_refs[:near],
         lambda k, s, i, cols: dact_of(grads_ref, second_refs[s], i, cols),
-        normed_ref,
+        lambda k, rows: jnp.concatenate([normed_ref[r] for r in rows], axis=1),
         act_ref,
         dpre_ref,
         mlp_ref,
@@ -279,7 +281,9 @@
     )
     for s in range(near):
         for i in range(blocks):
-            _, cols = places(table_ref, owners[near + s], blocks, i)
+            rows, cols = places(table_ref, owners[near + s], blocks, i)
+            picked = jnp.concatenate([normed_ref[r] for r in rows], axis=1)
+            far_picked_ref[s * blocks + i] = picked
             far_dact_ref[s * blocks + i] = dact_of(grads_ref, second_refs[near + s], i, cols)
 
 
@@ -295,12 +299,13 @@
             jax.ShapeDtypeStruct((width // BLK, rows, BLK), jnp.float32),
             jax.ShapeDtypeStruct((rows, width), jnp.float32),
             jax.ShapeDtypeStruct((rows, LANES), jnp.float32),
-            jax.ShapeDtypeStruct((width // BLK, rows, BLK), jnp.bfloat16),
+            jax.ShapeDtypeStruct((kept, rows, NNZ * BLK), jnp.bfloat16),
             jax.ShapeDtypeStruct((kept, rows, BLK), jnp.float32),
         ],
         in_specs=[vmem()] * (1 + len(args)),
         out_specs=[vmem()] * 6,
-        scratch_shapes=[pltpu.VMEM((kept, rows, BLK), jnp.bfloat16)] * 2
+        scratch_shapes=[pltpu.VMEM((width // BLK, rows, BLK), jnp.bfloat16)]
+        + [pltpu.VMEM((kept, rows, BLK), jnp.bfloat16)] * 2
         + [pltpu.VMEM((width // BLK, rows, BLK), jnp.bfloat16)]
         + [pltpu.SMEM(table.shape, jnp.int32), pltpu.SemaphoreType.DMA],
         compiler_params=pltpu.CompilerParams(vmem_limit_bytes=VMEM_LIMIT),
@@ -312,12 +317,11 @@
     refs, (table_ref, table_sem) = refs[:-2], refs[-2:]
     table_copy = pltpu.make_async_copy(table_in_ref, table_ref, table_sem)
     table_copy.start()
-    mlp_in_ref, back_in_ref, unit_ref, rstd_ref, normed_ref, dact_ref = refs[:6]
+    mlp_in_ref, back_in_ref, unit_ref, rstd_ref, picked_ref, dact_ref = refs[:6]
     first_refs, second_refs = refs[6 : 6 + near], refs[6 + near : 6 + 2 * near]
     out_ref, grad_out_ref, mlp_ref, back_ref, act_ref, dpre_ref = refs[6 + 2 * near :]
     mlp_ref[...] = mlp_in_ref[...]
     back_ref[...] = back_in_ref[...]
-    table_copy.wait()
     me = lax.axis_index("grp")
     hidden_blocks(
         table_ref,
@@ -325,11 +329,12 @@
         first_refs,
         second_refs,
         lambda k, s, i, cols: dact_ref[k],
-        normed_ref,
+        lambda k, rows: picked_ref[k],
         act_ref,
         dpre_ref,
         mlp_ref,
         back_ref,
+        table_copy.wait,
     )
     width_blocks = range(mlp_ref.shape[0])
     for d in width_blocks:

time: 38.6 us -> 38.4 us (level)
  no operation moved by 1% of the time
where the time goes in v7:
time: 38.4 us; the launch traced here: 38.3 us
  starting transfers between devices  22.3 us (58%)
  Pallas kernels  8.8 us (23%)
  waiting for transfers between devices  5.04 us (13%)
  local copies, waits for them, and re-layouts  1.37 us (4%)
  between operations  0.76 us (2%)
    ppermute x16, starting transfers between devices, exchange(): return lax.ppermute(x, axis, [(i, i ^ flip) for i in range(size)])  22.3 us
    ppermute x16, waiting for transfers between devices, exchange(): return lax.ppermute(x, axis, [(i, i ^ flip) for i in range(size)])  5.04 us
    pallas_call x1, Pallas kernels, mlp_far(): pl.pallas_call(functools.partial(far_kernel, near), out_shape=[jax.ShapeD...  2.7 us
    pallas_call x1, Pallas kernels, mlp_near(): pl.pallas_call(functools.partial(near_kernel, near), out_shape=[jax.Shape...  2.45 us
    pallas_call x1, Pallas kernels, attend_rest(): pl.pallas_call(functools.partial(attend_kernel, False, True, len(rest) //...  1.36 us
    unnamed x18, local copies, waits for them, and re-layouts  1.35 us
    pallas_call x1, Pallas kernels, attend_own(): pl.pallas_call(functools.partial(attend_kernel, True, False, 1), out_shap...  1.15 us
    pallas_call x1, Pallas kernels, pack(): pl.pallas_call(functools.partial(pack_kernel, seq_size), out_shape=[jax.S...  1.14 us
  transfers between devices with their start and end apart: 16, of which 3 were waited for; matrix products, arithmetic and copies ran while one was open for 0% of the time, Pallas kernels for 13%

profile of v7, /device:TPU:1, one launch (start us, length us, event | category | flops | bytes accessed | tf_op | source)
XLA Modules:
  0.0 38.3 jit_solution(14721282607958070307)
XLA Ops:
  0.6 0.6 %copy-done.5 = s32[1,1,8]{2,1,0:T(1,128)S(1)} copy-done((s32[1,1,8]{2,1,0:T(1,128)S(1)}, s32[1,1,8]{2,1,0:T(1,128)}, u32[]{:S(2)}) %copy-start.5) | copy-done | bytes 56
  1.3 1.1 %pack.1 = (bf16[400,128]{1,0:T(8,128)(2,1)S(1)}, bf16[400,128]{1,0:T(8,128)(2,1)S(1)}, bf16[400,128]{1,0:T(8,128)(2,1)S(1)}, bf16[400,128]{1,0:T(8,128)(2,1)S(1)}) custom-call(bf16[1,128,512]{2,1,0:T(8,128)(2,1)} %q_ref.1, bf16[1,128,512]{2,1,0:T(8,128)(2,1)} %k_ref.1, bf16[1,128,512]{2,1,0:T(8,128)(2,1)} %v_ref.1, s32[1,1,8]{2,1,0:T(1,128)S(1)} %copy-done.5), custom_call_target="tpu_custom_call" | custom-call | tf_op jit(solution)/shard_map/pack/pallas_call | solution.py:84
  2.4 2.2 %collective-permute-start = (bf16[400,128]{1,0:T(8,128)(2,1)S(1)}, bf16[400,128]{1,0:T(8,128)(2,1)S(1)}, u32[]{:S(2)}, u32[]{:S(2)}) collective-permute-start(bf16[400,128]{1,0:T(8,128)(2,1)S(1)} %get-tuple-element.26), channel_id=1, source_target_pairs={{0,2},{1,3},{2,0},{3,1},{4,6},{5,7},{6,4},{7,5},{8,10},{9,11},{10,... | collective-permute-start | bytes 307208 | tf_op jit(solution)/shard_map/ppermute | solution.py:45
  4.6 2.3 %collective-permute-start.1 = (bf16[400,128]{1,0:T(8,128)(2,1)S(1)}, bf16[400,128]{1,0:T(8,128)(2,1)S(1)}, u32[]{:S(2)}, u32[]{:S(2)}) collective-permute-start(bf16[400,128]{1,0:T(8,128)(2,1)S(1)} %get-tuple-element.27), channel_id=1, source_target_pairs={{0,4},{1,5},{2,6},{3,7},{4,0},{5,1},{6,2},{7,3},{8,12},{9,13},{10,... | collective-permute-start | bytes 307208 | tf_op jit(solution)/shard_map/ppermute | solution.py:45
  6.9 1.2 %collective-permute-start.12 = (bf16[8,2,128,128]{3,2,1,0:T(8,128)(2,1)}, bf16[8,2,128,128]{3,2,1,0:T(8,128)(2,1)S(1)}, u32[]{:S(2)}, u32[]{:S(2)}) collective-permute-start(bf16[8,2,128,128]{3,2,1,0:T(8,128)(2,1)} %refs_10_), channel_id=1, source_target_pairs={{0,16},{8,24},{16,0},{24,8},{1,17},{9,25},{17,1},{25,9},{2,18},{10... | collective-permute-start | bytes 1572872 | tf_op jit(solution)/shard_map/ppermute | solution.py:45
  8.4 1.3 %collective-permute-start.3 = (bf16[256,128]{1,0:T(8,128)(2,1)S(1)}, bf16[256,128]{1,0:T(8,128)(2,1)S(1)}, u32[]{:S(2)}, u32[]{:S(2)}) collective-permute-start(bf16[256,128]{1,0:T(8,128)(2,1)S(1)} %slice.12), channel_id=1, source_target_pairs={{0,1},{1,0},{2,3},{3,2},{4,5},{5,4},{6,7},{7,6},{8,9},{9,8},{10,11... | collective-permute-start | bytes 196616 | tf_op jit(solution)/shard_map/ppermute | solution.py:45
  9.7 0.8 %collective-permute-start.4 = (bf16[256,128]{1,0:T(8,128)(2,1)S(1)}, bf16[256,128]{1,0:T(8,128)(2,1)S(1)}, u32[]{:S(2)}, u32[]{:S(2)}) collective-permute-start(bf16[256,128]{1,0:T(8,128)(2,1)S(1)} %slice.16), channel_id=1, source_target_pairs={{0,1},{1,0},{2,3},{3,2},{4,5},{5,4},{6,7},{7,6},{8,9},{9,8},{10,11... | collective-permute-start | bytes 196616 | tf_op jit(solution)/shard_map/ppermute | solution.py:45
  10.5 3.2 %collective-permute-done.2.refs_3_ = bf16[400,128]{1,0:T(8,128)(2,1)S(1)} collective-permute-done((bf16[400,128]{1,0:T(8,128)(2,1)S(1)}, bf16[400,128]{1,0:T(8,128)(2,1)S(1)}, u32[]{:S(2)}, u32[]{:S(2)}) %collective-permute-start.2) | collective-permute-done | bytes 102432 | tf_op jit(solution)/shard_map/ppermute | solution.py:45
  13.7 1.2 %collective-permute-start.5 = (bf16[256,128]{1,0:T(8,128)(2,1)S(1)}, bf16[256,128]{1,0:T(8,128)(2,1)S(1)}, u32[]{:S(2)}, u32[]{:S(2)}) collective-permute-start(bf16[256,128]{1,0:T(8,128)(2,1)S(1)} %slice.17), channel_id=1, source_target_pairs={{0,1},{1,0},{2,3},{3,2},{4,5},{5,4},{6,7},{7,6},{8,9},{9,8},{10,11... | collective-permute-start | bytes 196616 | tf_op jit(solution)/shard_map/ppermute | solution.py:45
  14.9 0.3 collective-permute-start.6
  15.3 0.3 copy-done.8
  15.6 0.3 copy-done.7
  15.9 1.1 %attend_own.1 = (f32[4,256,128]{2,1,0:T(8,128)S(1)}, f32[4,256,128]{2,1,0:T(8,128)S(1)}, f32[4,256,128]{2,1,0:T(8,128)S(1)}, s32[4,32]{1,0:T(4,128)S(1)}, f32[1,1024]{1,0:T(1,128)S(1)}) custom-call(bf16[400,128]{1,0:T(8,128)(2,1)S(1)} %get-tuple-element.25.refs_0_, bf16[400,128]{1,0:T(8,128)(2,1)S(1)} %collective-permute-done.refs_1_, ...), custom_call_target="tpu_custom_call" | custom-call | flops 2150000128 | tf_op jit(solution)/shard_map/attend_own/pallas_call | solution.py:151
  17.1 1.3 %collective-permute-done.6.refs_7_ = bf16[256,128]{1,0:T(8,128)(2,1)S(1)} collective-permute-done((bf16[256,128]{1,0:T(8,128)(2,1)S(1)}, bf16[256,128]{1,0:T(8,128)(2,1)S(1)}, u32[]{:S(2)}, u32[]{:S(2)}) %collective-permute-start.6) | collective-permute-done | bytes 65568 | tf_op jit(solution)/shard_map/ppermute | solution.py:45
  18.4 1.4 %attend_rest.1 = (bf16[128,128]{1,0:T(8,128)(2,1)S(1)}, bf16[128,128]{1,0:T(8,128)(2,1)S(1)}, bf16[128,128]{1,0:T(8,128)(2,1)S(1)}, bf16[128,128]{1,0:T(8,128)(2,1)S(1)}) custom-call(bf16[400,128]{1,0:T(8,128)(2,1)S(1)} %get-tuple-element.25.refs_0_, bf16[400,128]{1,0:T(8,128)(2,1)S(1)} %collective-permute-done.refs_1_, ...), custom_call_target="tpu_custom_call" | custom-call | flops 2150000128 | tf_op jit(solution)/shard_map/attend_rest/pallas_call | solution.py:167
  19.8 2.6 %collective-permute-start.7 = (bf16[128,128]{1,0:T(8,128)(2,1)S(1)}, bf16[128,128]{1,0:T(8,128)(2,1)S(1)}, u32[]{:S(2)}, u32[]{:S(2)}) collective-permute-start(bf16[128,128]{1,0:T(8,128)(2,1)S(1)} %get-tuple-element.35), channel_id=1, source_target_pairs={{0,2},{1,3},{2,0},{3,1},{4,6},{5,7},{6,4},{7,5},{8,10},{9,11},{10,... | collective-permute-start | bytes 98312 | tf_op jit(solution)/shard_map/ppermute | solution.py:45
  22.4 1.0 %collective-permute-start.8 = (bf16[128,128]{1,0:T(8,128)(2,1)S(1)}, bf16[128,128]{1,0:T(8,128)(2,1)S(1)}, u32[]{:S(2)}, u32[]{:S(2)}) collective-permute-start(bf16[128,128]{1,0:T(8,128)(2,1)S(1)} %get-tuple-element.36), channel_id=1, source_target_pairs={{0,4},{1,5},{2,6},{3,7},{4,0},{5,1},{6,2},{7,3},{8,12},{9,13},{10,... | collective-permute-start | bytes 98312 | tf_op jit(solution)/shard_map/ppermute | solution.py:45
  23.4 1.1 %collective-permute-start.9 = (bf16[128,128]{1,0:T(8,128)(2,1)S(1)}, bf16[128,128]{1,0:T(8,128)(2,1)S(1)}, u32[]{:S(2)}, u32[]{:S(2)}) collective-permute-start(bf16[128,128]{1,0:T(8,128)(2,1)S(1)} %get-tuple-element.37), channel_id=1, source_target_pairs={{0,6},{1,7},{2,4},{3,5},{4,2},{5,3},{6,0},{7,1},{8,14},{9,15},{10,... | collective-permute-start | bytes 98312 | tf_op jit(solution)/shard_map/ppermute | solution.py:45
  24.5 4.2 %collective-permute-start.10 = (bf16[8,2,128,128]{3,2,1,0:T(8,128)(2,1)S(1)}, bf16[8,2,128,128]{3,2,1,0:T(8,128)(2,1)S(1)}, u32[]{:S(2)}, u32[]{:S(2)}) collective-permute-start(bf16[8,2,128,128]{3,2,1,0:T(8,128)(2,1)S(1)} %copy-done.2), channel_id=1, source_target_pairs={{0,8},{8,0},{16,24},{24,16},{1,9},{9,1},{17,25},{25,17},{2,10},{10... | collective-permute-start | bytes 1572872 | tf_op jit(solution)/shard_map/ppermute | solution.py:45
  28.8 1.3 %collective-permute-start.13 = (bf16[8,2,128,128]{3,2,1,0:T(8,128)(2,1)S(1)}, bf16[8,2,128,128]{3,2,1,0:T(8,128)(2,1)S(1)}, u32[]{:S(2)}, u32[]{:S(2)}) collective-permute-start(bf16[8,2,128,128]{3,2,1,0:T(8,128)(2,1)S(1)} %collective-permute-done.12.refs_12_.refs_8_), channel_id=1, source_target_pairs={{0,8},{8,0},{16,24},{24,16},{1,9},{9,1},{17,25},{25,17},{2,10},{10... | collective-permute-start | bytes 1572872 | tf_op jit(solution)/shard_map/ppermute | solution.py:45
  30.1 0.5 %collective-permute-done.14.refs_6_ = bf16[8,2,128,128]{3,2,1,0:T(8,128)(2,1)S(1)} collective-permute-done((bf16[8,2,128,128]{3,2,1,0:T(8,128)(2,1)}, bf16[8,2,128,128]{3,2,1,0:T(8,128)(2,1)S(1)}, u32[]{:S(2)}, u32[]{:S(2)}) %collective-permute-start.14) | collective-permute-done | bytes 524320 | tf_op jit(solution)/shard_map/ppermute | solution.py:45
  30.6 2.5 %collective-permute-start.15 = (bf16[8,2,128,128]{3,2,1,0:T(8,128)(2,1)S(1)}, bf16[8,2,128,128]{3,2,1,0:T(8,128)(2,1)S(1)}, u32[]{:S(2)}, u32[]{:S(2)}) collective-permute-start(bf16[8,2,128,128]{3,2,1,0:T(8,128)(2,1)S(1)} %collective-permute-done.14.refs_6_), channel_id=1, source_target_pairs={{0,8},{8,0},{16,24},{24,16},{1,9},{9,1},{17,25},{25,17},{2,10},{10... | collective-permute-start | bytes 1572872 | tf_op jit(solution)/shard_map/ppermute | solution.py:45
  33.1 2.5 %mlp_near.1 = (f32[8,128,128]{2,1,0:T(8,128)S(1)}, f32[8,128,128]{2,1,0:T(8,128)S(1)}, f32[128,1024]{1,0:T(8,128)S(1)}, f32[128,128]{1,0:T(8,128)S(1)}, bf16[16,...) custom-call(s32[4,32]{1,0:T(4,128)S(1)} %get-tuple-element.29.table_in_ref, ...), custom_call_target="tpu_custom_call" | custom-call | tf_op jit(solution)/shard_map/mlp_near/pallas_call | solution.py:295
  35.6 2.7 %mlp_far.1 = (bf16[1,128,1024]{2,1,0:T(8,128)(2,1)}, bf16[1,128,1024]{2,1,0:T(8,128)(2,1)}) custom-call(s32[4,32]{1,0:T(4,128)S(1)} %get-tuple-element.29.table_in_ref, f32[1,1024]{1,0:T(1,128)S(1)} %get-tuple-element.30.refs_6_.gain_ref, bf16[1,128,1024]{2,1,0:T(8,128)(2,1)S(1)} %copy-done.1, f32[8,128,128]{2,1,0:T(8,128)S(1)} %get-tuple-element.41.refs_0_, ...), custom_call_target="tpu_custom_call" | custom-call | tf_op jit(solution)/shard_map/mlp_far/pallas_call | solution.py:358
  (35 shorter events, 0.4 us)
Async XLA Ops:
  2.4 6.0 %collective-permute-start = (bf16[400,128]{1,0:T(8,128)(2,1)S(1)}, bf16[400,128]{1,0:T(8,128)(2,1)S(1)}, u32[]{:S(2)}, u32[]{:S(2)}) collective-permute-start(bf16[400,128]{1,0:T(8,128)(2,1)S(1)} %get-tuple-element.26), channel_id=1, source_target_pairs={{0,2},{1,3},{2,0},{3,1},{4,6},{5,7},{6,4},{7,5},{8,10},{9,11},{10,... | collective-permute-start | bytes 307208 | tf_op jit(solution)/shard_map/ppermute | solution.py:45
  4.6 5.1 %collective-permute-start.1 = (bf16[400,128]{1,0:T(8,128)(2,1)S(1)}, bf16[400,128]{1,0:T(8,128)(2,1)S(1)}, u32[]{:S(2)}, u32[]{:S(2)}) collective-permute-start(bf16[400,128]{1,0:T(8,128)(2,1)S(1)} %get-tuple-element.27), channel_id=1, source_target_pairs={{0,4},{1,5},{2,6},{3,7},{4,0},{5,1},{6,2},{7,3},{8,12},{9,13},{10,... | collective-permute-start | bytes 307208 | tf_op jit(solution)/shard_map/ppermute | solution.py:45
  6.9 6.8 %collective-permute-start.2 = (bf16[400,128]{1,0:T(8,128)(2,1)S(1)}, bf16[400,128]{1,0:T(8,128)(2,1)S(1)}, u32[]{:S(2)}, u32[]{:S(2)}) collective-permute-start(bf16[400,128]{1,0:T(8,128)(2,1)S(1)} %get-tuple-element.28), channel_id=1, source_target_pairs={{0,6},{1,7},{2,4},{3,5},{4,2},{5,3},{6,0},{7,1},{8,14},{9,15},{10,... | collective-permute-start | bytes 307208 | tf_op jit(solution)/shard_map/ppermute | solution.py:45
  6.9 17.6 %collective-permute-start.12 = (bf16[8,2,128,128]{3,2,1,0:T(8,128)(2,1)}, bf16[8,2,128,128]{3,2,1,0:T(8,128)(2,1)S(1)}, u32[]{:S(2)}, u32[]{:S(2)}) collective-permute-start(bf16[8,2,128,128]{3,2,1,0:T(8,128)(2,1)} %refs_10_), channel_id=1, source_target_pairs={{0,16},{8,24},{16,0},{24,8},{1,17},{9,25},{17,1},{25,9},{2,18},{10... | collective-permute-start | bytes 1572872 | tf_op jit(solution)/shard_map/ppermute | solution.py:45
  8.2 22.4 %collective-permute-start.14 = (bf16[8,2,128,128]{3,2,1,0:T(8,128)(2,1)}, bf16[8,2,128,128]{3,2,1,0:T(8,128)(2,1)S(1)}, u32[]{:S(2)}, u32[]{:S(2)}) collective-permute-start(bf16[8,2,128,128]{3,2,1,0:T(8,128)(2,1)} %refs_8_), channel_id=1, source_target_pairs={{0,16},{8,24},{16,0},{24,8},{1,17},{9,25},{17,1},{25,9},{2,18},{10... | collective-permute-start | bytes 1572872 | tf_op jit(solution)/shard_map/ppermute | solution.py:45
  8.4 6.5 %collective-permute-start.3 = (bf16[256,128]{1,0:T(8,128)(2,1)S(1)}, bf16[256,128]{1,0:T(8,128)(2,1)S(1)}, u32[]{:S(2)}, u32[]{:S(2)}) collective-permute-start(bf16[256,128]{1,0:T(8,128)(2,1)S(1)} %slice.12), channel_id=1, source_target_pairs={{0,1},{1,0},{2,3},{3,2},{4,5},{5,4},{6,7},{7,6},{8,9},{9,8},{10,11... | collective-permute-start | bytes 196616 | tf_op jit(solution)/shard_map/ppermute | solution.py:45
  9.7 7.4 %collective-permute-start.4 = (bf16[256,128]{1,0:T(8,128)(2,1)S(1)}, bf16[256,128]{1,0:T(8,128)(2,1)S(1)}, u32[]{:S(2)}, u32[]{:S(2)}) collective-permute-start(bf16[256,128]{1,0:T(8,128)(2,1)S(1)} %slice.16), channel_id=1, source_target_pairs={{0,1},{1,0},{2,3},{3,2},{4,5},{5,4},{6,7},{7,6},{8,9},{9,8},{10,11... | collective-permute-start | bytes 196616 | tf_op jit(solution)/shard_map/ppermute | solution.py:45
  13.7 3.4 %collective-permute-start.5 = (bf16[256,128]{1,0:T(8,128)(2,1)S(1)}, bf16[256,128]{1,0:T(8,128)(2,1)S(1)}, u32[]{:S(2)}, u32[]{:S(2)}) collective-permute-start(bf16[256,128]{1,0:T(8,128)(2,1)S(1)} %slice.17), channel_id=1, source_target_pairs={{0,1},{1,0},{2,3},{3,2},{4,5},{5,4},{6,7},{7,6},{8,9},{9,8},{10,11... | collective-permute-start | bytes 196616 | tf_op jit(solution)/shard_map/ppermute | solution.py:45
  14.9 0.7 %copy-start.8 = (s32[32,2]{0,1:T(2,128)S(1)}, s32[32,2]{0,1:T(2,128)}, u32[]{:S(2)}) copy-start(s32[32,2]{0,1:T(2,128)} %param.22) | copy-start | bytes 772
  14.9 0.7 %copy-start.6 = (f32[1024]{0:T(1024)S(1)}, f32[1024]{0:T(1024)}, u32[]{:S(2)}) copy-start(f32[1024]{0:T(1024)} %param.18) | copy-start | bytes 12292
  14.9 3.5 %collective-permute-start.6 = (bf16[256,128]{1,0:T(8,128)(2,1)S(1)}, bf16[256,128]{1,0:T(8,128)(2,1)S(1)}, u32[]{:S(2)}, u32[]{:S(2)}) collective-permute-start(bf16[256,128]{1,0:T(8,128)(2,1)S(1)} %slice.18), channel_id=1, source_target_pairs={{0,1},{1,0},{2,3},{3,2},{4,5},{5,4},{6,7},{7,6},{8,9},{9,8},{10,11... | collective-permute-start | bytes 196616 | tf_op jit(solution)/shard_map/ppermute | solution.py:45
  15.3 0.7 %copy-start.7 = (s32[32,2]{0,1:T(2,128)S(1)}, s32[32,2]{0,1:T(2,128)}, u32[]{:S(2)}) copy-start(s32[32,2]{0,1:T(2,128)} %param.20) | copy-start | bytes 772
  18.4 6.1 %copy-start.2 = (bf16[8,2,128,128]{3,2,1,0:T(8,128)(2,1)S(1)}, bf16[8,2,128,128]{3,2,1,0:T(8,128)(2,1)}, u32[]{:S(2)}) copy-start(bf16[8,2,128,128]{3,2,1,0:T(8,128)(2,1)} %refs_8_) | copy-start | bytes 1572868
  18.4 10.3 %copy-start.3 = (bf16[8,2,128,128]{3,2,1,0:T(8,128)(2,1)S(1)}, bf16[8,2,128,128]{3,2,1,0:T(8,128)(2,1)}, u32[]{:S(2)}) copy-start(bf16[8,2,128,128]{3,2,1,0:T(8,128)(2,1)} %refs_10_) | copy-start | bytes 1572868
  18.4 14.7 %copy-start = (bf16[512,1024]{1,0:T(8,128)(2,1)S(1)}, bf16[512,1024]{1,0:T(8,128)(2,1)}, u32[]{:S(2)}) copy-start(bf16[512,1024]{1,0:T(8,128)(2,1)} %refs_4_.1) | copy-start | bytes 3145732
  18.4 14.7 %copy-start.1 = (bf16[1,128,1024]{2,1,0:T(8,128)(2,1)S(1)}, bf16[1,128,1024]{2,1,0:T(8,128)(2,1)}, u32[]{:S(2)}) copy-start(bf16[1,128,1024]{2,1,0:T(8,128)(2,1)} %grad_ref.1) | copy-start | bytes 786436
  18.4 14.7 %copy-start.4 = (bf16[1,128,1024]{2,1,0:T(8,128)(2,1)S(1)}, bf16[1,128,1024]{2,1,0:T(8,128)(2,1)}, u32[]{:S(2)}) copy-start(bf16[1,128,1024]{2,1,0:T(8,128)(2,1)} %refs_5_.1) | copy-start | bytes 786436
  19.8 8.9 %collective-permute-start.7 = (bf16[128,128]{1,0:T(8,128)(2,1)S(1)}, bf16[128,128]{1,0:T(8,128)(2,1)S(1)}, u32[]{:S(2)}, u32[]{:S(2)}) collective-permute-start(bf16[128,128]{1,0:T(8,128)(2,1)S(1)} %get-tuple-element.35), channel_id=1, source_target_pairs={{0,2},{1,3},{2,0},{3,1},{4,6},{5,7},{6,4},{7,5},{8,10},{9,11},{10,... | collective-permute-start | bytes 98312 | tf_op jit(solution)/shard_map/ppermute | solution.py:45
  22.4 6.4 %collective-permute-start.8 = (bf16[128,128]{1,0:T(8,128)(2,1)S(1)}, bf16[128,128]{1,0:T(8,128)(2,1)S(1)}, u32[]{:S(2)}, u32[]{:S(2)}) collective-permute-start(bf16[128,128]{1,0:T(8,128)(2,1)S(1)} %get-tuple-element.36), channel_id=1, source_target_pairs={{0,4},{1,5},{2,6},{3,7},{4,0},{5,1},{6,2},{7,3},{8,12},{9,13},{10,... | collective-permute-start | bytes 98312 | tf_op jit(solution)/shard_map/ppermute | solution.py:45
  23.4 6.7 %collective-permute-start.9 = (bf16[128,128]{1,0:T(8,128)(2,1)S(1)}, bf16[128,128]{1,0:T(8,128)(2,1)S(1)}, u32[]{:S(2)}, u32[]{:S(2)}) collective-permute-start(bf16[128,128]{1,0:T(8,128)(2,1)S(1)} %get-tuple-element.37), channel_id=1, source_target_pairs={{0,6},{1,7},{2,4},{3,5},{4,2},{5,3},{6,0},{7,1},{8,14},{9,15},{10,... | collective-permute-start | bytes 98312 | tf_op jit(solution)/shard_map/ppermute | solution.py:45
  24.5 8.5 %collective-permute-start.10 = (bf16[8,2,128,128]{3,2,1,0:T(8,128)(2,1)S(1)}, bf16[8,2,128,128]{3,2,1,0:T(8,128)(2,1)S(1)}, u32[]{:S(2)}, u32[]{:S(2)}) collective-permute-start(bf16[8,2,128,128]{3,2,1,0:T(8,128)(2,1)S(1)} %copy-done.2), channel_id=1, source_target_pairs={{0,8},{8,0},{16,24},{24,16},{1,9},{9,1},{17,25},{25,17},{2,10},{10... | collective-permute-start | bytes 1572872 | tf_op jit(solution)/shard_map/ppermute | solution.py:45
  28.7 4.4 %collective-permute-start.11 = (bf16[8,2,128,128]{3,2,1,0:T(8,128)(2,1)S(1)}, bf16[8,2,128,128]{3,2,1,0:T(8,128)(2,1)S(1)}, u32[]{:S(2)}, u32[]{:S(2)}) collective-permute-start(bf16[8,2,128,128]{3,2,1,0:T(8,128)(2,1)S(1)} %copy-done.3), channel_id=1, source_target_pairs={{0,8},{8,0},{16,24},{24,16},{1,9},{9,1},{17,25},{25,17},{2,10},{10... | collective-permute-start | bytes 1572872 | tf_op jit(solution)/shard_map/ppermute | solution.py:45
  28.8 4.3 %collective-permute-start.13 = (bf16[8,2,128,128]{3,2,1,0:T(8,128)(2,1)S(1)}, bf16[8,2,128,128]{3,2,1,0:T(8,128)(2,1)S(1)}, u32[]{:S(2)}, u32[]{:S(2)}) collective-permute-start(bf16[8,2,128,128]{3,2,1,0:T(8,128)(2,1)S(1)} %collective-permute-done.12.refs_12_.refs_8_), channel_id=1, source_target_pairs={{0,8},{8,0},{16,24},{24,16},{1,9},{9,1},{17,25},{25,17},{2,10},{10... | collective-permute-start | bytes 1572872 | tf_op jit(solution)/shard_map/ppermute | solution.py:45
  30.6 5.0 %collective-permute-start.15 = (bf16[8,2,128,128]{3,2,1,0:T(8,128)(2,1)S(1)}, bf16[8,2,128,128]{3,2,1,0:T(8,128)(2,1)S(1)}, u32[]{:S(2)}, u32[]{:S(2)}) collective-permute-start(bf16[8,2,128,128]{3,2,1,0:T(8,128)(2,1)S(1)} %collective-permute-done.14.refs_6_), channel_id=1, source_target_pairs={{0,8},{8,0},{16,24},{24,16},{1,9},{9,1},{17,25},{25,17},{2,10},{10... | collective-permute-start | bytes 1572872 | tf_op jit(solution)/shard_map/ppermute | solution.py:45
  (1 other events, 0.7 us)

commit v8 on v7

--- a/solution.py
+++ b/solution.py
@@ -246,12 +246,12 @@
     split_blocks(grad_ref, grads_ref)
     group = lax.rem(lax.axis_index("seq") // HEAD_BIT, QUADS)
     hidden = tokens_ref[0].astype(jnp.float32)
-    for s in range(QUADS):
-        hidden = hidden + jnp.dot(
-            attn_refs[s][...],
-            proj_ref[block_of(lax.bitwise_xor(group, s)), :],
-            preferred_element_type=jnp.float32,
-        )
+    places_of = [block_of(lax.bitwise_xor(group, s)) for s in range(QUADS)]
+    hidden = hidden + jnp.dot(
+        jnp.concatenate([ref[...] for ref in attn_refs], axis=1),
+        jnp.concatenate([proj_ref[place, :] for place in places_of], axis=0),
+        preferred_element_type=jnp.float32,
+    )
     mean = jnp.mean(hidden, axis=1, keepdims=True)
     centred = hidden - mean
     rstd = lax.rsqrt(jnp.mean(centred * centred, axis=1, keepdims=True) + 1e-06)

time: 38.4 us -> 38.4 us (level)
  no operation moved by 1% of the time
where the time goes in v8:
time: 38.4 us; the launch traced here: 38.3 us
  starting transfers between devices  22.3 us (58%)
  Pallas kernels  8.79 us (23%)
  waiting for transfers between devices  5.04 us (13%)
  local copies, waits for them, and re-layouts  1.37 us (4%)
  between operations  0.76 us (2%)
    ppermute x16, starting transfers between devices, exchange(): return lax.ppermute(x, axis, [(i, i ^ flip) for i in range(size)])  22.3 us
    ppermute x16, waiting for transfers between devices, exchange(): return lax.ppermute(x, axis, [(i, i ^ flip) for i in range(size)])  5.04 us
    pallas_call x1, Pallas kernels, mlp_far(): pl.pallas_call(functools.partial(far_kernel, near), out_shape=[jax.ShapeD...  2.7 us
    pallas_call x1, Pallas kernels, mlp_near(): pl.pallas_call(functools.partial(near_kernel, near), out_shape=[jax.Shape...  2.44 us
    pallas_call x1, Pallas kernels, attend_rest(): pl.pallas_call(functools.partial(attend_kernel, False, True, len(rest) //...  1.36 us
    unnamed x18, local copies, waits for them, and re-layouts  1.35 us
    pallas_call x1, Pallas kernels, attend_own(): pl.pallas_call(functools.partial(attend_kernel, True, False, 1), out_shap...  1.15 us
    pallas_call x1, Pallas kernels, pack(): pl.pallas_call(functools.partial(pack_kernel, seq_size), out_shape=[jax.S...  1.14 us
  transfers between devices with their start and end apart: 16, of which 3 were waited for; matrix products, arithmetic and copies ran while one was open for 0% of the time, Pallas kernels for 13%

profile of v8, /device:TPU:1, one launch (start us, length us, event | category | flops | bytes accessed | tf_op | source)
XLA Modules:
  0.0 38.3 jit_solution(6726042464355721011)
XLA Ops:
  0.6 0.6 %copy-done.5 = s32[1,1,8]{2,1,0:T(1,128)S(1)} copy-done((s32[1,1,8]{2,1,0:T(1,128)S(1)}, s32[1,1,8]{2,1,0:T(1,128)}, u32[]{:S(2)}) %copy-start.5) | copy-done | bytes 56
  1.3 1.1 %pack.1 = (bf16[400,128]{1,0:T(8,128)(2,1)S(1)}, bf16[400,128]{1,0:T(8,128)(2,1)S(1)}, bf16[400,128]{1,0:T(8,128)(2,1)S(1)}, bf16[400,128]{1,0:T(8,128)(2,1)S(1)}) custom-call(bf16[1,128,512]{2,1,0:T(8,128)(2,1)} %q_ref.1, bf16[1,128,512]{2,1,0:T(8,128)(2,1)} %k_ref.1, bf16[1,128,512]{2,1,0:T(8,128)(2,1)} %v_ref.1, s32[1,1,8]{2,1,0:T(1,128)S(1)} %copy-done.5), custom_call_target="tpu_custom_call" | custom-call | tf_op jit(solution)/shard_map/pack/pallas_call | solution.py:84
  2.4 2.2 %collective-permute-start = (bf16[400,128]{1,0:T(8,128)(2,1)S(1)}, bf16[400,128]{1,0:T(8,128)(2,1)S(1)}, u32[]{:S(2)}, u32[]{:S(2)}) collective-permute-start(bf16[400,128]{1,0:T(8,128)(2,1)S(1)} %get-tuple-element.26), channel_id=1, source_target_pairs={{0,2},{1,3},{2,0},{3,1},{4,6},{5,7},{6,4},{7,5},{8,10},{9,11},{10,... | collective-permute-start | bytes 307208 | tf_op jit(solution)/shard_map/ppermute | solution.py:45
  4.6 2.3 %collective-permute-start.1 = (bf16[400,128]{1,0:T(8,128)(2,1)S(1)}, bf16[400,128]{1,0:T(8,128)(2,1)S(1)}, u32[]{:S(2)}, u32[]{:S(2)}) collective-permute-start(bf16[400,128]{1,0:T(8,128)(2,1)S(1)} %get-tuple-element.27), channel_id=1, source_target_pairs={{0,4},{1,5},{2,6},{3,7},{4,0},{5,1},{6,2},{7,3},{8,12},{9,13},{10,... | collective-permute-start | bytes 307208 | tf_op jit(solution)/shard_map/ppermute | solution.py:45
  6.9 1.2 %collective-permute-start.12 = (bf16[8,2,128,128]{3,2,1,0:T(8,128)(2,1)}, bf16[8,2,128,128]{3,2,1,0:T(8,128)(2,1)S(1)}, u32[]{:S(2)}, u32[]{:S(2)}) collective-permute-start(bf16[8,2,128,128]{3,2,1,0:T(8,128)(2,1)} %refs_10_), channel_id=1, source_target_pairs={{0,16},{8,24},{16,0},{24,8},{1,17},{9,25},{17,1},{25,9},{2,18},{10... | collective-permute-start | bytes 1572872 | tf_op jit(solution)/shard_map/ppermute | solution.py:45
  8.4 1.3 %collective-permute-start.3 = (bf16[256,128]{1,0:T(8,128)(2,1)S(1)}, bf16[256,128]{1,0:T(8,128)(2,1)S(1)}, u32[]{:S(2)}, u32[]{:S(2)}) collective-permute-start(bf16[256,128]{1,0:T(8,128)(2,1)S(1)} %slice.12), channel_id=1, source_target_pairs={{0,1},{1,0},{2,3},{3,2},{4,5},{5,4},{6,7},{7,6},{8,9},{9,8},{10,11... | collective-permute-start | bytes 196616 | tf_op jit(solution)/shard_map/ppermute | solution.py:45
  9.7 0.8 %collective-permute-start.4 = (bf16[256,128]{1,0:T(8,128)(2,1)S(1)}, bf16[256,128]{1,0:T(8,128)(2,1)S(1)}, u32[]{:S(2)}, u32[]{:S(2)}) collective-permute-start(bf16[256,128]{1,0:T(8,128)(2,1)S(1)} %slice.16), channel_id=1, source_target_pairs={{0,1},{1,0},{2,3},{3,2},{4,5},{5,4},{6,7},{7,6},{8,9},{9,8},{10,11... | collective-permute-start | bytes 196616 | tf_op jit(solution)/shard_map/ppermute | solution.py:45
  10.5 3.2 %collective-permute-done.2.refs_3_ = bf16[400,128]{1,0:T(8,128)(2,1)S(1)} collective-permute-done((bf16[400,128]{1,0:T(8,128)(2,1)S(1)}, bf16[400,128]{1,0:T(8,128)(2,1)S(1)}, u32[]{:S(2)}, u32[]{:S(2)}) %collective-permute-start.2) | collective-permute-done | bytes 102432 | tf_op jit(solution)/shard_map/ppermute | solution.py:45
  13.7 1.2 %collective-permute-start.5 = (bf16[256,128]{1,0:T(8,128)(2,1)S(1)}, bf16[256,128]{1,0:T(8,128)(2,1)S(1)}, u32[]{:S(2)}, u32[]{:S(2)}) collective-permute-start(bf16[256,128]{1,0:T(8,128)(2,1)S(1)} %slice.17), channel_id=1, source_target_pairs={{0,1},{1,0},{2,3},{3,2},{4,5},{5,4},{6,7},{7,6},{8,9},{9,8},{10,11... | collective-permute-start | bytes 196616 | tf_op jit(solution)/shard_map/ppermute | solution.py:45
  14.9 0.3 collective-permute-start.6
  15.3 0.3 copy-done.8
  15.6 0.3 copy-done.7
  15.9 1.1 %attend_own.1 = (f32[4,256,128]{2,1,0:T(8,128)S(1)}, f32[4,256,128]{2,1,0:T(8,128)S(1)}, f32[4,256,128]{2,1,0:T(8,128)S(1)}, s32[4,32]{1,0:T(4,128)S(1)}, f32[1,1024]{1,0:T(1,128)S(1)}) custom-call(bf16[400,128]{1,0:T(8,128)(2,1)S(1)} %get-tuple-element.25.refs_0_, bf16[400,128]{1,0:T(8,128)(2,1)S(1)} %collective-permute-done.refs_1_, ...), custom_call_target="tpu_custom_call" | custom-call | flops 2150000128 | tf_op jit(solution)/shard_map/attend_own/pallas_call | solution.py:151
  17.1 1.3 %collective-permute-done.6.refs_7_ = bf16[256,128]{1,0:T(8,128)(2,1)S(1)} collective-permute-done((bf16[256,128]{1,0:T(8,128)(2,1)S(1)}, bf16[256,128]{1,0:T(8,128)(2,1)S(1)}, u32[]{:S(2)}, u32[]{:S(2)}) %collective-permute-start.6) | collective-permute-done | bytes 65568 | tf_op jit(solution)/shard_map/ppermute | solution.py:45
  18.4 1.4 %attend_rest.1 = (bf16[128,128]{1,0:T(8,128)(2,1)S(1)}, bf16[128,128]{1,0:T(8,128)(2,1)S(1)}, bf16[128,128]{1,0:T(8,128)(2,1)S(1)}, bf16[128,128]{1,0:T(8,128)(2,1)S(1)}) custom-call(bf16[400,128]{1,0:T(8,128)(2,1)S(1)} %get-tuple-element.25.refs_0_, bf16[400,128]{1,0:T(8,128)(2,1)S(1)} %collective-permute-done.refs_1_, ...), custom_call_target="tpu_custom_call" | custom-call | flops 2150000128 | tf_op jit(solution)/shard_map/attend_rest/pallas_call | solution.py:167
  19.8 2.6 %collective-permute-start.7 = (bf16[128,128]{1,0:T(8,128)(2,1)S(1)}, bf16[128,128]{1,0:T(8,128)(2,1)S(1)}, u32[]{:S(2)}, u32[]{:S(2)}) collective-permute-start(bf16[128,128]{1,0:T(8,128)(2,1)S(1)} %get-tuple-element.35), channel_id=1, source_target_pairs={{0,2},{1,3},{2,0},{3,1},{4,6},{5,7},{6,4},{7,5},{8,10},{9,11},{10,... | collective-permute-start | bytes 98312 | tf_op jit(solution)/shard_map/ppermute | solution.py:45
  22.4 1.0 %collective-permute-start.8 = (bf16[128,128]{1,0:T(8,128)(2,1)S(1)}, bf16[128,128]{1,0:T(8,128)(2,1)S(1)}, u32[]{:S(2)}, u32[]{:S(2)}) collective-permute-start(bf16[128,128]{1,0:T(8,128)(2,1)S(1)} %get-tuple-element.36), channel_id=1, source_target_pairs={{0,4},{1,5},{2,6},{3,7},{4,0},{5,1},{6,2},{7,3},{8,12},{9,13},{10,... | collective-permute-start | bytes 98312 | tf_op jit(solution)/shard_map/ppermute | solution.py:45
  23.4 1.1 %collective-permute-start.9 = (bf16[128,128]{1,0:T(8,128)(2,1)S(1)}, bf16[128,128]{1,0:T(8,128)(2,1)S(1)}, u32[]{:S(2)}, u32[]{:S(2)}) collective-permute-start(bf16[128,128]{1,0:T(8,128)(2,1)S(1)} %get-tuple-element.37), channel_id=1, source_target_pairs={{0,6},{1,7},{2,4},{3,5},{4,2},{5,3},{6,0},{7,1},{8,14},{9,15},{10,... | collective-permute-start | bytes 98312 | tf_op jit(solution)/shard_map/ppermute | solution.py:45
  24.5 4.2 %collective-permute-start.10 = (bf16[8,2,128,128]{3,2,1,0:T(8,128)(2,1)S(1)}, bf16[8,2,128,128]{3,2,1,0:T(8,128)(2,1)S(1)}, u32[]{:S(2)}, u32[]{:S(2)}) collective-permute-start(bf16[8,2,128,128]{3,2,1,0:T(8,128)(2,1)S(1)} %copy-done.2), channel_id=1, source_target_pairs={{0,8},{8,0},{16,24},{24,16},{1,9},{9,1},{17,25},{25,17},{2,10},{10... | collective-permute-start | bytes 1572872 | tf_op jit(solution)/shard_map/ppermute | solution.py:45
  28.8 1.3 %collective-permute-start.13 = (bf16[8,2,128,128]{3,2,1,0:T(8,128)(2,1)S(1)}, bf16[8,2,128,128]{3,2,1,0:T(8,128)(2,1)S(1)}, u32[]{:S(2)}, u32[]{:S(2)}) collective-permute-start(bf16[8,2,128,128]{3,2,1,0:T(8,128)(2,1)S(1)} %collective-permute-done.12.refs_12_.refs_8_), channel_id=1, source_target_pairs={{0,8},{8,0},{16,24},{24,16},{1,9},{9,1},{17,25},{25,17},{2,10},{10... | collective-permute-start | bytes 1572872 | tf_op jit(solution)/shard_map/ppermute | solution.py:45
  30.1 0.5 %collective-permute-done.14.refs_6_ = bf16[8,2,128,128]{3,2,1,0:T(8,128)(2,1)S(1)} collective-permute-done((bf16[8,2,128,128]{3,2,1,0:T(8,128)(2,1)}, bf16[8,2,128,128]{3,2,1,0:T(8,128)(2,1)S(1)}, u32[]{:S(2)}, u32[]{:S(2)}) %collective-permute-start.14) | collective-permute-done | bytes 524320 | tf_op jit(solution)/shard_map/ppermute | solution.py:45
  30.6 2.5 %collective-permute-start.15 = (bf16[8,2,128,128]{3,2,1,0:T(8,128)(2,1)S(1)}, bf16[8,2,128,128]{3,2,1,0:T(8,128)(2,1)S(1)}, u32[]{:S(2)}, u32[]{:S(2)}) collective-permute-start(bf16[8,2,128,128]{3,2,1,0:T(8,128)(2,1)S(1)} %collective-permute-done.14.refs_6_), channel_id=1, source_target_pairs={{0,8},{8,0},{16,24},{24,16},{1,9},{9,1},{17,25},{25,17},{2,10},{10... | collective-permute-start | bytes 1572872 | tf_op jit(solution)/shard_map/ppermute | solution.py:45
  33.1 2.4 %mlp_near.1 = (f32[8,128,128]{2,1,0:T(8,128)S(1)}, f32[8,128,128]{2,1,0:T(8,128)S(1)}, f32[128,1024]{1,0:T(8,128)S(1)}, f32[128,128]{1,0:T(8,128)S(1)}, bf16[16,...) custom-call(s32[4,32]{1,0:T(4,128)S(1)} %get-tuple-element.29.table_in_ref, ...), custom_call_target="tpu_custom_call" | custom-call | tf_op jit(solution)/shard_map/mlp_near/pallas_call | solution.py:295
  35.6 2.7 %mlp_far.1 = (bf16[1,128,1024]{2,1,0:T(8,128)(2,1)}, bf16[1,128,1024]{2,1,0:T(8,128)(2,1)}) custom-call(s32[4,32]{1,0:T(4,128)S(1)} %get-tuple-element.29.table_in_ref, f32[1,1024]{1,0:T(1,128)S(1)} %get-tuple-element.30.refs_6_.gain_ref, bf16[1,128,1024]{2,1,0:T(8,128)(2,1)S(1)} %copy-done.1, f32[8,128,128]{2,1,0:T(8,128)S(1)} %get-tuple-element.41.refs_0_, ...), custom_call_target="tpu_custom_call" | custom-call | tf_op jit(solution)/shard_map/mlp_far/pallas_call | solution.py:358
  (35 shorter events, 0.4 us)
Async XLA Ops:
  2.4 6.0 %collective-permute-start = (bf16[400,128]{1,0:T(8,128)(2,1)S(1)}, bf16[400,128]{1,0:T(8,128)(2,1)S(1)}, u32[]{:S(2)}, u32[]{:S(2)}) collective-permute-start(bf16[400,128]{1,0:T(8,128)(2,1)S(1)} %get-tuple-element.26), channel_id=1, source_target_pairs={{0,2},{1,3},{2,0},{3,1},{4,6},{5,7},{6,4},{7,5},{8,10},{9,11},{10,... | collective-permute-start | bytes 307208 | tf_op jit(solution)/shard_map/ppermute | solution.py:45
  4.6 5.1 %collective-permute-start.1 = (bf16[400,128]{1,0:T(8,128)(2,1)S(1)}, bf16[400,128]{1,0:T(8,128)(2,1)S(1)}, u32[]{:S(2)}, u32[]{:S(2)}) collective-permute-start(bf16[400,128]{1,0:T(8,128)(2,1)S(1)} %get-tuple-element.27), channel_id=1, source_target_pairs={{0,4},{1,5},{2,6},{3,7},{4,0},{5,1},{6,2},{7,3},{8,12},{9,13},{10,... | collective-permute-start | bytes 307208 | tf_op jit(solution)/shard_map/ppermute | solution.py:45
  6.9 6.8 %collective-permute-start.2 = (bf16[400,128]{1,0:T(8,128)(2,1)S(1)}, bf16[400,128]{1,0:T(8,128)(2,1)S(1)}, u32[]{:S(2)}, u32[]{:S(2)}) collective-permute-start(bf16[400,128]{1,0:T(8,128)(2,1)S(1)} %get-tuple-element.28), channel_id=1, source_target_pairs={{0,6},{1,7},{2,4},{3,5},{4,2},{5,3},{6,0},{7,1},{8,14},{9,15},{10,... | collective-permute-start | bytes 307208 | tf_op jit(solution)/shard_map/ppermute | solution.py:45
  6.9 17.6 %collective-permute-start.12 = (bf16[8,2,128,128]{3,2,1,0:T(8,128)(2,1)}, bf16[8,2,128,128]{3,2,1,0:T(8,128)(2,1)S(1)}, u32[]{:S(2)}, u32[]{:S(2)}) collective-permute-start(bf16[8,2,128,128]{3,2,1,0:T(8,128)(2,1)} %refs_10_), channel_id=1, source_target_pairs={{0,16},{8,24},{16,0},{24,8},{1,17},{9,25},{17,1},{25,9},{2,18},{10... | collective-permute-start | bytes 1572872 | tf_op jit(solution)/shard_map/ppermute | solution.py:45
  8.2 22.4 %collective-permute-start.14 = (bf16[8,2,128,128]{3,2,1,0:T(8,128)(2,1)}, bf16[8,2,128,128]{3,2,1,0:T(8,128)(2,1)S(1)}, u32[]{:S(2)}, u32[]{:S(2)}) collective-permute-start(bf16[8,2,128,128]{3,2,1,0:T(8,128)(2,1)} %refs_8_), channel_id=1, source_target_pairs={{0,16},{8,24},{16,0},{24,8},{1,17},{9,25},{17,1},{25,9},{2,18},{10... | collective-permute-start | bytes 1572872 | tf_op jit(solution)/shard_map/ppermute | solution.py:45
  8.4 6.5 %collective-permute-start.3 = (bf16[256,128]{1,0:T(8,128)(2,1)S(1)}, bf16[256,128]{1,0:T(8,128)(2,1)S(1)}, u32[]{:S(2)}, u32[]{:S(2)}) collective-permute-start(bf16[256,128]{1,0:T(8,128)(2,1)S(1)} %slice.12), channel_id=1, source_target_pairs={{0,1},{1,0},{2,3},{3,2},{4,5},{5,4},{6,7},{7,6},{8,9},{9,8},{10,11... | collective-permute-start | bytes 196616 | tf_op jit(solution)/shard_map/ppermute | solution.py:45
  9.7 7.4 %collective-permute-start.4 = (bf16[256,128]{1,0:T(8,128)(2,1)S(1)}, bf16[256,128]{1,0:T(8,128)(2,1)S(1)}, u32[]{:S(2)}, u32[]{:S(2)}) collective-permute-start(bf16[256,128]{1,0:T(8,128)(2,1)S(1)} %slice.16), channel_id=1, source_target_pairs={{0,1},{1,0},{2,3},{3,2},{4,5},{5,4},{6,7},{7,6},{8,9},{9,8},{10,11... | collective-permute-start | bytes 196616 | tf_op jit(solution)/shard_map/ppermute | solution.py:45
  13.7 3.4 %collective-permute-start.5 = (bf16[256,128]{1,0:T(8,128)(2,1)S(1)}, bf16[256,128]{1,0:T(8,128)(2,1)S(1)}, u32[]{:S(2)}, u32[]{:S(2)}) collective-permute-start(bf16[256,128]{1,0:T(8,128)(2,1)S(1)} %slice.17), channel_id=1, source_target_pairs={{0,1},{1,0},{2,3},{3,2},{4,5},{5,4},{6,7},{7,6},{8,9},{9,8},{10,11... | collective-permute-start | bytes 196616 | tf_op jit(solution)/shard_map/ppermute | solution.py:45
  14.9 0.7 %copy-start.8 = (s32[32,2]{0,1:T(2,128)S(1)}, s32[32,2]{0,1:T(2,128)}, u32[]{:S(2)}) copy-start(s32[32,2]{0,1:T(2,128)} %param.22) | copy-start | bytes 772
  14.9 0.7 %copy-start.6 = (f32[1024]{0:T(1024)S(1)}, f32[1024]{0:T(1024)}, u32[]{:S(2)}) copy-start(f32[1024]{0:T(1024)} %param.18) | copy-start | bytes 12292
  14.9 3.5 %collective-permute-start.6 = (bf16[256,128]{1,0:T(8,128)(2,1)S(1)}, bf16[256,128]{1,0:T(8,128)(2,1)S(1)}, u32[]{:S(2)}, u32[]{:S(2)}) collective-permute-start(bf16[256,128]{1,0:T(8,128)(2,1)S(1)} %slice.18), channel_id=1, source_target_pairs={{0,1},{1,0},{2,3},{3,2},{4,5},{5,4},{6,7},{7,6},{8,9},{9,8},{10,11... | collective-permute-start | bytes 196616 | tf_op jit(solution)/shard_map/ppermute | solution.py:45
  15.3 0.7 %copy-start.7 = (s32[32,2]{0,1:T(2,128)S(1)}, s32[32,2]{0,1:T(2,128)}, u32[]{:S(2)}) copy-start(s32[32,2]{0,1:T(2,128)} %param.20) | copy-start | bytes 772
  18.4 6.1 %copy-start.2 = (bf16[8,2,128,128]{3,2,1,0:T(8,128)(2,1)S(1)}, bf16[8,2,128,128]{3,2,1,0:T(8,128)(2,1)}, u32[]{:S(2)}) copy-start(bf16[8,2,128,128]{3,2,1,0:T(8,128)(2,1)} %refs_8_) | copy-start | bytes 1572868
  18.4 10.3 %copy-start.3 = (bf16[8,2,128,128]{3,2,1,0:T(8,128)(2,1)S(1)}, bf16[8,2,128,128]{3,2,1,0:T(8,128)(2,1)}, u32[]{:S(2)}) copy-start(bf16[8,2,128,128]{3,2,1,0:T(8,128)(2,1)} %refs_10_) | copy-start | bytes 1572868
  18.4 14.7 %copy-start = (bf16[512,1024]{1,0:T(8,128)(2,1)S(1)}, bf16[512,1024]{1,0:T(8,128)(2,1)}, u32[]{:S(2)}) copy-start(bf16[512,1024]{1,0:T(8,128)(2,1)} %refs_4_.1) | copy-start | bytes 3145732
  18.4 14.7 %copy-start.1 = (bf16[1,128,1024]{2,1,0:T(8,128)(2,1)S(1)}, bf16[1,128,1024]{2,1,0:T(8,128)(2,1)}, u32[]{:S(2)}) copy-start(bf16[1,128,1024]{2,1,0:T(8,128)(2,1)} %grad_ref.1) | copy-start | bytes 786436
  18.4 14.7 %copy-start.4 = (bf16[1,128,1024]{2,1,0:T(8,128)(2,1)S(1)}, bf16[1,128,1024]{2,1,0:T(8,128)(2,1)}, u32[]{:S(2)}) copy-start(bf16[1,128,1024]{2,1,0:T(8,128)(2,1)} %refs_5_.1) | copy-start | bytes 786436
  19.8 8.9 %collective-permute-start.7 = (bf16[128,128]{1,0:T(8,128)(2,1)S(1)}, bf16[128,128]{1,0:T(8,128)(2,1)S(1)}, u32[]{:S(2)}, u32[]{:S(2)}) collective-permute-start(bf16[128,128]{1,0:T(8,128)(2,1)S(1)} %get-tuple-element.35), channel_id=1, source_target_pairs={{0,2},{1,3},{2,0},{3,1},{4,6},{5,7},{6,4},{7,5},{8,10},{9,11},{10,... | collective-permute-start | bytes 98312 | tf_op jit(solution)/shard_map/ppermute | solution.py:45
  22.4 6.4 %collective-permute-start.8 = (bf16[128,128]{1,0:T(8,128)(2,1)S(1)}, bf16[128,128]{1,0:T(8,128)(2,1)S(1)}, u32[]{:S(2)}, u32[]{:S(2)}) collective-permute-start(bf16[128,128]{1,0:T(8,128)(2,1)S(1)} %get-tuple-element.36), channel_id=1, source_target_pairs={{0,4},{1,5},{2,6},{3,7},{4,0},{5,1},{6,2},{7,3},{8,12},{9,13},{10,... | collective-permute-start | bytes 98312 | tf_op jit(solution)/shard_map/ppermute | solution.py:45
  23.4 6.7 %collective-permute-start.9 = (bf16[128,128]{1,0:T(8,128)(2,1)S(1)}, bf16[128,128]{1,0:T(8,128)(2,1)S(1)}, u32[]{:S(2)}, u32[]{:S(2)}) collective-permute-start(bf16[128,128]{1,0:T(8,128)(2,1)S(1)} %get-tuple-element.37), channel_id=1, source_target_pairs={{0,6},{1,7},{2,4},{3,5},{4,2},{5,3},{6,0},{7,1},{8,14},{9,15},{10,... | collective-permute-start | bytes 98312 | tf_op jit(solution)/shard_map/ppermute | solution.py:45
  24.5 8.5 %collective-permute-start.10 = (bf16[8,2,128,128]{3,2,1,0:T(8,128)(2,1)S(1)}, bf16[8,2,128,128]{3,2,1,0:T(8,128)(2,1)S(1)}, u32[]{:S(2)}, u32[]{:S(2)}) collective-permute-start(bf16[8,2,128,128]{3,2,1,0:T(8,128)(2,1)S(1)} %copy-done.2), channel_id=1, source_target_pairs={{0,8},{8,0},{16,24},{24,16},{1,9},{9,1},{17,25},{25,17},{2,10},{10... | collective-permute-start | bytes 1572872 | tf_op jit(solution)/shard_map/ppermute | solution.py:45
  28.7 4.4 %collective-permute-start.11 = (bf16[8,2,128,128]{3,2,1,0:T(8,128)(2,1)S(1)}, bf16[8,2,128,128]{3,2,1,0:T(8,128)(2,1)S(1)}, u32[]{:S(2)}, u32[]{:S(2)}) collective-permute-start(bf16[8,2,128,128]{3,2,1,0:T(8,128)(2,1)S(1)} %copy-done.3), channel_id=1, source_target_pairs={{0,8},{8,0},{16,24},{24,16},{1,9},{9,1},{17,25},{25,17},{2,10},{10... | collective-permute-start | bytes 1572872 | tf_op jit(solution)/shard_map/ppermute | solution.py:45
  28.8 4.3 %collective-permute-start.13 = (bf16[8,2,128,128]{3,2,1,0:T(8,128)(2,1)S(1)}, bf16[8,2,128,128]{3,2,1,0:T(8,128)(2,1)S(1)}, u32[]{:S(2)}, u32[]{:S(2)}) collective-permute-start(bf16[8,2,128,128]{3,2,1,0:T(8,128)(2,1)S(1)} %collective-permute-done.12.refs_12_.refs_8_), channel_id=1, source_target_pairs={{0,8},{8,0},{16,24},{24,16},{1,9},{9,1},{17,25},{25,17},{2,10},{10... | collective-permute-start | bytes 1572872 | tf_op jit(solution)/shard_map/ppermute | solution.py:45
  30.6 5.0 %collective-permute-start.15 = (bf16[8,2,128,128]{3,2,1,0:T(8,128)(2,1)S(1)}, bf16[8,2,128,128]{3,2,1,0:T(8,128)(2,1)S(1)}, u32[]{:S(2)}, u32[]{:S(2)}) collective-permute-start(bf16[8,2,128,128]{3,2,1,0:T(8,128)(2,1)S(1)} %collective-permute-done.14.refs_6_), channel_id=1, source_target_pairs={{0,8},{8,0},{16,24},{24,16},{1,9},{9,1},{17,25},{25,17},{2,10},{10... | collective-permute-start | bytes 1572872 | tf_op jit(solution)/shard_map/ppermute | solution.py:45
  (1 other events, 0.7 us)
